TPU v7x, 128 devices: a whole 4x4x4 slice. The times are simulated.
128 devices in a mesh: ctx: 16 (over z_lo, x, core), tp: 8 (over z_hi, y).
Axes of the slice: x: 4, y: 4, z: 4 (z_hi: 2, z_lo: 2; z = z_hi * 2 + z_lo), core: 2. Of those that a mesh axis runs over, the one named last changes fastest.
Arguments:
- query_proj: float32 [6144, 8192], P('ctx', 'tp'), may hold values from -6 to 6
- key_proj: float32 [6144, 8192], P('ctx', 'tp'), may hold values from -6 to 6
- value_proj: float32 [6144, 8192], P('ctx', 'tp'), may hold values from -6 to 6
- short_taps: float32 [3, 3, 8192], P(None, None, 'tp'), may hold values from -4 to 4
- pole_rates: float32 [16, 8192], P(None, 'tp'), may hold values from 1.6276042e-06 to 0.05
- residues: float32 [16, 8192], P(None, 'tp'), may hold values from -0.06 to 0.06
- skip_gain: float32 [8192], P('tp'), may hold values from -3 to 3
- out_weight: bfloat16 [8192, 8192], P('tp', 'ctx'), may hold values from -0.09375 to 0.09375
Outputs:
- block_out: float32 [6144, 8192], P('ctx', 'tp')
All inputs are finite; a program needn't handle non-finite values.
Results may differ from a plain program's by a relative error of at most 0.0029.
Values may be sent and summed in bfloat16 or wider, within the bound.
No kernel may reach another device: no remote copies, remote signals or barrier semaphores. Data moves between devices by JAX's collectives and lax.ppermute only.
A program may use at most 128 MiB of HBM per device.

v0:
```python
import jax
import jax.numpy as jnp
import numpy as np
from jax import lax
from jax.sharding import PartitionSpec as P

HI = lax.Precision.HIGHEST


def shifted(value, axis, by):
    size = lax.axis_size(axis)
    pairs = [(i, i + by) for i in range(size) if 0 <= i + by < size]
    return lax.ppermute(value, axis, pairs)


def short_filter(signal, rim_part, tap_set):
    extended = jnp.concatenate([rim_part, signal], axis=0)
    return tap_set[0] * signal + tap_set[1] * extended[1:-1] + tap_set[2] * extended[:-2]


def modal_blocks(forcing, decays, residues, modal_state):
    block_len = 32
    steps_at = jnp.arange(block_len, dtype=jnp.float32)
    powers = jnp.exp(-decays[None] * steps_at[:, None, None])
    lead_powers = powers * jnp.exp(-decays)[None]
    behind = powers[::-1]
    kernel = jnp.einsum("tmc,mc->tc", powers, residues, precision=HI)
    offset_grid = np.arange(block_len)[:, None] - np.arange(block_len)[None, :]
    toeplitz = jnp.where((offset_grid >= 0)[:, :, None], kernel[np.clip(offset_grid, 0, None)], 0.0)
    weighted = lead_powers * residues[None]
    block_decay = jnp.exp(-decays * block_len)
    blocks = forcing.reshape(-1, block_len, forcing.shape[1])

    def advance(carried, block):
        produced = jnp.einsum("tsc,sc->tc", toeplitz, block, precision=HI)
        produced = produced + jnp.einsum("tmc,mc->tc", weighted, carried, precision=HI)
        carried = block_decay * carried + jnp.einsum("tmc,tc->mc", behind, block, precision=HI)
        return (carried, produced)

    last_state, outputs = lax.scan(advance, modal_state, blocks)
    return (last_state, outputs.reshape(forcing.shape), lead_powers)


def on_device(
    query_proj, key_proj, value_proj, short_taps, pole_rates, residues, skip_gain, out_weight
):
    rim_rows = shifted((query_proj[-2:], key_proj[-2:], value_proj[-2:]), "ctx", 1)
    query_feat = short_filter(query_proj, rim_rows[0], short_taps[0])
    key_feat = short_filter(key_proj, rim_rows[1], short_taps[1])
    value_feat = short_filter(value_proj, rim_rows[2], short_taps[2])
    gated_input = key_feat * value_feat
    local_rows = gated_input.shape[0]
    channels = gated_input.shape[1]
    zero_state = jnp.zeros(pole_rates.shape, jnp.float32)
    last_state, convolved, lead_powers = modal_blocks(gated_input, pole_rates, residues, zero_state)
    device_decay = jnp.exp(-pole_rates * local_rows)

    def relay(index_now, carried):
        return shifted(device_decay * carried + last_state, "ctx", 1)

    entering = lax.fori_loop(0, lax.axis_size("ctx") - 1, relay, zero_state)
    block_count = local_rows // 32
    block_starts = jnp.arange(block_count, dtype=jnp.float32) * 32.0
    start_powers = jnp.exp(-pole_rates[None] * block_starts[:, None, None])
    seeded = start_powers * (residues * entering)[None]
    correction = jnp.einsum("bmc,tmc->btc", seeded, lead_powers, precision=HI).reshape(
        local_rows, channels
    )
    convolved = convolved + correction + skip_gain[None] * gated_input
    hidden = (query_feat * convolved).astype(jnp.bfloat16)
    terms = jnp.dot(
        hidden,
        lax.all_gather(out_weight, "ctx", axis=1, tiled=True),
        preferred_element_type=jnp.float32,
    )
    return lax.psum_scatter(terms, "tp", scatter_dimension=1, tiled=True)


def solution(mesh):
    in_specs = (
        P("ctx", "tp"),
        P("ctx", "tp"),
        P("ctx", "tp"),
        P(None, None, "tp"),
        P(None, "tp"),
        P(None, "tp"),
        P("tp"),
        P("tp", "ctx"),
    )
    out_specs = P("ctx", "tp")
    return jax.shard_map(
        on_device, mesh=mesh, in_specs=in_specs, out_specs=out_specs, check_vma=False
    )
```

profile of v0, /device:TPU:1, one launch (start us, length us, event | category | flops | bytes accessed | tf_op | source)
XLA Modules:
  0.0 426.1 jit_solution(13766712275190252399)
XLA Ops:
  8.1 4.5 %collective-permute-start.2 = (f32[2,1024]{1,0:T(2,128)S(1)}, f32[2,1024]{1,0:T(2,128)S(1)}, u32[]{:S(2)}, u32[]{:S(2)}) collective-permute-start(f32[2,1024]{1,0:T(2,128)S(1)} %slice.83), channel_id=1, source_target_pairs={{0,8},{8,16},{16,24},{24,32},{32,40},{40,48},{48,56},{56,64},{64,7... | collective-permute-start | bytes 24584 | tf_op jit(solution)/shard_map/ppermute | solution.py:13
  13.3 1.9 collective-permute-start.3
  16.0 3.5 collective-permute-start.1
  20.4 1.4 multiply_reduce_fusion.3
  21.8 5.4 %gather_fusion = f32[1024,1024]{1,0:T(8,128)} fusion(f32[32,1024]{1,0:T(8,128)S(1)} %bitcast.57, s32[1024]{0:T(1024)S(1)} %broadcast_clamp_fusion), kind=kCustom, calls=%fused_computation | custom fusion | bytes 8392704 | tf_op jit(solution)/shard_map/gather | solution.py:29
  27.3 2.7 fusion.9
  30.0 1.1 copy-done
  31.1 2.3 broadcast_select_fusion
  33.6 1.7 rev.3
  35.3 7.7 %copy.24 = f32[32,16,1024]{0,1,2:T(8,128)} copy(f32[32,16,1024]{2,1,0:T(8,128)} %get-tuple-element.145) | data formatting | bytes 4194304 | tf_op jit(solution)/shard_map/mul | solution.py:25
  43.0 6.8 %fusion.14 = f32[384,1024]{1,0:T(8,128)} fusion(f32[2,1024]{1,0:T(2,128)S(1)} %collective-permute-done.3, f32[384,1024]{1,0:T(8,128)} %param.17, f32[2,1024]{1,0:T(2,128)S(1)} %collective-permute-done.2, f32[384,1024]{1,0:T(8,128)} %param.16, f32[1024]{0:T(1024)S(1)} %bitcast.66, f32[1024]{0:T(1024)S(1)} %bitcast.67, f32[1024]{0:T(1024)S(1)} %bitcast.62, ...), kind=kLoop, calls=%fused_computation.31 | loop fusion | flops 5898240 | bytes 4759552 | tf_op jit(solution)/shard_map/mul | solution.py:51
  49.9 67.3 %while.24 = (s32[]{:T(128)}, f32[16,1024]{1,0:T(8,128)S(1)}, f32[12,32,1024]{2,1,0:T(8,128)}, f32[16,1024]{1,0:T(8,128)S(1)}, f32[12,32,1024]{2,1,0:T(8,128)}, /...) while((s32[]{:T(128)}, f32[16,1024]{1,0:T(8,128)S(1)}, ...), condition=%wide.region_1.2_spmd.clone, body=%wide.region_0.1_spmd.clone.sunk | while | flops 5767171 | bytes 8127107 | solution.py:40
  49.9 0.9 dynamic-slice_bitcast_fusion.2
  51.8 3.1 multiply_reduce_fusion.8
  55.6 0.9 dynamic-slice_bitcast_fusion.2
  57.5 3.1 multiply_reduce_fusion.8
  61.3 0.9 dynamic-slice_bitcast_fusion.2
  63.2 3.0 multiply_reduce_fusion.8
  66.9 0.9 dynamic-slice_bitcast_fusion.2
  68.9 3.0 multiply_reduce_fusion.8
  74.5 3.0 multiply_reduce_fusion.8
  80.2 3.0 multiply_reduce_fusion.8
  85.8 3.0 multiply_reduce_fusion.8
  91.4 3.0 multiply_reduce_fusion.8
  97.0 2.9 multiply_reduce_fusion.8
  102.5 2.9 multiply_reduce_fusion.8
  108.1 2.9 multiply_reduce_fusion.8
  113.6 2.9 multiply_reduce_fusion.8
  117.2 87.5 %while.23 = (s32[]{:T(128)}, f32[16,1024]{1,0:T(8,128)S(1)}, f32[16,1024]{1,0:T(8,128)S(1)}, f32[16,1024]{1,0:T(8,128)S(1)}, s32[]{:T(128)}) while((s32[]{:T(128)}, f32[16,1024]{1,0:T(8,128)S(1)}, f32[16,1024]{1,0:T(8,128)S(1)}, f32[16,1024]{1,0:T(8,128)S(1)}, s32[]{:T(128)}) %tuple.53), condition=%wide.region_3.4_spmd, body=%wide.region_2.3_spmd.sunk | while | flops 32770 | bytes 524389 | solution.py:61
  117.2 1.9 collective-permute-start
  119.2 1.3 collective-permute-done
  120.5 4.3 %collective-permute-start = (f32[16,1024]{1,0:T(8,128)S(1)}, f32[16,1024]{1,0:T(8,128)S(1)}, u32[]{:S(2)}, u32[]{:S(2)}) collective-permute-start(f32[16,1024]{1,0:T(8,128)S(1)} %multiply_add_fusion.2), channel_id=1, source_target_pairs={{0,8},{8,16},{16,24},{24,32},{32,40},{40,48},{48,56},{56,64},{64,7... | collective-permute-start | bytes 196616 | tf_op jit(solution)/shard_map/while/body/eval_jaxpr/ppermute | solution.py:13
  124.8 1.3 collective-permute-done
  126.1 4.3 %collective-permute-start = (f32[16,1024]{1,0:T(8,128)S(1)}, f32[16,1024]{1,0:T(8,128)S(1)}, u32[]{:S(2)}, u32[]{:S(2)}) collective-permute-start(f32[16,1024]{1,0:T(8,128)S(1)} %multiply_add_fusion.2), channel_id=1, source_target_pairs={{0,8},{8,16},{16,24},{24,32},{32,40},{40,48},{48,56},{56,64},{64,7... | collective-permute-start | bytes 196616 | tf_op jit(solution)/shard_map/while/body/eval_jaxpr/ppermute | solution.py:13
  130.4 1.3 collective-permute-done
  131.7 4.3 %collective-permute-start = (f32[16,1024]{1,0:T(8,128)S(1)}, f32[16,1024]{1,0:T(8,128)S(1)}, u32[]{:S(2)}, u32[]{:S(2)}) collective-permute-start(f32[16,1024]{1,0:T(8,128)S(1)} %multiply_add_fusion.2), channel_id=1, source_target_pairs={{0,8},{8,16},{16,24},{24,32},{32,40},{40,48},{48,56},{56,64},{64,7... | collective-permute-start | bytes 196616 | tf_op jit(solution)/shard_map/while/body/eval_jaxpr/ppermute | solution.py:13
  136.0 1.3 collective-permute-done
  137.3 4.3 %collective-permute-start = (f32[16,1024]{1,0:T(8,128)S(1)}, f32[16,1024]{1,0:T(8,128)S(1)}, u32[]{:S(2)}, u32[]{:S(2)}) collective-permute-start(f32[16,1024]{1,0:T(8,128)S(1)} %multiply_add_fusion.2), channel_id=1, source_target_pairs={{0,8},{8,16},{16,24},{24,32},{32,40},{40,48},{48,56},{56,64},{64,7... | collective-permute-start | bytes 196616 | tf_op jit(solution)/shard_map/while/body/eval_jaxpr/ppermute | solution.py:13
  141.6 1.3 collective-permute-done
  142.9 4.3 %collective-permute-start = (f32[16,1024]{1,0:T(8,128)S(1)}, f32[16,1024]{1,0:T(8,128)S(1)}, u32[]{:S(2)}, u32[]{:S(2)}) collective-permute-start(f32[16,1024]{1,0:T(8,128)S(1)} %multiply_add_fusion.2), channel_id=1, source_target_pairs={{0,8},{8,16},{16,24},{24,32},{32,40},{40,48},{48,56},{56,64},{64,7... | collective-permute-start | bytes 196616 | tf_op jit(solution)/shard_map/while/body/eval_jaxpr/ppermute | solution.py:13
  147.2 1.3 collective-permute-done
  148.5 4.3 %collective-permute-start = (f32[16,1024]{1,0:T(8,128)S(1)}, f32[16,1024]{1,0:T(8,128)S(1)}, u32[]{:S(2)}, u32[]{:S(2)}) collective-permute-start(f32[16,1024]{1,0:T(8,128)S(1)} %multiply_add_fusion.2), channel_id=1, source_target_pairs={{0,8},{8,16},{16,24},{24,32},{32,40},{40,48},{48,56},{56,64},{64,7... | collective-permute-start | bytes 196616 | tf_op jit(solution)/shard_map/while/body/eval_jaxpr/ppermute | solution.py:13
  152.8 1.3 collective-permute-done
  154.1 4.3 %collective-permute-start = (f32[16,1024]{1,0:T(8,128)S(1)}, f32[16,1024]{1,0:T(8,128)S(1)}, u32[]{:S(2)}, u32[]{:S(2)}) collective-permute-start(f32[16,1024]{1,0:T(8,128)S(1)} %multiply_add_fusion.2), channel_id=1, source_target_pairs={{0,8},{8,16},{16,24},{24,32},{32,40},{40,48},{48,56},{56,64},{64,7... | collective-permute-start | bytes 196616 | tf_op jit(solution)/shard_map/while/body/eval_jaxpr/ppermute | solution.py:13
  158.4 1.3 collective-permute-done
  159.7 4.3 %collective-permute-start = (f32[16,1024]{1,0:T(8,128)S(1)}, f32[16,1024]{1,0:T(8,128)S(1)}, u32[]{:S(2)}, u32[]{:S(2)}) collective-permute-start(f32[16,1024]{1,0:T(8,128)S(1)} %multiply_add_fusion.2), channel_id=1, source_target_pairs={{0,8},{8,16},{16,24},{24,32},{32,40},{40,48},{48,56},{56,64},{64,7... | collective-permute-start | bytes 196616 | tf_op jit(solution)/shard_map/while/body/eval_jaxpr/ppermute | solution.py:13
  164.0 1.3 collective-permute-done
  165.3 4.3 %collective-permute-start = (f32[16,1024]{1,0:T(8,128)S(1)}, f32[16,1024]{1,0:T(8,128)S(1)}, u32[]{:S(2)}, u32[]{:S(2)}) collective-permute-start(f32[16,1024]{1,0:T(8,128)S(1)} %multiply_add_fusion.2), channel_id=1, source_target_pairs={{0,8},{8,16},{16,24},{24,32},{32,40},{40,48},{48,56},{56,64},{64,7... | collective-permute-start | bytes 196616 | tf_op jit(solution)/shard_map/while/body/eval_jaxpr/ppermute | solution.py:13
  169.6 1.3 collective-permute-done
  170.9 4.3 %collective-permute-start = (f32[16,1024]{1,0:T(8,128)S(1)}, f32[16,1024]{1,0:T(8,128)S(1)}, u32[]{:S(2)}, u32[]{:S(2)}) collective-permute-start(f32[16,1024]{1,0:T(8,128)S(1)} %multiply_add_fusion.2), channel_id=1, source_target_pairs={{0,8},{8,16},{16,24},{24,32},{32,40},{40,48},{48,56},{56,64},{64,7... | collective-permute-start | bytes 196616 | tf_op jit(solution)/shard_map/while/body/eval_jaxpr/ppermute | solution.py:13
  175.2 1.3 collective-permute-done
  176.5 4.3 %collective-permute-start = (f32[16,1024]{1,0:T(8,128)S(1)}, f32[16,1024]{1,0:T(8,128)S(1)}, u32[]{:S(2)}, u32[]{:S(2)}) collective-permute-start(f32[16,1024]{1,0:T(8,128)S(1)} %multiply_add_fusion.2), channel_id=1, source_target_pairs={{0,8},{8,16},{16,24},{24,32},{32,40},{40,48},{48,56},{56,64},{64,7... | collective-permute-start | bytes 196616 | tf_op jit(solution)/shard_map/while/body/eval_jaxpr/ppermute | solution.py:13
  180.8 1.3 collective-permute-done
  182.1 5.9 %collective-permute-start = (f32[16,1024]{1,0:T(8,128)S(1)}, f32[16,1024]{1,0:T(8,128)S(1)}, u32[]{:S(2)}, u32[]{:S(2)}) collective-permute-start(f32[16,1024]{1,0:T(8,128)S(1)} %multiply_add_fusion.2), channel_id=1, source_target_pairs={{0,8},{8,16},{16,24},{24,32},{32,40},{40,48},{48,56},{56,64},{64,7... | collective-permute-start | bytes 196616 | tf_op jit(solution)/shard_map/while/body/eval_jaxpr/ppermute | solution.py:13
  188.0 1.3 collective-permute-done
  189.3 6.4 %collective-permute-start = (f32[16,1024]{1,0:T(8,128)S(1)}, f32[16,1024]{1,0:T(8,128)S(1)}, u32[]{:S(2)}, u32[]{:S(2)}) collective-permute-start(f32[16,1024]{1,0:T(8,128)S(1)} %multiply_add_fusion.2), channel_id=1, source_target_pairs={{0,8},{8,16},{16,24},{24,32},{32,40},{40,48},{48,56},{56,64},{64,7... | collective-permute-start | bytes 196616 | tf_op jit(solution)/shard_map/while/body/eval_jaxpr/ppermute | solution.py:13
  195.7 1.3 collective-permute-done
  197.0 6.4 %collective-permute-start = (f32[16,1024]{1,0:T(8,128)S(1)}, f32[16,1024]{1,0:T(8,128)S(1)}, u32[]{:S(2)}, u32[]{:S(2)}) collective-permute-start(f32[16,1024]{1,0:T(8,128)S(1)} %multiply_add_fusion.2), channel_id=1, source_target_pairs={{0,8},{8,16},{16,24},{24,32},{32,40},{40,48},{48,56},{56,64},{64,7... | collective-permute-start | bytes 196616 | tf_op jit(solution)/shard_map/while/body/eval_jaxpr/ppermute | solution.py:13
  203.4 1.3 collective-permute-done
  204.9 13.1 %fusion.2 = f32[1024,32,12]{1,2,0:T(8,128)} fusion(f32[32,16,1024]{0,1,2:T(8,128)} %copy.24, f32[16,1024]{0,1:T(8,128)S(1)} %copy.23, f32[12]{0:T(128)S(1)} %iota_multiply_fusion, f32[16,1024]{0,1:T(8,128)S(1)} %copy.22), kind=kOutput, calls=%fused_computation.10 | convolution fusion | flops 75890688 | bytes 3801136 | tf_op jit(solution)/shard_map/bmc,tmc->btc/dot_general | solution.py:66
  218.1 5.7 %copy.25 = f32[1024,32,12]{0,1,2:T(8,128)S(1)} copy(f32[1024,32,12]{1,2,0:T(8,128)} %fusion.2) | data formatting | bytes 3145728 | tf_op jit(solution)/shard_map/bmc,tmc->btc/dot_general | solution.py:66
  224.1 1.1 copy-done.1
  226.3 14.8 %fusion.29 = f32[384,8192]{1,0:T(8,128)} fusion(bf16[384,1024]{1,0:T(8,128)(2,1)S(1)} %fusion.24, bf16[1024,8192]{1,0:T(8,128)(2,1)} %all-gather.2.cloned.1.call-done), kind=kOutput, calls=%fused_computation.56 | convolution fusion | flops 6442450944 | bytes 30146560 | tf_op jit(solution)/shard_map/dot_general | solution.py:71
  241.2 178.1 %reduce-scatter.2.cloned.1.call-done = f32[384,1024]{1,0:T(8,128)} async-done(((f32[384,8192]{1,0:T(8,128)}), f32[384,1024]{1,0:T(8,128)}) %reduce-scatter.2.cloned.1.call-update) | async-done | bytes 1572880 | tf_op jit(solution)/shard_map/reduce_scatter | solution.py:76
  (110 shorter events, 33.7 us)
Async XLA Ops:
  6.5 15.3 %copy-start.7 = (s32[1024]{0:T(1024)S(1)}, s32[1024]{0:T(1024)}, u32[]{:S(2)}) copy-start(s32[1024]{0:T(1024)} %constant.37) | copy-start | bytes 12292
  6.5 219.8 %all-gather.2.cloned.1.call-start = ((), (), s32[]{:S(2)}) async-start(), calls=%async_computation.1 | async-start | bytes 17825792 | tf_op jit(solution)/shard_map/all_gather | solution.py:73
  7.3 412.0 %reduce-scatter.2.cloned.1.call-start = ((), (), s32[]{:S(2)}) async-start(), calls=%async_computation.2 | async-start | bytes 14155776 | tf_op jit(solution)/shard_map/reduce_scatter | solution.py:76
  8.1 34.9 %collective-permute-start.2 = (f32[2,1024]{1,0:T(2,128)S(1)}, f32[2,1024]{1,0:T(2,128)S(1)}, u32[]{:S(2)}, u32[]{:S(2)}) collective-permute-start(f32[2,1024]{1,0:T(2,128)S(1)} %slice.83), channel_id=1, source_target_pairs={{0,8},{8,16},{16,24},{24,32},{32,40},{40,48},{48,56},{56,64},{64,7... | collective-permute-start | bytes 24584 | tf_op jit(solution)/shard_map/ppermute | solution.py:13
  13.3 29.7 %collective-permute-start.3 = (f32[2,1024]{1,0:T(2,128)S(1)}, f32[2,1024]{1,0:T(2,128)S(1)}, u32[]{:S(2)}, u32[]{:S(2)}) collective-permute-start(f32[2,1024]{1,0:T(2,128)S(1)} %slice.89), channel_id=1, source_target_pairs={{0,8},{8,16},{16,24},{24,32},{32,40},{40,48},{48,56},{56,64},{64,7... | collective-permute-start | bytes 24584 | tf_op jit(solution)/shard_map/ppermute | solution.py:13
  16.0 208.0 %collective-permute-start.1 = (f32[2,1024]{1,0:T(2,128)S(1)}, f32[2,1024]{1,0:T(2,128)S(1)}, u32[]{:S(2)}, u32[]{:S(2)}) collective-permute-start(f32[2,1024]{1,0:T(2,128)S(1)} %slice.77), channel_id=1, source_target_pairs={{0,8},{8,16},{16,24},{24,32},{32,40},{40,48},{48,56},{56,64},{64,7... | collective-permute-start | bytes 24584 | tf_op jit(solution)/shard_map/ppermute | solution.py:13
  21.8 5.4 %copy-start.5 = (f32[3,3,1024]{2,1,0:T(4,128)S(1)}, f32[3,3,1024]{2,1,0:T(4,128)}, u32[]{:S(2)}) copy-start(f32[3,3,1024]{2,1,0:T(4,128)} %param.18) | copy-start | bytes 110596
  27.3 3.8 copy-start
  27.3 3.8 copy-start.6
  43.0 6.9 %copy-start.4 = (f32[16,1024]{1,0:T(8,128)S(1)}, f32[16,1024]{1,0:T(8,128)}, u32[]{:S(2)}) copy-start(f32[16,1024]{1,0:T(8,128)} %param.20) | copy-start | bytes 196612
  117.2 3.2 collective-permute-start
  120.5 5.6 %collective-permute-start = (f32[16,1024]{1,0:T(8,128)S(1)}, f32[16,1024]{1,0:T(8,128)S(1)}, u32[]{:S(2)}, u32[]{:S(2)}) collective-permute-start(f32[16,1024]{1,0:T(8,128)S(1)} %multiply_add_fusion.2), channel_id=1, source_target_pairs={{0,8},{8,16},{16,24},{24,32},{32,40},{40,48},{48,56},{56,64},{64,7... | collective-permute-start | bytes 196616 | tf_op jit(solution)/shard_map/while/body/eval_jaxpr/ppermute | solution.py:13
  126.1 5.6 %collective-permute-start = (f32[16,1024]{1,0:T(8,128)S(1)}, f32[16,1024]{1,0:T(8,128)S(1)}, u32[]{:S(2)}, u32[]{:S(2)}) collective-permute-start(f32[16,1024]{1,0:T(8,128)S(1)} %multiply_add_fusion.2), channel_id=1, source_target_pairs={{0,8},{8,16},{16,24},{24,32},{32,40},{40,48},{48,56},{56,64},{64,7... | collective-permute-start | bytes 196616 | tf_op jit(solution)/shard_map/while/body/eval_jaxpr/ppermute | solution.py:13
  131.7 5.6 %collective-permute-start = (f32[16,1024]{1,0:T(8,128)S(1)}, f32[16,1024]{1,0:T(8,128)S(1)}, u32[]{:S(2)}, u32[]{:S(2)}) collective-permute-start(f32[16,1024]{1,0:T(8,128)S(1)} %multiply_add_fusion.2), channel_id=1, source_target_pairs={{0,8},{8,16},{16,24},{24,32},{32,40},{40,48},{48,56},{56,64},{64,7... | collective-permute-start | bytes 196616 | tf_op jit(solution)/shard_map/while/body/eval_jaxpr/ppermute | solution.py:13
  137.3 5.6 %collective-permute-start = (f32[16,1024]{1,0:T(8,128)S(1)}, f32[16,1024]{1,0:T(8,128)S(1)}, u32[]{:S(2)}, u32[]{:S(2)}) collective-permute-start(f32[16,1024]{1,0:T(8,128)S(1)} %multiply_add_fusion.2), channel_id=1, source_target_pairs={{0,8},{8,16},{16,24},{24,32},{32,40},{40,48},{48,56},{56,64},{64,7... | collective-permute-start | bytes 196616 | tf_op jit(solution)/shard_map/while/body/eval_jaxpr/ppermute | solution.py:13
  142.9 5.6 %collective-permute-start = (f32[16,1024]{1,0:T(8,128)S(1)}, f32[16,1024]{1,0:T(8,128)S(1)}, u32[]{:S(2)}, u32[]{:S(2)}) collective-permute-start(f32[16,1024]{1,0:T(8,128)S(1)} %multiply_add_fusion.2), channel_id=1, source_target_pairs={{0,8},{8,16},{16,24},{24,32},{32,40},{40,48},{48,56},{56,64},{64,7... | collective-permute-start | bytes 196616 | tf_op jit(solution)/shard_map/while/body/eval_jaxpr/ppermute | solution.py:13
  148.5 5.6 %collective-permute-start = (f32[16,1024]{1,0:T(8,128)S(1)}, f32[16,1024]{1,0:T(8,128)S(1)}, u32[]{:S(2)}, u32[]{:S(2)}) collective-permute-start(f32[16,1024]{1,0:T(8,128)S(1)} %multiply_add_fusion.2), channel_id=1, source_target_pairs={{0,8},{8,16},{16,24},{24,32},{32,40},{40,48},{48,56},{56,64},{64,7... | collective-permute-start | bytes 196616 | tf_op jit(solution)/shard_map/while/body/eval_jaxpr/ppermute | solution.py:13
  154.1 5.6 %collective-permute-start = (f32[16,1024]{1,0:T(8,128)S(1)}, f32[16,1024]{1,0:T(8,128)S(1)}, u32[]{:S(2)}, u32[]{:S(2)}) collective-permute-start(f32[16,1024]{1,0:T(8,128)S(1)} %multiply_add_fusion.2), channel_id=1, source_target_pairs={{0,8},{8,16},{16,24},{24,32},{32,40},{40,48},{48,56},{56,64},{64,7... | collective-permute-start | bytes 196616 | tf_op jit(solution)/shard_map/while/body/eval_jaxpr/ppermute | solution.py:13
  159.7 5.6 %collective-permute-start = (f32[16,1024]{1,0:T(8,128)S(1)}, f32[16,1024]{1,0:T(8,128)S(1)}, u32[]{:S(2)}, u32[]{:S(2)}) collective-permute-start(f32[16,1024]{1,0:T(8,128)S(1)} %multiply_add_fusion.2), channel_id=1, source_target_pairs={{0,8},{8,16},{16,24},{24,32},{32,40},{40,48},{48,56},{56,64},{64,7... | collective-permute-start | bytes 196616 | tf_op jit(solution)/shard_map/while/body/eval_jaxpr/ppermute | solution.py:13
  165.3 5.6 %collective-permute-start = (f32[16,1024]{1,0:T(8,128)S(1)}, f32[16,1024]{1,0:T(8,128)S(1)}, u32[]{:S(2)}, u32[]{:S(2)}) collective-permute-start(f32[16,1024]{1,0:T(8,128)S(1)} %multiply_add_fusion.2), channel_id=1, source_target_pairs={{0,8},{8,16},{16,24},{24,32},{32,40},{40,48},{48,56},{56,64},{64,7... | collective-permute-start | bytes 196616 | tf_op jit(solution)/shard_map/while/body/eval_jaxpr/ppermute | solution.py:13
  170.9 5.6 %collective-permute-start = (f32[16,1024]{1,0:T(8,128)S(1)}, f32[16,1024]{1,0:T(8,128)S(1)}, u32[]{:S(2)}, u32[]{:S(2)}) collective-permute-start(f32[16,1024]{1,0:T(8,128)S(1)} %multiply_add_fusion.2), channel_id=1, source_target_pairs={{0,8},{8,16},{16,24},{24,32},{32,40},{40,48},{48,56},{56,64},{64,7... | collective-permute-start | bytes 196616 | tf_op jit(solution)/shard_map/while/body/eval_jaxpr/ppermute | solution.py:13
  176.5 5.6 %collective-permute-start = (f32[16,1024]{1,0:T(8,128)S(1)}, f32[16,1024]{1,0:T(8,128)S(1)}, u32[]{:S(2)}, u32[]{:S(2)}) collective-permute-start(f32[16,1024]{1,0:T(8,128)S(1)} %multiply_add_fusion.2), channel_id=1, source_target_pairs={{0,8},{8,16},{16,24},{24,32},{32,40},{40,48},{48,56},{56,64},{64,7... | collective-permute-start | bytes 196616 | tf_op jit(solution)/shard_map/while/body/eval_jaxpr/ppermute | solution.py:13
  182.1 7.2 %collective-permute-start = (f32[16,1024]{1,0:T(8,128)S(1)}, f32[16,1024]{1,0:T(8,128)S(1)}, u32[]{:S(2)}, u32[]{:S(2)}) collective-permute-start(f32[16,1024]{1,0:T(8,128)S(1)} %multiply_add_fusion.2), channel_id=1, source_target_pairs={{0,8},{8,16},{16,24},{24,32},{32,40},{40,48},{48,56},{56,64},{64,7... | collective-permute-start | bytes 196616 | tf_op jit(solution)/shard_map/while/body/eval_jaxpr/ppermute | solution.py:13
  189.3 7.7 %collective-permute-start = (f32[16,1024]{1,0:T(8,128)S(1)}, f32[16,1024]{1,0:T(8,128)S(1)}, u32[]{:S(2)}, u32[]{:S(2)}) collective-permute-start(f32[16,1024]{1,0:T(8,128)S(1)} %multiply_add_fusion.2), channel_id=1, source_target_pairs={{0,8},{8,16},{16,24},{24,32},{32,40},{40,48},{48,56},{56,64},{64,7... | collective-permute-start | bytes 196616 | tf_op jit(solution)/shard_map/while/body/eval_jaxpr/ppermute | solution.py:13
  197.0 7.7 %collective-permute-start = (f32[16,1024]{1,0:T(8,128)S(1)}, f32[16,1024]{1,0:T(8,128)S(1)}, u32[]{:S(2)}, u32[]{:S(2)}) collective-permute-start(f32[16,1024]{1,0:T(8,128)S(1)} %multiply_add_fusion.2), channel_id=1, source_target_pairs={{0,8},{8,16},{16,24},{24,32},{32,40},{40,48},{48,56},{56,64},{64,7... | collective-permute-start | bytes 196616 | tf_op jit(solution)/shard_map/while/body/eval_jaxpr/ppermute | solution.py:13
  218.1 5.7 %copy-start.3 = (f32[12,32,1024]{2,1,0:T(8,128)S(1)}, f32[12,32,1024]{2,1,0:T(8,128)}, u32[]{:S(2)}) copy-start(f32[12,32,1024]{2,1,0:T(8,128)} %get-tuple-element.70) | copy-start | bytes 4718596
  223.7 1.4 copy-start.1
  223.7 1.9 copy-start.2
  223.8 1.9 copy-start.8
Sparse Core Ops, SparseCore 0:
  9.0 95.2 all-gather.1
  241.3 177.9 reduce-scatter.1
where the time goes:
time: 428 us; the launch traced here: 426 us
  waiting for transfers between devices  198 us (46%)
  starting transfers between devices  77.4 us (18%)
  other arithmetic  71.4 us (17%)
  local copies, waits for them, and re-layouts  36.9 us (9%)
  matrix products  28 us (7%)
  between operations  13.6 us (3%)
    reduce_scatter x1, waiting for transfers between devices, on_device(): return lax.psum_scatter(terms, 'tp', scatter_dimension=1, tiled=True)  178 us
    ppermute x18, starting transfers between devices, shifted(): return lax.ppermute(value, axis, pairs)  77.4 us
    dot_general x12, other arithmetic, advance(): produced = jnp.einsum('tsc,sc->tc', toeplitz, block, precision=HI)  35.8 us
    ppermute x18, waiting for transfers between devices, shifted(): return lax.ppermute(value, axis, pairs)  19.6 us
    dot_general x1, matrix products, on_device(): jnp.dot(hidden, lax.all_gather(out_weight, 'ctx', axis=1, tiled=True), pr...  14.8 us
    dot_general x1, matrix products, on_device(): jnp.einsum('bmc,tmc->btc', seeded, lead_powers, precision=HI)  13.1 us
    while x12, local copies, waits for them, and re-layouts  11 us
  transfers between devices with their start and end apart: 20, of which 16 were waited for; matrix products, arithmetic and copies ran while one was open for 28% of the time, Pallas kernels for 0%

commit v1 on v0

v1 whole, which is shorter than its diff:
```python
import functools
import itertools

import jax
import jax.numpy as jnp
from jax import lax
from jax.experimental import pallas as pl
from jax.experimental.pallas import tpu as pltpu
from jax.sharding import Mesh, PartitionSpec as P

AXES = ("zl", "x", "core", "zh", "y")
SIZES = {"zl": 2, "x": 4, "core": 2, "zh": 2, "y": 4}
CTX = ("zl", "x", "core")
TP = ("zh", "y")
SEGS = 8
LANES = 128


def coords(axes):
    for values in itertools.product(*[range(SIZES[a]) for a in axes]):
        yield dict(zip(axes, values))


def place(axes, at):
    index = 0
    for a in axes:
        index = index * SIZES[a] + at[a]
    return index


def permute(value, axes, move):
    pairs = [(place(axes, at), place(axes, move(at))) for at in coords(axes)]
    return lax.ppermute(value, axes, pairs)


def moved(value, axis, by):
    return permute(value, (axis,), lambda at: {axis: (at[axis] + by) % SIZES[axis]})


def onward(value, axis):
    axes = tuple(a for a in AXES if a in (axis, "core"))

    def move(at):
        step = 1 if at["core"] == 0 else -1
        return {**at, axis: (at[axis] + step) % SIZES[axis]}

    return permute(value, axes, move)


def turned(value):
    def move(at):
        return {
            "zl": at["zh"],
            "x": (2 * at["x"] - at["y"]) % 4,
            "core": at["core"],
            "zh": at["zl"],
            "y": at["x"],
        }

    return permute(value, AXES, move)


def later(value, by):
    size = 16
    return lax.ppermute(value, CTX, [(i, i + by) for i in range(size - by)])


def rows_of(ref, j, seg_len):
    return ref[pl.ds(j, SEGS, stride=seg_len), :]


def local_kernel(seg_len, modes, q_ref, k_ref, v_ref, halo_ref, taps_ref, rates_ref, res_ref, skip_ref, y_ref, qf_ref, total_ref, carry_ref):
    wide = (SEGS, LANES)
    sub = lax.broadcasted_iota(jnp.int32, wide, 0)
    rates = rates_ref[...]
    pole = jnp.exp(-rates)

    def spread(row):
        return jnp.broadcast_to(row, wide)

    taps = [[spread(taps_ref[3 * a + b : 3 * a + b + 1, :]) for b in range(3)] for a in range(3)]
    skip = spread(skip_ref[...])
    poles = [spread(pole[m : m + 1, :]) for m in range(modes)]
    gains = [spread(res_ref[m : m + 1, :]) for m in range(modes)]

    def before(ref, back, halo_row):
        rolled = pltpu.roll(rows_of(ref, seg_len - back, seg_len), 1, 0)
        return jnp.where(sub == 0, spread(halo_ref[halo_row : halo_row + 1, :]), rolled)

    refs = (q_ref, k_ref, v_ref)
    past = tuple((before(ref, 1, 2 * a + 1), before(ref, 2, 2 * a)) for a, ref in enumerate(refs))

    def step(j, carried):
        past, states = carried
        feats, new_past = [], []
        for a, ref in enumerate(refs):
            now = rows_of(ref, j, seg_len)
            one, two = past[a]
            feats.append(taps[a][0] * now + taps[a][1] * one + taps[a][2] * two)
            new_past.append((now, one))
        gated = feats[1] * feats[2]
        parts = [skip * gated, None, None, None]
        new_states = []
        for m in range(modes):
            state = poles[m] * states[m] + gated
            new_states.append(state)
            term = gains[m] * state
            parts[m % 4] = term if parts[m % 4] is None else parts[m % 4] + term
        y_ref[j] = (parts[0] + parts[1]) + (parts[2] + parts[3])
        qf_ref[j] = feats[0]
        return tuple(new_past), tuple(new_states)

    zeros = tuple(jnp.zeros(wide, jnp.float32) for _ in range(modes))
    _, ends = lax.fori_loop(0, seg_len, step, (past, zeros), unroll=4)

    seg = jnp.exp(-float(seg_len) * rates)
    for m in range(modes):
        power = spread(seg[m : m + 1, :])
        run = ends[m]
        for by in (1, 2, 4):
            run = run + jnp.where(sub >= by, power * pltpu.roll(run, by, 0), 0.0)
            power = power * power
        total_ref[m : m + 1, :] = run[SEGS - 1 : SEGS, :]
        carry_ref[m] = jnp.where(sub >= 1, pltpu.roll(run, 1, 0), 0.0)


def finish_kernel(seg_len, modes, y_ref, qf_ref, carry_ref, entering_ref, rates_ref, res_ref, hidden_ref, rows_ref):
    wide = (SEGS, LANES)
    sub = lax.broadcasted_iota(jnp.int32, wide, 0).astype(jnp.float32)
    rates = rates_ref[...]
    pole = jnp.exp(-rates)
    poles, starts = [], []
    for m in range(modes):
        rate = jnp.broadcast_to(rates[m : m + 1, :], wide)
        come = jnp.exp(-float(seg_len) * sub * rate) * jnp.broadcast_to(entering_ref[m : m + 1, :], wide)
        poles.append(jnp.broadcast_to(pole[m : m + 1, :], wide))
        starts.append(jnp.broadcast_to(res_ref[m : m + 1, :], wide) * (carry_ref[m] + come))

    def step(j, states):
        parts = [y_ref[j], None, None, None]
        new_states = []
        for m in range(modes):
            state = poles[m] * states[m]
            new_states.append(state)
            parts[m % 4] = state if parts[m % 4] is None else parts[m % 4] + state
        rows_ref[pl.ds(j, SEGS, stride=seg_len), :] = qf_ref[j] * ((parts[0] + parts[1]) + (parts[2] + parts[3]))
        return tuple(new_states)

    lax.fori_loop(0, seg_len, step, tuple(starts), unroll=4)
    hidden_ref[...] = rows_ref[...].astype(jnp.bfloat16)


def local_part(q, k, v, halo, taps, rates, res, skip):
    rows, channels = q.shape
    modes = rates.shape[0]
    seg_len = rows // SEGS
    tall = pl.BlockSpec((rows, LANES), lambda c: (0, c))

    def short(n):
        return pl.BlockSpec((n, LANES), lambda c: (0, c))

    cube = pl.BlockSpec((seg_len, SEGS, LANES), lambda c: (0, 0, c))
    mode_cube = pl.BlockSpec((modes, SEGS, LANES), lambda c: (0, 0, c))
    f32 = jnp.float32
    return pl.pallas_call(
        functools.partial(local_kernel, seg_len, modes),
        grid=(channels // LANES,),
        in_specs=[tall, tall, tall, short(6), short(9), short(modes), short(modes), short(1)],
        out_specs=[cube, cube, short(modes), mode_cube],
        out_shape=[
            jax.ShapeDtypeStruct((seg_len, SEGS, channels), f32),
            jax.ShapeDtypeStruct((seg_len, SEGS, channels), f32),
            jax.ShapeDtypeStruct((modes, channels), f32),
            jax.ShapeDtypeStruct((modes, SEGS, channels), f32),
        ],
        compiler_params=pltpu.CompilerParams(vmem_limit_bytes=24 * 2**20),
        cost_estimate=pl.CostEstimate(flops=40_000_000, bytes_accessed=9_000_000, transcendentals=0),
        name="local_part",
    )(q, k, v, halo, taps, rates, res, skip)


def finish_part(y, qf, carry, entering, rates, res):
    seg_len, _, channels = y.shape
    modes = rates.shape[0]
    rows = seg_len * SEGS

    def short(n):
        return pl.BlockSpec((n, LANES), lambda c: (0, c))

    cube = pl.BlockSpec((seg_len, SEGS, LANES), lambda c: (0, 0, c))
    mode_cube = pl.BlockSpec((modes, SEGS, LANES), lambda c: (0, 0, c))
    return pl.pallas_call(
        functools.partial(finish_kernel, seg_len, modes),
        grid=(channels // LANES,),
        in_specs=[cube, cube, mode_cube, short(modes), short(modes), short(modes)],
        out_specs=pl.BlockSpec((rows, LANES), lambda c: (0, c)),
        out_shape=jax.ShapeDtypeStruct((rows, channels), jnp.bfloat16),
        scratch_shapes=[pltpu.VMEM((rows, LANES), jnp.float32)],
        compiler_params=pltpu.CompilerParams(vmem_limit_bytes=24 * 2**20),
        cost_estimate=pl.CostEstimate(flops=15_000_000, bytes_accessed=4_000_000, transcendentals=0),
        name="finish_part",
    )(y, qf, carry, entering, rates, res)


def pick(first, second):
    return jnp.where(lax.axis_index("core") == 0, first, second)


def spread_over(own, ring, pair):
    got = {(0, 0): own}
    got[0, -1] = moved(own, ring, 1)
    got[0, 1] = moved(own, ring, -1)
    got[1, 0] = moved(own, pair, 1)
    got[0, 2] = onward(pick(got[0, -1], got[0, 1]), ring)
    got[1, -1] = moved(got[1, 0], ring, 1)
    got[1, 1] = moved(got[1, 0], ring, -1)
    got[1, 2] = onward(pick(got[1, -1], got[1, 1]), ring)
    return got


def on_device(q, k, v, short_taps, rates, res, skip, weight):
    channels = rates.shape[1]
    halo = later(jnp.concatenate([q[-2:], k[-2:], v[-2:]], axis=0), 1)
    block = turned(weight)
    y, qf, total, carry = local_part(
        q, k, v, halo, short_taps.reshape(9, channels), rates, res, skip.reshape(1, channels)
    )
    rows = q.shape[0]

    def device_decay(times):
        return jnp.exp(-rates * float(rows * times))

    near = later(total, 1) + device_decay(1) * later(total, 2) + device_decay(2) * later(total, 3)
    window = total + device_decay(1) * near
    entering = (
        near
        + device_decay(3) * later(window, 4)
        + device_decay(7) * later(window, 8)
        + device_decay(11) * later(window, 12)
    )
    hidden = finish_part(y, qf, carry, entering, rates, res)

    weights = spread_over(block, "x", "zl")
    hiddens = spread_over(hidden, "y", "zh")

    slots = [(a, b) for a in (0, 1) for b in (0, 1, 2, -1)]
    held = jnp.stack([hiddens[s] for s in slots])
    flip = (lax.axis_index("zh") + lax.axis_index("zl")) % 2
    turn = lax.axis_index("y") - lax.axis_index("x")
    own = jnp.zeros((rows, weight.shape[1]), jnp.float32)
    other = jnp.zeros((rows, weight.shape[1]), jnp.float32)
    for a, b in slots:
        swapped = moved(weights[a, b], "core", 1)
        slot = ((a + flip) % 2) * 4 + (turn - b) % 4
        term = lax.dynamic_index_in_dim(held, slot, 0, keepdims=False)
        own = own + jnp.dot(term, weights[a, b], preferred_element_type=jnp.float32)
        other = other + jnp.dot(term, swapped, preferred_element_type=jnp.float32)
    first = lax.axis_index("core") == 0
    return jnp.concatenate([jnp.where(first, own, other), jnp.where(first, other, own)], axis=1)


def solution(mesh):
    fine = Mesh(mesh.devices.reshape(tuple(SIZES[a] for a in AXES)), AXES)
    in_specs = (
        P(CTX, TP),
        P(CTX, TP),
        P(CTX, TP),
        P(None, None, TP),
        P(None, TP),
        P(None, TP),
        P(TP),
        P(TP, CTX),
    )
    return jax.shard_map(on_device, mesh=fine, in_specs=in_specs, out_specs=P(CTX, TP), check_vma=False)
```

time: 428 us -> 198 us (0.46)
  waiting for transfers between devices: 198 us -> 70.9 us
  other arithmetic: 71.4 us -> 1.78 us
  local copies, waits for them, and re-layouts: 36.9 us -> 11.2 us
  matrix products: 28 us -> 9.17 us
  between operations: 13.6 us -> 0.39 us
  starting transfers between devices: 77.4 us -> 89.5 us
  Pallas kernels: 0 us -> 11 us
    reduce_scatter x1 -> x0, waiting for transfers between devices: 178 us -> none  [on_device(): return lax.psum_scatter(terms, 'tp', scatter_dimension=1, tiled=True)]
    ppermute x18 -> x30, waiting for transfers between devices: 19.6 us -> 70.9 us  [the longest x23 67.6 us: permute(): return lax.ppermute(value, axes, pairs)]
    dot_general x37 -> x0, other arithmetic: 49 us -> none  [the longest x12 35.8 us: advance(): produced = jnp.einsum('tsc,sc->tc', toeplitz, block, precision=HI)]
    dot_general x2 -> x16, matrix products: 28 us -> 9.17 us  [the longest x8 4.59 us: on_device(): own = own + jnp.dot(term, weights[a, b], preferred_element_type=jnp.float32)]
    ppermute x18 -> x30, starting transfers between devices: 77.4 us -> 89.5 us  [the longest x23 64.3 us: permute(): return lax.ppermute(value, axes, pairs)]
    pallas_call x0 -> x2, Pallas kernels: none -> 11 us  [the longest x1 7.61 us: local_part(): pl.pallas_call(functools.partial(local_kernel, seg_len, modes), grid=(cha...]
    while x12 -> x0, local copies, waits for them, and re-layouts: 11 us -> none
    mul x4 -> x0, other arithmetic: 9.54 us -> none  [the longest x1 6.84 us: on_device(): gated_input = key_feat * value_feat]
  transfers between devices with their start and end apart: 20 -> 30, of which waited for: 16 -> 12; matrix products, arithmetic and copies ran while one was open for 28% -> 6% of each run, Pallas kernels for 0% -> 0%
where the time goes in v1:
time: 198 us; the launch traced here: 194 us
  starting transfers between devices  89.5 us (45%)
  waiting for transfers between devices  70.9 us (36%)
  local copies, waits for them, and re-layouts  11.2 us (6%)
  Pallas kernels  11 us (6%)
  matrix products  9.17 us (5%)
    ppermute x23, waiting for transfers between devices, permute(): return lax.ppermute(value, axes, pairs)  67.6 us
    ppermute x23, starting transfers between devices, permute(): return lax.ppermute(value, axes, pairs)  64.3 us
    ppermute x7, starting transfers between devices, later(): return lax.ppermute(value, CTX, [(i, i + by) for i in range(size - by)])  25.2 us
    unnamed x19, local copies, waits for them, and re-layouts  8.09 us
    pallas_call x1, Pallas kernels, local_part(): pl.pallas_call(functools.partial(local_kernel, seg_len, modes), grid=(cha...  7.61 us
    dot_general x8, matrix products, on_device(): own = own + jnp.dot(term, weights[a, b], preferred_element_type=jnp.float32)  4.59 us
    dot_general x8, matrix products, on_device(): other = other + jnp.dot(term, swapped, preferred_element_type=jnp.float32)  4.58 us
  transfers between devices with their start and end apart: 30, of which 12 were waited for; matrix products, arithmetic and copies ran while one was open for 6% of the time, Pallas kernels for 0%

profile of v1, /device:TPU:1, one launch (start us, length us, event | category | flops | bytes accessed | tf_op | source)
XLA Modules:
  0.0 194.0 jit_solution(17720105099504343077)
XLA Ops:
  0.0 0.8 slice.10
  0.8 0.8 slice.11
  1.5 0.8 slice.9
  2.3 4.5 %collective-permute-start = (f32[6,1024]{1,0:T(8,128)S(1)}, f32[6,1024]{1,0:T(8,128)S(1)}, u32[]{:S(2)}, u32[]{:S(2)}) collective-permute-start(f32[6,1024]{1,0:T(8,128)S(1)} %pad_maximum_fusion.1), channel_id=1, source_target_pairs={{0,8},{8,16},{16,24},{24,32},{32,40},{40,48},{48,56},{56,64},{64,7... | collective-permute-start | bytes 73736 | tf_op jit(solution)/shard_map/ppermute | solution.py:65
  6.8 0.8 reshape.6.taps_ref
  7.8 1.4 copy-done
  9.2 1.4 copy-done.1
  10.6 1.4 copy-done.2
  12.1 0.8 copy-done.3
  12.9 0.8 copy-done.4
  13.7 0.7 copy-done.5
  14.4 7.6 %local_part.1 = (f32[48,8,1024]{2,1,0:T(8,128)S(1)}, f32[48,8,1024]{2,1,0:T(8,128)S(1)}, f32[16,1024]{1,0:T(8,128)S(1)}, f32[16,8,1024]{2,1,0:T(8,128)S(1)}) custom-call(f32[384,1024]{1,0:T(8,128)S(1)} %copy-done, f32[384,1024]{1,0:T(8,128)S(1)} %copy-done.1, f32[384,1024]{1,0:T(8,128)S(1)} %copy-done.2, f32[6,1024]{1,0:T(8,128)S(1)} %collective-permute-done.halo_ref, ...), custom_call_target="tpu_custom_call" | custom-call | flops 40000000 | bytes 9000000 | tf_op jit(solution)/shard_map/local_part/pallas_call | solution.py:165
  22.0 4.2 %collective-permute-start.1 = (f32[16,1024]{1,0:T(8,128)S(1)}, f32[16,1024]{1,0:T(8,128)S(1)}, u32[]{:S(2)}, u32[]{:S(2)}) collective-permute-start(f32[16,1024]{1,0:T(8,128)S(1)} %get-tuple-element.12), channel_id=1, source_target_pairs={{0,8},{8,16},{16,24},{24,32},{32,40},{40,48},{48,56},{56,64},{64,7... | collective-permute-start | bytes 196616 | tf_op jit(solution)/shard_map/ppermute | solution.py:65
  26.3 3.1 %collective-permute-start.2 = (f32[16,1024]{1,0:T(8,128)S(1)}, f32[16,1024]{1,0:T(8,128)S(1)}, u32[]{:S(2)}, u32[]{:S(2)}) collective-permute-start(f32[16,1024]{1,0:T(8,128)S(1)} %get-tuple-element.12), channel_id=1, source_target_pairs={{0,16},{8,24},{16,32},{24,40},{32,48},{40,56},{48,64},{56,72},{64,... | collective-permute-start | bytes 196616 | tf_op jit(solution)/shard_map/ppermute | solution.py:65
  29.4 3.4 %collective-permute-start.3 = (f32[16,1024]{1,0:T(8,128)S(1)}, f32[16,1024]{1,0:T(8,128)S(1)}, u32[]{:S(2)}, u32[]{:S(2)}) collective-permute-start(f32[16,1024]{1,0:T(8,128)S(1)} %get-tuple-element.12), channel_id=1, source_target_pairs={{0,24},{8,32},{16,40},{24,48},{32,56},{40,64},{48,72},{56,80},{64,... | collective-permute-start | bytes 196616 | tf_op jit(solution)/shard_map/ppermute | solution.py:65
  32.9 1.9 collective-permute-done.3
  34.8 7.1 %collective-permute-start.4 = (f32[16,1024]{1,0:T(8,128)S(1)}, f32[16,1024]{1,0:T(8,128)S(1)}, u32[]{:S(2)}, u32[]{:S(2)}) collective-permute-start(f32[16,1024]{1,0:T(8,128)S(1)} %multiply_add_fusion.1), channel_id=1, source_target_pairs={{0,32},{8,40},{16,48},{24,56},{32,64},{40,72},{48,80},{56,88},{64,... | collective-permute-start | bytes 196616 | tf_op jit(solution)/shard_map/ppermute | solution.py:65
  41.8 1.6 collective-permute-start.5
  43.4 1.3 collective-permute-start.6
  44.7 1.3 collective-permute-done.6
  46.1 3.4 %finish_part.1 = bf16[384,1024]{1,0:T(8,128)(2,1)S(1)} custom-call(f32[48,8,1024]{2,1,0:T(8,128)S(1)} %get-tuple-element.9.y_ref, f32[48,8,1024]{2,1,0:T(8,128)S(1)} %get-tuple-element.10.qf_ref, f32[16,8,1024]{2,1,0:T(8,128)S(1)} %get-tuple-element.11.carry_ref, f32[16,1024]{1,0:T(8,128)S(1)} %multiply_add_fusion.entering_ref, f32[16,1024]{1,0:T(8,128)S(1)} %copy-done.3, ...), custom_call_target="tpu_custom_call" | custom-call | flops 15000000 | bytes 4000000 | tf_op jit(solution)/shard_map/finish_part/pallas_call | solution.py:192
  49.5 3.4 %collective-permute-start.10 = (bf16[384,1024]{1,0:T(8,128)(2,1)S(1)}, bf16[384,1024]{1,0:T(8,128)(2,1)}, u32[]{:S(2)}, u32[]{:S(2)}) collective-permute-start(bf16[384,1024]{1,0:T(8,128)(2,1)S(1)} %finish_part.1), channel_id=1, source_target_pairs={{0,4},{4,0},{1,5},{5,1},{2,6},{6,2},{3,7},{7,3},{8,12},{12,8},{9,1... | collective-permute-start | bytes 2359304 | tf_op jit(solution)/shard_map/ppermute | solution.py:33
  52.9 2.7 %collective-permute-start.7 = (bf16[384,1024]{1,0:T(8,128)(2,1)S(1)}, bf16[384,1024]{1,0:T(8,128)(2,1)S(1)}, u32[]{:S(2)}, u32[]{:S(2)}) collective-permute-start(bf16[384,1024]{1,0:T(8,128)(2,1)S(1)} %finish_part.1), channel_id=1, source_target_pairs={{0,3},{1,0},{2,1},{3,2},{4,7},{5,4},{6,5},{7,6},{8,11},{9,8},{10,9... | collective-permute-start | bytes 2359304 | tf_op jit(solution)/shard_map/ppermute | solution.py:33
  55.6 1.9 collective-permute-start.14
  57.5 11.3 %collective-permute-done.10 = bf16[384,1024]{1,0:T(8,128)(2,1)} collective-permute-done((bf16[384,1024]{1,0:T(8,128)(2,1)S(1)}, bf16[384,1024]{1,0:T(8,128)(2,1)}, u32[]{:S(2)}, u32[]{:S(2)}) %collective-permute-start.10) | collective-permute-done | bytes 786464 | tf_op jit(solution)/shard_map/ppermute | solution.py:33
  68.8 11.2 %collective-permute-start.11 = (bf16[384,1024]{1,0:T(8,128)(2,1)}, bf16[384,1024]{1,0:T(8,128)(2,1)S(1)}, u32[]{:S(2)}, u32[]{:S(2)}) collective-permute-start(bf16[384,1024]{1,0:T(8,128)(2,1)} %collective-permute-done.10), channel_id=1, source_target_pairs={{0,3},{1,0},{2,1},{3,2},{4,7},{5,4},{6,5},{7,6},{8,11},{9,8},{10,9... | collective-permute-start | bytes 2359304 | tf_op jit(solution)/shard_map/ppermute | solution.py:33
  80.3 12.3 %collective-permute-done.8 = bf16[384,1024]{1,0:T(8,128)(2,1)S(1)} collective-permute-done((bf16[384,1024]{1,0:T(8,128)(2,1)S(1)}, bf16[384,1024]{1,0:T(8,128)(2,1)S(1)}, u32[]{:S(2)}, u32[]{:S(2)}) %collective-permute-start.8) | collective-permute-done | bytes 786464 | tf_op jit(solution)/shard_map/ppermute | solution.py:33
  92.7 2.5 %collective-permute-start.9 = (bf16[384,1024]{1,0:T(8,128)(2,1)S(1)}, bf16[384,1024]{1,0:T(8,128)(2,1)S(1)}, u32[]{:S(2)}, u32[]{:S(2)}) collective-permute-start(bf16[384,1024]{1,0:T(8,128)(2,1)S(1)} %broadcast_select_fusion.3), channel_id=1, source_target_pairs={{0,1},{1,2},{2,3},{3,0},{8,11},{9,8},{10,9},{11,10},{4,5},{5,6},{6... | collective-permute-start | bytes 2359304 | tf_op jit(solution)/shard_map/ppermute | solution.py:33
  95.3 6.3 %collective-permute-start.22 = (bf16[1024,512]{1,0:T(8,128)(2,1)S(1)}, bf16[1024,512]{1,0:T(8,128)(2,1)S(1)}, u32[]{:S(2)}, u32[]{:S(2)}) collective-permute-start(bf16[1024,512]{1,0:T(8,128)(2,1)S(1)} %collective-permute-done.14), channel_id=1, source_target_pairs={{0,8},{8,0},{1,9},{9,1},{2,10},{10,2},{3,11},{11,3},{4,12},{12,4},... | collective-permute-start | bytes 3145736 | tf_op jit(solution)/shard_map/ppermute | solution.py:33
  101.5 7.1 %collective-permute-start.16 = (bf16[1024,512]{1,0:T(8,128)(2,1)S(1)}, bf16[1024,512]{1,0:T(8,128)(2,1)S(1)}, u32[]{:S(2)}, u32[]{:S(2)}) collective-permute-start(bf16[1024,512]{1,0:T(8,128)(2,1)S(1)} %collective-permute-done.14), channel_id=1, source_target_pairs={{0,16},{16,32},{32,48},{48,0},{1,17},{17,33},{33,49},{49,1},{2,18}... | collective-permute-start | bytes 3145736 | tf_op jit(solution)/shard_map/ppermute | solution.py:33
  108.7 0.9 collective-permute-done.12
  109.6 2.4 %collective-permute-start.18 = (bf16[1024,512]{1,0:T(8,128)(2,1)S(1)}, bf16[1024,512]{1,0:T(8,128)(2,1)S(1)}, u32[]{:S(2)}, u32[]{:S(2)}) collective-permute-start(bf16[1024,512]{1,0:T(8,128)(2,1)S(1)} %collective-permute-done.14), channel_id=1, source_target_pairs={{0,64},{64,0},{1,65},{65,1},{2,66},{66,2},{3,67},{67,3},{4,68},{68... | collective-permute-start | bytes 3145736 | tf_op jit(solution)/shard_map/ppermute | solution.py:33
  112.0 2.3 %collective-permute-start.13 = (bf16[384,1024]{1,0:T(8,128)(2,1)S(1)}, bf16[384,1024]{1,0:T(8,128)(2,1)S(1)}, u32[]{:S(2)}, u32[]{:S(2)}) collective-permute-start(bf16[384,1024]{1,0:T(8,128)(2,1)S(1)} %broadcast_select_fusion.2), channel_id=1, source_target_pairs={{0,1},{1,2},{2,3},{3,0},{8,11},{9,8},{10,9},{11,10},{4,5},{5,6},{6... | collective-permute-start | bytes 2359304 | tf_op jit(solution)/shard_map/ppermute | solution.py:33
  114.5 1.2 bitcast_dynamic-update-slice_fusion.3
  115.7 10.5 %collective-permute-done.15 = bf16[1024,512]{1,0:T(8,128)(2,1)S(1)} collective-permute-done((bf16[1024,512]{1,0:T(8,128)(2,1)S(1)}, bf16[1024,512]{1,0:T(8,128)(2,1)S(1)}, u32[]{:S(2)}, u32[]{:S(2)}) %collective-permute-start.15) | collective-permute-done | bytes 1048608 | tf_op jit(solution)/shard_map/ppermute | solution.py:33
  126.4 2.8 %collective-permute-start.17 = (bf16[1024,512]{1,0:T(8,128)(2,1)S(1)}, bf16[1024,512]{1,0:T(8,128)(2,1)S(1)}, u32[]{:S(2)}, u32[]{:S(2)}) collective-permute-start(bf16[1024,512]{1,0:T(8,128)(2,1)S(1)} %broadcast_select_fusion.1), channel_id=1, source_target_pairs={{0,16},{8,56},{16,32},{24,8},{32,48},{40,24},{48,0},{56,40},{1,17}... | collective-permute-start | bytes 3145736 | tf_op jit(solution)/shard_map/ppermute | solution.py:33
  129.1 1.2 collective-permute-done.18
  130.3 5.7 %collective-permute-start.26 = (bf16[1024,512]{1,0:T(8,128)(2,1)S(1)}, bf16[1024,512]{1,0:T(8,128)(2,1)S(1)}, u32[]{:S(2)}, u32[]{:S(2)}) collective-permute-start(bf16[1024,512]{1,0:T(8,128)(2,1)S(1)} %collective-permute-done.18), channel_id=1, source_target_pairs={{0,8},{8,0},{1,9},{9,1},{2,10},{10,2},{3,11},{11,3},{4,12},{12,4},... | collective-permute-start | bytes 3145736 | tf_op jit(solution)/shard_map/ppermute | solution.py:33
  136.1 1.8 collective-permute-start.20
  137.9 0.6 fusion.28
  138.5 0.4 collective-permute-start.23
  139.0 0.6 fusion.26
  139.5 0.6 fusion.16
  140.1 23.9 %collective-permute-done.19 = bf16[1024,512]{1,0:T(8,128)(2,1)S(1)} collective-permute-done((bf16[1024,512]{1,0:T(8,128)(2,1)S(1)}, bf16[1024,512]{1,0:T(8,128)(2,1)S(1)}, u32[]{:S(2)}, u32[]{:S(2)}) %collective-permute-start.19) | collective-permute-done | bytes 1048608 | tf_op jit(solution)/shard_map/ppermute | solution.py:33
  164.0 2.1 %collective-permute-done.20 = bf16[1024,512]{1,0:T(8,128)(2,1)S(1)} collective-permute-done((bf16[1024,512]{1,0:T(8,128)(2,1)S(1)}, bf16[1024,512]{1,0:T(8,128)(2,1)S(1)}, u32[]{:S(2)}, u32[]{:S(2)}) %collective-permute-start.20) | collective-permute-done | bytes 1048608 | tf_op jit(solution)/shard_map/ppermute | solution.py:33
  166.2 1.5 collective-permute-start.21
  167.8 4.4 %collective-permute-start.27 = (bf16[1024,512]{1,0:T(8,128)(2,1)S(1)}, bf16[1024,512]{1,0:T(8,128)(2,1)S(1)}, u32[]{:S(2)}, u32[]{:S(2)}) collective-permute-start(bf16[1024,512]{1,0:T(8,128)(2,1)S(1)} %collective-permute-done.19), channel_id=1, source_target_pairs={{0,8},{8,0},{1,9},{9,1},{2,10},{10,2},{3,11},{11,3},{4,12},{12,4},... | collective-permute-start | bytes 3145736 | tf_op jit(solution)/shard_map/ppermute | solution.py:33
  172.2 0.6 fusion.14
  172.8 0.6 fusion.22
  173.4 0.6 fusion
  174.0 0.6 fusion.1
  174.6 1.4 collective-permute-done.24
  176.3 3.9 %collective-permute-done.21 = bf16[1024,512]{1,0:T(8,128)(2,1)S(1)} collective-permute-done((bf16[1024,512]{1,0:T(8,128)(2,1)S(1)}, bf16[1024,512]{1,0:T(8,128)(2,1)S(1)}, u32[]{:S(2)}, u32[]{:S(2)}) %collective-permute-start.21) | collective-permute-done | bytes 1048608 | tf_op jit(solution)/shard_map/ppermute | solution.py:33
  180.2 7.2 %collective-permute-start.28 = (bf16[1024,512]{1,0:T(8,128)(2,1)S(1)}, bf16[1024,512]{1,0:T(8,128)(2,1)S(1)}, u32[]{:S(2)}, u32[]{:S(2)}) collective-permute-start(bf16[1024,512]{1,0:T(8,128)(2,1)S(1)} %collective-permute-done.21), channel_id=1, source_target_pairs={{0,8},{8,0},{1,9},{9,1},{2,10},{10,2},{3,11},{11,3},{4,12},{12,4},... | collective-permute-start | bytes 3145736 | tf_op jit(solution)/shard_map/ppermute | solution.py:33
  187.5 0.6 fusion.20
  188.1 0.6 fusion.3
  188.6 0.6 fusion.10
  189.2 0.6 fusion.2
  189.8 0.6 convolution_add_fusion.4
  190.4 0.6 fusion.4
  191.0 0.6 fusion.8
  191.6 0.6 fusion.5
  192.2 0.6 broadcast_select_fusion.5
  192.8 1.3 pad_maximum_fusion
  (46 shorter events, 1.8 us)
Async XLA Ops:
  2.3 5.5 %collective-permute-start = (f32[6,1024]{1,0:T(8,128)S(1)}, f32[6,1024]{1,0:T(8,128)S(1)}, u32[]{:S(2)}, u32[]{:S(2)}) collective-permute-start(f32[6,1024]{1,0:T(8,128)S(1)} %pad_maximum_fusion.1), channel_id=1, source_target_pairs={{0,8},{8,16},{16,24},{24,32},{32,40},{40,48},{48,56},{56,64},{64,7... | collective-permute-start | bytes 73736 | tf_op jit(solution)/shard_map/ppermute | solution.py:65
  7.8 1.4 copy-start
  9.2 1.4 copy-start.1
  10.6 1.4 copy-start.2
  12.1 0.8 copy-start.3
  12.9 0.8 copy-start.4
  13.7 0.7 copy-start.5
  22.0 10.8 %collective-permute-start.1 = (f32[16,1024]{1,0:T(8,128)S(1)}, f32[16,1024]{1,0:T(8,128)S(1)}, u32[]{:S(2)}, u32[]{:S(2)}) collective-permute-start(f32[16,1024]{1,0:T(8,128)S(1)} %get-tuple-element.12), channel_id=1, source_target_pairs={{0,8},{8,16},{16,24},{24,32},{32,40},{40,48},{48,56},{56,64},{64,7... | collective-permute-start | bytes 196616 | tf_op jit(solution)/shard_map/ppermute | solution.py:65
  26.3 6.6 %collective-permute-start.2 = (f32[16,1024]{1,0:T(8,128)S(1)}, f32[16,1024]{1,0:T(8,128)S(1)}, u32[]{:S(2)}, u32[]{:S(2)}) collective-permute-start(f32[16,1024]{1,0:T(8,128)S(1)} %get-tuple-element.12), channel_id=1, source_target_pairs={{0,16},{8,24},{16,32},{24,40},{32,48},{40,56},{48,64},{56,72},{64,... | collective-permute-start | bytes 196616 | tf_op jit(solution)/shard_map/ppermute | solution.py:65
  29.4 5.3 %collective-permute-start.3 = (f32[16,1024]{1,0:T(8,128)S(1)}, f32[16,1024]{1,0:T(8,128)S(1)}, u32[]{:S(2)}, u32[]{:S(2)}) collective-permute-start(f32[16,1024]{1,0:T(8,128)S(1)} %get-tuple-element.12), channel_id=1, source_target_pairs={{0,24},{8,32},{16,40},{24,48},{32,56},{40,64},{48,72},{56,80},{64,... | collective-permute-start | bytes 196616 | tf_op jit(solution)/shard_map/ppermute | solution.py:65
  34.8 9.9 %collective-permute-start.4 = (f32[16,1024]{1,0:T(8,128)S(1)}, f32[16,1024]{1,0:T(8,128)S(1)}, u32[]{:S(2)}, u32[]{:S(2)}) collective-permute-start(f32[16,1024]{1,0:T(8,128)S(1)} %multiply_add_fusion.1), channel_id=1, source_target_pairs={{0,32},{8,40},{16,48},{24,56},{32,64},{40,72},{48,80},{56,88},{64,... | collective-permute-start | bytes 196616 | tf_op jit(solution)/shard_map/ppermute | solution.py:65
  41.8 2.9 %collective-permute-start.5 = (f32[16,1024]{1,0:T(8,128)S(1)}, f32[16,1024]{1,0:T(8,128)S(1)}, u32[]{:S(2)}, u32[]{:S(2)}) collective-permute-start(f32[16,1024]{1,0:T(8,128)S(1)} %multiply_add_fusion.1), channel_id=1, source_target_pairs={{0,64},{8,72},{16,80},{24,88},{32,96},{40,104},{48,112},{56,120},{... | collective-permute-start | bytes 196616 | tf_op jit(solution)/shard_map/ppermute | solution.py:65
  43.4 2.6 %collective-permute-start.6 = (f32[16,1024]{1,0:T(8,128)S(1)}, f32[16,1024]{1,0:T(8,128)S(1)}, u32[]{:S(2)}, u32[]{:S(2)}) collective-permute-start(f32[16,1024]{1,0:T(8,128)S(1)} %multiply_add_fusion.1), channel_id=1, source_target_pairs={{0,96},{8,104},{16,112},{24,120},{1,97},{9,105},{17,113},{25,121},... | collective-permute-start | bytes 196616 | tf_op jit(solution)/shard_map/ppermute | solution.py:65
  49.5 19.3 %collective-permute-start.10 = (bf16[384,1024]{1,0:T(8,128)(2,1)S(1)}, bf16[384,1024]{1,0:T(8,128)(2,1)}, u32[]{:S(2)}, u32[]{:S(2)}) collective-permute-start(bf16[384,1024]{1,0:T(8,128)(2,1)S(1)} %finish_part.1), channel_id=1, source_target_pairs={{0,4},{4,0},{1,5},{5,1},{2,6},{6,2},{3,7},{7,3},{8,12},{12,8},{9,1... | collective-permute-start | bytes 2359304 | tf_op jit(solution)/shard_map/ppermute | solution.py:33
  52.9 27.4 %collective-permute-start.7 = (bf16[384,1024]{1,0:T(8,128)(2,1)S(1)}, bf16[384,1024]{1,0:T(8,128)(2,1)S(1)}, u32[]{:S(2)}, u32[]{:S(2)}) collective-permute-start(bf16[384,1024]{1,0:T(8,128)(2,1)S(1)} %finish_part.1), channel_id=1, source_target_pairs={{0,3},{1,0},{2,1},{3,2},{4,7},{5,4},{6,5},{7,6},{8,11},{9,8},{10,9... | collective-permute-start | bytes 2359304 | tf_op jit(solution)/shard_map/ppermute | solution.py:33
  55.6 37.0 %collective-permute-start.8 = (bf16[384,1024]{1,0:T(8,128)(2,1)S(1)}, bf16[384,1024]{1,0:T(8,128)(2,1)S(1)}, u32[]{:S(2)}, u32[]{:S(2)}) collective-permute-start(bf16[384,1024]{1,0:T(8,128)(2,1)S(1)} %finish_part.1), channel_id=1, source_target_pairs={{0,1},{1,2},{2,3},{3,0},{4,5},{5,6},{6,7},{7,4},{8,9},{9,10},{10,1... | collective-permute-start | bytes 2359304 | tf_op jit(solution)/shard_map/ppermute | solution.py:33
  55.6 39.6 %collective-permute-start.14 = (bf16[1024,512]{1,0:T(8,128)(2,1)}, bf16[1024,512]{1,0:T(8,128)(2,1)S(1)}, u32[]{:S(2)}, u32[]{:S(2)}) collective-permute-start(bf16[1024,512]{1,0:T(8,128)(2,1)} %param.15), channel_id=1, source_target_pairs={{0,0},{1,48},{2,32},{3,16},{4,64},{5,112},{6,96},{7,80},{8,8},{9,5... | collective-permute-start | bytes 3145736 | tf_op jit(solution)/shard_map/ppermute | solution.py:33
  68.8 32.7 %collective-permute-start.11 = (bf16[384,1024]{1,0:T(8,128)(2,1)}, bf16[384,1024]{1,0:T(8,128)(2,1)S(1)}, u32[]{:S(2)}, u32[]{:S(2)}) collective-permute-start(bf16[384,1024]{1,0:T(8,128)(2,1)} %collective-permute-done.10), channel_id=1, source_target_pairs={{0,3},{1,0},{2,1},{3,2},{4,7},{5,4},{6,5},{7,6},{8,11},{9,8},{10,9... | collective-permute-start | bytes 2359304 | tf_op jit(solution)/shard_map/ppermute | solution.py:33
  80.0 29.5 %collective-permute-start.12 = (bf16[384,1024]{1,0:T(8,128)(2,1)}, bf16[384,1024]{1,0:T(8,128)(2,1)S(1)}, u32[]{:S(2)}, u32[]{:S(2)}) collective-permute-start(bf16[384,1024]{1,0:T(8,128)(2,1)} %collective-permute-done.10), channel_id=1, source_target_pairs={{0,1},{1,2},{2,3},{3,0},{4,5},{5,6},{6,7},{7,4},{8,9},{9,10},{10,1... | collective-permute-start | bytes 2359304 | tf_op jit(solution)/shard_map/ppermute | solution.py:33
  92.7 19.3 %collective-permute-start.9 = (bf16[384,1024]{1,0:T(8,128)(2,1)S(1)}, bf16[384,1024]{1,0:T(8,128)(2,1)S(1)}, u32[]{:S(2)}, u32[]{:S(2)}) collective-permute-start(bf16[384,1024]{1,0:T(8,128)(2,1)S(1)} %broadcast_select_fusion.3), channel_id=1, source_target_pairs={{0,1},{1,2},{2,3},{3,0},{8,11},{9,8},{10,9},{11,10},{4,5},{5,6},{6... | collective-permute-start | bytes 2359304 | tf_op jit(solution)/shard_map/ppermute | solution.py:33
  95.3 43.3 %collective-permute-start.22 = (bf16[1024,512]{1,0:T(8,128)(2,1)S(1)}, bf16[1024,512]{1,0:T(8,128)(2,1)S(1)}, u32[]{:S(2)}, u32[]{:S(2)}) collective-permute-start(bf16[1024,512]{1,0:T(8,128)(2,1)S(1)} %collective-permute-done.14), channel_id=1, source_target_pairs={{0,8},{8,0},{1,9},{9,1},{2,10},{10,2},{3,11},{11,3},{4,12},{12,4},... | collective-permute-start | bytes 3145736 | tf_op jit(solution)/shard_map/ppermute | solution.py:33
  101.5 24.7 %collective-permute-start.15 = (bf16[1024,512]{1,0:T(8,128)(2,1)S(1)}, bf16[1024,512]{1,0:T(8,128)(2,1)S(1)}, u32[]{:S(2)}, u32[]{:S(2)}) collective-permute-start(bf16[1024,512]{1,0:T(8,128)(2,1)S(1)} %collective-permute-done.14), channel_id=1, source_target_pairs={{0,48},{16,0},{32,16},{48,32},{1,49},{17,1},{33,17},{49,33},{2,50}... | collective-permute-start | bytes 3145736 | tf_op jit(solution)/shard_map/ppermute | solution.py:33
  101.5 24.7 %collective-permute-start.16 = (bf16[1024,512]{1,0:T(8,128)(2,1)S(1)}, bf16[1024,512]{1,0:T(8,128)(2,1)S(1)}, u32[]{:S(2)}, u32[]{:S(2)}) collective-permute-start(bf16[1024,512]{1,0:T(8,128)(2,1)S(1)} %collective-permute-done.14), channel_id=1, source_target_pairs={{0,16},{16,32},{32,48},{48,0},{1,17},{17,33},{33,49},{49,1},{2,18}... | collective-permute-start | bytes 3145736 | tf_op jit(solution)/shard_map/ppermute | solution.py:33
  109.6 20.8 %collective-permute-start.18 = (bf16[1024,512]{1,0:T(8,128)(2,1)S(1)}, bf16[1024,512]{1,0:T(8,128)(2,1)S(1)}, u32[]{:S(2)}, u32[]{:S(2)}) collective-permute-start(bf16[1024,512]{1,0:T(8,128)(2,1)S(1)} %collective-permute-done.14), channel_id=1, source_target_pairs={{0,64},{64,0},{1,65},{65,1},{2,66},{66,2},{3,67},{67,3},{4,68},{68... | collective-permute-start | bytes 3145736 | tf_op jit(solution)/shard_map/ppermute | solution.py:33
  112.0 24.0 %collective-permute-start.13 = (bf16[384,1024]{1,0:T(8,128)(2,1)S(1)}, bf16[384,1024]{1,0:T(8,128)(2,1)S(1)}, u32[]{:S(2)}, u32[]{:S(2)}) collective-permute-start(bf16[384,1024]{1,0:T(8,128)(2,1)S(1)} %broadcast_select_fusion.2), channel_id=1, source_target_pairs={{0,1},{1,2},{2,3},{3,0},{8,11},{9,8},{10,9},{11,10},{4,5},{5,6},{6... | collective-permute-start | bytes 2359304 | tf_op jit(solution)/shard_map/ppermute | solution.py:33
  126.4 41.4 %collective-permute-start.17 = (bf16[1024,512]{1,0:T(8,128)(2,1)S(1)}, bf16[1024,512]{1,0:T(8,128)(2,1)S(1)}, u32[]{:S(2)}, u32[]{:S(2)}) collective-permute-start(bf16[1024,512]{1,0:T(8,128)(2,1)S(1)} %broadcast_select_fusion.1), channel_id=1, source_target_pairs={{0,16},{8,56},{16,32},{24,8},{32,48},{40,24},{48,0},{56,40},{1,17}... | collective-permute-start | bytes 3145736 | tf_op jit(solution)/shard_map/ppermute | solution.py:33
  130.3 41.8 %collective-permute-start.26 = (bf16[1024,512]{1,0:T(8,128)(2,1)S(1)}, bf16[1024,512]{1,0:T(8,128)(2,1)S(1)}, u32[]{:S(2)}, u32[]{:S(2)}) collective-permute-start(bf16[1024,512]{1,0:T(8,128)(2,1)S(1)} %collective-permute-done.18), channel_id=1, source_target_pairs={{0,8},{8,0},{1,9},{9,1},{2,10},{10,2},{3,11},{11,3},{4,12},{12,4},... | collective-permute-start | bytes 3145736 | tf_op jit(solution)/shard_map/ppermute | solution.py:33
  136.0 28.0 %collective-permute-start.19 = (bf16[1024,512]{1,0:T(8,128)(2,1)S(1)}, bf16[1024,512]{1,0:T(8,128)(2,1)S(1)}, u32[]{:S(2)}, u32[]{:S(2)}) collective-permute-start(bf16[1024,512]{1,0:T(8,128)(2,1)S(1)} %collective-permute-done.18), channel_id=1, source_target_pairs={{0,48},{16,0},{32,16},{48,32},{1,49},{17,1},{33,17},{49,33},{2,50}... | collective-permute-start | bytes 3145736 | tf_op jit(solution)/shard_map/ppermute | solution.py:33
  136.1 30.1 %collective-permute-start.20 = (bf16[1024,512]{1,0:T(8,128)(2,1)S(1)}, bf16[1024,512]{1,0:T(8,128)(2,1)S(1)}, u32[]{:S(2)}, u32[]{:S(2)}) collective-permute-start(bf16[1024,512]{1,0:T(8,128)(2,1)S(1)} %collective-permute-done.18), channel_id=1, source_target_pairs={{0,16},{16,32},{32,48},{48,0},{1,17},{17,33},{33,49},{49,1},{2,18}... | collective-permute-start | bytes 3145736 | tf_op jit(solution)/shard_map/ppermute | solution.py:33
  138.5 49.5 %collective-permute-start.23 = (bf16[1024,512]{1,0:T(8,128)(2,1)S(1)}, bf16[1024,512]{1,0:T(8,128)(2,1)S(1)}, u32[]{:S(2)}, u32[]{:S(2)}) collective-permute-start(bf16[1024,512]{1,0:T(8,128)(2,1)S(1)} %collective-permute-done.15), channel_id=1, source_target_pairs={{0,8},{8,0},{1,9},{9,1},{2,10},{10,2},{3,11},{11,3},{4,12},{12,4},... | collective-permute-start | bytes 3145736 | tf_op jit(solution)/shard_map/ppermute | solution.py:33
  164.0 26.4 %collective-permute-start.25 = (bf16[1024,512]{1,0:T(8,128)(2,1)S(1)}, bf16[1024,512]{1,0:T(8,128)(2,1)S(1)}, u32[]{:S(2)}, u32[]{:S(2)}) collective-permute-start(bf16[1024,512]{1,0:T(8,128)(2,1)S(1)} %collective-permute-done.16), channel_id=1, source_target_pairs={{0,8},{8,0},{1,9},{9,1},{2,10},{10,2},{3,11},{11,3},{4,12},{12,4},... | collective-permute-start | bytes 3145736 | tf_op jit(solution)/shard_map/ppermute | solution.py:33
  166.2 14.0 %collective-permute-start.21 = (bf16[1024,512]{1,0:T(8,128)(2,1)S(1)}, bf16[1024,512]{1,0:T(8,128)(2,1)S(1)}, u32[]{:S(2)}, u32[]{:S(2)}) collective-permute-start(bf16[1024,512]{1,0:T(8,128)(2,1)S(1)} %broadcast_select_fusion), channel_id=1, source_target_pairs={{0,16},{8,56},{16,32},{24,8},{32,48},{40,24},{48,0},{56,40},{1,17}... | collective-permute-start | bytes 3145736 | tf_op jit(solution)/shard_map/ppermute | solution.py:33
  167.8 23.8 %collective-permute-start.27 = (bf16[1024,512]{1,0:T(8,128)(2,1)S(1)}, bf16[1024,512]{1,0:T(8,128)(2,1)S(1)}, u32[]{:S(2)}, u32[]{:S(2)}) collective-permute-start(bf16[1024,512]{1,0:T(8,128)(2,1)S(1)} %collective-permute-done.19), channel_id=1, source_target_pairs={{0,8},{8,0},{1,9},{9,1},{2,10},{10,2},{3,11},{11,3},{4,12},{12,4},... | collective-permute-start | bytes 3145736 | tf_op jit(solution)/shard_map/ppermute | solution.py:33
  172.1 3.8 %collective-permute-start.24 = (bf16[1024,512]{1,0:T(8,128)(2,1)S(1)}, bf16[1024,512]{1,0:T(8,128)(2,1)S(1)}, u32[]{:S(2)}, u32[]{:S(2)}) collective-permute-start(bf16[1024,512]{1,0:T(8,128)(2,1)S(1)} %collective-permute-done.17), channel_id=1, source_target_pairs={{0,8},{8,0},{1,9},{9,1},{2,10},{10,2},{3,11},{11,3},{4,12},{12,4},... | collective-permute-start | bytes 3145736 | tf_op jit(solution)/shard_map/ppermute | solution.py:33
  175.9 16.2 %collective-permute-start.29 = (bf16[1024,512]{1,0:T(8,128)(2,1)S(1)}, bf16[1024,512]{1,0:T(8,128)(2,1)S(1)}, u32[]{:S(2)}, u32[]{:S(2)}) collective-permute-start(bf16[1024,512]{1,0:T(8,128)(2,1)S(1)} %collective-permute-done.20), channel_id=1, source_target_pairs={{0,8},{8,0},{1,9},{9,1},{2,10},{10,2},{3,11},{11,3},{4,12},{12,4},... | collective-permute-start | bytes 3145736 | tf_op jit(solution)/shard_map/ppermute | solution.py:33
  180.2 10.7 %collective-permute-start.28 = (bf16[1024,512]{1,0:T(8,128)(2,1)S(1)}, bf16[1024,512]{1,0:T(8,128)(2,1)S(1)}, u32[]{:S(2)}, u32[]{:S(2)}) collective-permute-start(bf16[1024,512]{1,0:T(8,128)(2,1)S(1)} %collective-permute-done.21), channel_id=1, source_target_pairs={{0,8},{8,0},{1,9},{9,1},{2,10},{10,2},{3,11},{11,3},{4,12},{12,4},... | collective-permute-start | bytes 3145736 | tf_op jit(solution)/shard_map/ppermute | solution.py:33

commit v2 on v1

--- a/solution.py
+++ b/solution.py
@@ -60,9 +60,8 @@
     return permute(value, AXES, move)
 
 
-def later(value, by):
-    size = 16
-    return lax.ppermute(value, CTX, [(i, i + by) for i in range(size - by)])
+def tie(*values):
+    return lax.optimization_barrier(values)
 
 
 def rows_of(ref, j, seg_len):
@@ -78,7 +77,7 @@
     def spread(row):
         return jnp.broadcast_to(row, wide)
 
-    taps = [[spread(taps_ref[3 * a + b : 3 * a + b + 1, :]) for b in range(3)] for a in range(3)]
+    taps = [[spread(taps_ref[a, b : b + 1, :]) for b in range(3)] for a in range(3)]
     skip = spread(skip_ref[...])
     poles = [spread(pole[m : m + 1, :]) for m in range(modes)]
     gains = [spread(res_ref[m : m + 1, :]) for m in range(modes)]
@@ -88,7 +87,7 @@
         return jnp.where(sub == 0, spread(halo_ref[halo_row : halo_row + 1, :]), rolled)
 
     refs = (q_ref, k_ref, v_ref)
-    past = tuple((before(ref, 1, 2 * a + 1), before(ref, 2, 2 * a)) for a, ref in enumerate(refs))
+    past = tuple((before(ref, 1, 8 * a + 7), before(ref, 2, 8 * a + 6)) for a, ref in enumerate(refs))
 
     def step(j, carried):
         past, states = carried
@@ -150,6 +149,27 @@
     hidden_ref[...] = rows_ref[...].astype(jnp.bfloat16)
 
 
+def tail_kernel(q_ref, k_ref, v_ref, out_ref):
+    out_ref[0:8, :] = q_ref[...]
+    out_ref[8:16, :] = k_ref[...]
+    out_ref[16:24, :] = v_ref[...]
+
+
+def last_tokens(q, k, v):
+    rows, channels = q.shape
+    last = pl.BlockSpec((8, channels), lambda i: (rows // 8 - 1, 0))
+    return pl.pallas_call(
+        tail_kernel,
+        grid=(1,),
+        in_specs=[last] * 3,
+        out_specs=pl.BlockSpec((24, channels), lambda i: (0, 0)),
+        out_shape=jax.ShapeDtypeStruct((24, channels), jnp.float32),
+        compiler_params=pltpu.CompilerParams(vmem_limit_bytes=56 * 2**20),
+        cost_estimate=pl.CostEstimate(flops=0, bytes_accessed=0, transcendentals=0),
+        name="last_tokens",
+    )(q, k, v)
+
+
 def local_part(q, k, v, halo, taps, rates, res, skip):
     rows, channels = q.shape
     modes = rates.shape[0]
@@ -165,7 +185,7 @@
     return pl.pallas_call(
         functools.partial(local_kernel, seg_len, modes),
         grid=(channels // LANES,),
-        in_specs=[tall, tall, tall, short(6), short(9), short(modes), short(modes), short(1)],
+        in_specs=[tall, tall, tall, short(24), pl.BlockSpec((3, 3, LANES), lambda c: (0, 0, c)), short(modes), short(modes), short(1)],
         out_specs=[cube, cube, short(modes), mode_cube],
         out_shape=[
             jax.ShapeDtypeStruct((seg_len, SEGS, channels), f32),
@@ -173,8 +193,8 @@
             jax.ShapeDtypeStruct((modes, channels), f32),
             jax.ShapeDtypeStruct((modes, SEGS, channels), f32),
         ],
-        compiler_params=pltpu.CompilerParams(vmem_limit_bytes=24 * 2**20),
-        cost_estimate=pl.CostEstimate(flops=40_000_000, bytes_accessed=9_000_000, transcendentals=0),
+        compiler_params=pltpu.CompilerParams(vmem_limit_bytes=56 * 2**20),
+        cost_estimate=pl.CostEstimate(flops=0, bytes_accessed=0, transcendentals=0),
         name="local_part",
     )(q, k, v, halo, taps, rates, res, skip)
 
@@ -196,8 +216,8 @@
         out_specs=pl.BlockSpec((rows, LANES), lambda c: (0, c)),
         out_shape=jax.ShapeDtypeStruct((rows, channels), jnp.bfloat16),
         scratch_shapes=[pltpu.VMEM((rows, LANES), jnp.float32)],
-        compiler_params=pltpu.CompilerParams(vmem_limit_bytes=24 * 2**20),
-        cost_estimate=pl.CostEstimate(flops=15_000_000, bytes_accessed=4_000_000, transcendentals=0),
+        compiler_params=pltpu.CompilerParams(vmem_limit_bytes=56 * 2**20),
+        cost_estimate=pl.CostEstimate(flops=0, bytes_accessed=0, transcendentals=0),
         name="finish_part",
     )(y, qf, carry, entering, rates, res)
 
@@ -206,55 +226,115 @@
     return jnp.where(lax.axis_index("core") == 0, first, second)
 
 
-def spread_over(own, ring, pair):
-    got = {(0, 0): own}
-    got[0, -1] = moved(own, ring, 1)
-    got[0, 1] = moved(own, ring, -1)
-    got[1, 0] = moved(own, pair, 1)
-    got[0, 2] = onward(pick(got[0, -1], got[0, 1]), ring)
-    got[1, -1] = moved(got[1, 0], ring, 1)
-    got[1, 1] = moved(got[1, 0], ring, -1)
-    got[1, 2] = onward(pick(got[1, -1], got[1, 1]), ring)
-    return got
+def entering_state(total, decay, also):
+    core, x, zl = lax.axis_index("core"), lax.axis_index("x"), lax.axis_index("zl")
+    beside = moved(total, "core", 1)
+    chip = jnp.where(core == 0, decay(1) * total + beside, decay(1) * beside + total)
+    near = jnp.zeros_like(total)
+    plane = decay(2 * (3 - x)) * chip
+    for back in (1, 2, 3):
+        came = moved(chip, "x", back)
+        near = near + jnp.where(x >= back, decay(2 * back - 2) * came, 0.0)
+        plane = plane + decay(2 * (3 - (x - back) % 4)) * came
+    plane, also = tie(plane, also)
+    before = moved(plane, "zl", 1)
+    at_chip = near + jnp.where(zl == 1, decay(2 * x) * before, 0.0)
+    return jnp.where(core == 0, at_chip, decay(1) * at_chip + beside), also
 
 
 def on_device(q, k, v, short_taps, rates, res, skip, weight):
     channels = rates.shape[1]
-    halo = later(jnp.concatenate([q[-2:], k[-2:], v[-2:]], axis=0), 1)
+    rows = q.shape[0]
+    tails = last_tokens(q, k, v)
+    ctx_at = lax.axis_index(CTX)
+
+    def onto_next(at):
+        index = (place(CTX, at) + 1) % 16
+        return {"zl": index // 8, "x": index // 2 % 4, "core": index % 2}
+
+    halo, weight = tie(permute(tails, CTX, onto_next), weight)
+    halo = jnp.where(ctx_at == 0, 0.0, halo)
     block = turned(weight)
     y, qf, total, carry = local_part(
-        q, k, v, halo, short_taps.reshape(9, channels), rates, res, skip.reshape(1, channels)
+        q, k, v, halo, short_taps, rates, res, skip.reshape(1, channels)
     )
-    rows = q.shape[0]
-
-    def device_decay(times):
-        return jnp.exp(-rates * float(rows * times))
-
-    near = later(total, 1) + device_decay(1) * later(total, 2) + device_decay(2) * later(total, 3)
-    window = total + device_decay(1) * near
-    entering = (
-        near
-        + device_decay(3) * later(window, 4)
-        + device_decay(7) * later(window, 8)
-        + device_decay(11) * later(window, 12)
+
+    def decay(times):
+        return jnp.exp(-rates * jnp.asarray(rows * times, jnp.float32))
+
+    def turn_x(block):
+        return onward(block, "x")
+
+    def turn_y(block):
+        return onward(block, "y")
+
+    def across(block):
+        return moved(block, "zl", 1)
+
+    def swap(block):
+        return moved(block, "core", 1)
+
+    entering, block = entering_state(total, decay, block)
+    w, s, h = {(0, 0): block}, {}, {}
+    w[0, 1] = turn_x(block)
+    hidden = finish_part(y, qf, carry, entering, rates, res)
+
+    hidden, w[0, 1] = tie(hidden, w[0, 1])
+    h[0, 0] = hidden
+    plus, minus = moved(hidden, "y", 1), moved(hidden, "y", -1)
+    h[1, 0] = moved(hidden, "zh", 1)
+    w[1, 0] = across(block)
+    w[0, 2] = turn_x(w[0, 1])
+
+    plus, minus, h[1, 0], w[1, 0], w[0, 2] = tie(plus, minus, h[1, 0], w[1, 0], w[0, 2])
+    h[0, 1], h[0, 3] = plus, minus
+    h[0, 2] = onward(pick(plus, minus), "y")
+    plus, minus = moved(h[1, 0], "y", 1), moved(h[1, 0], "y", -1)
+    w[0, 3] = turn_x(w[0, 2])
+    w[1, 1] = turn_x(w[1, 0])
+
+    plus, minus, h[0, 2], w[0, 1], w[0, 2], w[0, 3], w[1, 0], w[1, 1] = tie(
+        plus, minus, h[0, 2], w[0, 1], w[0, 2], w[0, 3], w[1, 0], w[1, 1]
     )
-    hidden = finish_part(y, qf, carry, entering, rates, res)
-
-    weights = spread_over(block, "x", "zl")
-    hiddens = spread_over(hidden, "y", "zh")
-
-    slots = [(a, b) for a in (0, 1) for b in (0, 1, 2, -1)]
-    held = jnp.stack([hiddens[s] for s in slots])
+    w[1, 3] = across(w[0, 3])
+    w[1, 2] = turn_x(w[1, 1])
+    for at in ((0, 0), (0, 1), (0, 2), (0, 3), (1, 0), (1, 1)):
+        s[at] = swap(w[at])
+    h[1, 1], h[1, 3] = plus, minus
+    h[1, 2] = onward(pick(plus, minus), "y")
+    for at in ((1, 2), (1, 3)):
+        s[at] = swap(w[at])
+
+    slots = [(a, b) for a in (0, 1) for b in range(4)]
+    late = h[1, 2]
+    held = jnp.stack([jnp.zeros_like(late) if at == (1, 2) else h[at] for at in slots])
     flip = (lax.axis_index("zh") + lax.axis_index("zl")) % 2
-    turn = lax.axis_index("y") - lax.axis_index("x")
+    apart = lax.axis_index("y") - lax.axis_index("x")
+    sign = jnp.where(lax.axis_index("core") == 0, 1, -1)
     own = jnp.zeros((rows, weight.shape[1]), jnp.float32)
     other = jnp.zeros((rows, weight.shape[1]), jnp.float32)
+
+    def dot(a, b):
+        return jnp.dot(a, b, preferred_element_type=jnp.float32)
+
+    def term(a, b):
+        slot = ((a + flip) % 2) * 4 + (-apart - b) % 4
+        return lax.dynamic_index_in_dim(held, slot, 0, keepdims=False)
+
     for a, b in slots:
-        swapped = moved(weights[a, b], "core", 1)
-        slot = ((a + flip) % 2) * 4 + (turn - b) % 4
-        term = lax.dynamic_index_in_dim(held, slot, 0, keepdims=False)
-        own = own + jnp.dot(term, weights[a, b], preferred_element_type=jnp.float32)
-        other = other + jnp.dot(term, swapped, preferred_element_type=jnp.float32)
+        own = own + dot(term(a, sign * b), w[a, b])
+        other = other + dot(term(a, -sign * b), s[a, b])
+
+    def add_late(at_own, at_other):
+        def add(own, other, late):
+            return own + dot(late, w[at_own]), other + dot(late, s[at_other])
+
+        return add
+
+    plane = (1 + flip) % 2
+    ring = (-apart - 2) % 4
+    branches = [add_late((a, b), (a, (-b) % 4)) for a in (0, 1) for b in range(4)]
+    own, other = lax.switch(plane * 4 + (sign * ring) % 4, branches, own, other, late)
     first = lax.axis_index("core") == 0
     return jnp.concatenate([jnp.where(first, own, other), jnp.where(first, other, own)], axis=1)
 

time: 198 us -> 164 us (0.83)
  the two profiles are of different devices: /device:TPU:1 before, /device:TPU:6 now
where the time goes in v2:
time: 164 us; the launch traced here: 162 us
  waiting for transfers between devices  69.6 us (42%)
  starting transfers between devices  44 us (27%)
  Pallas kernels  18.4 us (11%)
  matrix products  16.6 us (10%)
  local copies, waits for them, and re-layouts  7.24 us (4%)
  other arithmetic  5.89 us (4%)
    ppermute x29, waiting for transfers between devices, permute(): return lax.ppermute(value, axes, pairs)  69.6 us
    ppermute x29, starting transfers between devices, permute(): return lax.ppermute(value, axes, pairs)  44 us
    dot_general x18, matrix products, dot(): return jnp.dot(a, b, preferred_element_type=jnp.float32)  16.6 us
    pallas_call x1, Pallas kernels, local_part(): pl.pallas_call(functools.partial(local_kernel, seg_len, modes), grid=(cha...  9.96 us
    pallas_call x1, Pallas kernels, finish_part(): pl.pallas_call(functools.partial(finish_kernel, seg_len, modes), grid=(ch...  7.01 us
    unnamed x19, local copies, waits for them, and re-layouts  6.06 us
  transfers between devices with their start and end apart: 29, of which 15 were waited for; matrix products, arithmetic and copies ran while one was open for 16% of the time, Pallas kernels for 10%

profile of v2, /device:TPU:6, one launch (start us, length us, event | category | flops | bytes accessed | tf_op | source)
XLA Modules:
  0.0 162.2 jit_solution(10996416749000559604)
XLA Ops:
  0.0 1.5 last_tokens.1
  1.5 4.2 %collective-permute-done = f32[24,1024]{1,0:T(8,128)S(1)} collective-permute-done((f32[24,1024]{1,0:T(8,128)}, f32[24,1024]{1,0:T(8,128)S(1)}, u32[]{:S(2)}, u32[]{:S(2)}) %collective-permute-start) | collective-permute-done | bytes 98336 | tf_op jit(solution)/shard_map/ppermute | solution.py:33
  5.7 5.2 %collective-permute-start.5 = (bf16[1024,512]{1,0:T(8,128)(2,1)}, bf16[1024,512]{1,0:T(8,128)(2,1)}, u32[]{:S(2)}, u32[]{:S(2)}) collective-permute-start(bf16[1024,512]{1,0:T(8,128)(2,1)} %param.23), channel_id=1, source_target_pairs={{0,0},{1,48},{2,32},{3,16},{4,64},{5,112},{6,96},{7,80},{8,8},{9,5... | collective-permute-start | bytes 3145736 | tf_op jit(solution)/shard_map/ppermute | solution.py:33
  10.9 0.6 broadcast_select_fusion.4.halo_ref
  11.6 10.0 %local_part.1 = (f32[48,8,1024]{2,1,0:T(8,128)}, f32[48,8,1024]{2,1,0:T(8,128)}, f32[16,1024]{1,0:T(8,128)}, f32[16,8,1024]{2,1,0:T(8,128)}) custom-call(f32[384,1024]{1,0:T(8,128)} %q_ref.3, f32[384,1024]{1,0:T(8,128)} %k_ref.3, f32[384,1024]{1,0:T(8,128)} %v_ref.3, f32[24,1024]{1,0:T(8,128)} %broadcast_select_fusion.4.halo_ref, f32[3,3,1024]{2,1,0:T(4,128)} %taps_ref.1, ...), custom_call_target="tpu_custom_call" | custom-call | tf_op jit(solution)/shard_map/local_part/pallas_call | solution.py:185
  21.6 1.4 collective-permute-done.1
  23.1 0.9 add_select_fusion.1
  23.9 2.9 %collective-permute-start.4 = (f32[16,1024]{1,0:T(8,128)S(1)}, f32[16,1024]{1,0:T(8,128)S(1)}, u32[]{:S(2)}, u32[]{:S(2)}) collective-permute-start(f32[16,1024]{1,0:T(8,128)S(1)} %add_select_fusion.1), channel_id=1, source_target_pairs={{0,48},{16,0},{32,16},{48,32},{1,49},{17,1},{33,17},{49,33},{2,50}... | collective-permute-start | bytes 196616 | tf_op jit(solution)/shard_map/ppermute | solution.py:33
  26.8 5.4 %collective-permute-start.3 = (f32[16,1024]{1,0:T(8,128)S(1)}, f32[16,1024]{1,0:T(8,128)S(1)}, u32[]{:S(2)}, u32[]{:S(2)}) collective-permute-start(f32[16,1024]{1,0:T(8,128)S(1)} %add_select_fusion.1), channel_id=1, source_target_pairs={{0,32},{16,48},{32,0},{48,16},{1,33},{17,49},{33,1},{49,17},{2,34}... | collective-permute-start | bytes 196616 | tf_op jit(solution)/shard_map/ppermute | solution.py:33
  32.2 2.6 %collective-permute-done.4 = f32[16,1024]{1,0:T(8,128)S(1)} collective-permute-done((f32[16,1024]{1,0:T(8,128)S(1)}, f32[16,1024]{1,0:T(8,128)S(1)}, u32[]{:S(2)}, u32[]{:S(2)}) %collective-permute-start.4) | collective-permute-done | bytes 65568 | tf_op jit(solution)/shard_map/ppermute | solution.py:33
  34.8 1.0 collective-permute-done.3
  35.8 1.2 collective-permute-done.2
  37.0 2.7 %collective-permute-start.7 = (bf16[1024,512]{1,0:T(8,128)(2,1)}, bf16[1024,512]{1,0:T(8,128)(2,1)S(1)}, u32[]{:S(2)}, u32[]{:S(2)}) collective-permute-start(bf16[1024,512]{1,0:T(8,128)(2,1)} %collective-permute-done.5), channel_id=1, source_target_pairs={{0,16},{8,56},{16,32},{24,8},{32,48},{40,24},{48,0},{56,40},{1,17}... | collective-permute-start | bytes 3145736 | tf_op jit(solution)/shard_map/ppermute | solution.py:33
  39.8 3.3 %collective-permute-start.6 = (f32[16,1024]{1,0:T(8,128)S(1)}, f32[16,1024]{1,0:T(8,128)S(1)}, u32[]{:S(2)}, u32[]{:S(2)}) collective-permute-start(f32[16,1024]{1,0:T(8,128)S(1)} %multiply_add_fusion), channel_id=1, source_target_pairs={{0,64},{64,0},{1,65},{65,1},{2,66},{66,2},{3,67},{67,3},{4,68},{68... | collective-permute-start | bytes 196616 | tf_op jit(solution)/shard_map/ppermute | solution.py:33
  43.1 3.0 %collective-permute-done.6 = f32[16,1024]{1,0:T(8,128)S(1)} collective-permute-done((f32[16,1024]{1,0:T(8,128)S(1)}, f32[16,1024]{1,0:T(8,128)S(1)}, u32[]{:S(2)}, u32[]{:S(2)}) %collective-permute-start.6) | collective-permute-done | bytes 65568 | tf_op jit(solution)/shard_map/ppermute | solution.py:33
  46.0 0.7 add_select_fusion.entering_ref
  46.7 7.0 %finish_part.1 = bf16[384,1024]{1,0:T(8,128)(2,1)} custom-call(f32[48,8,1024]{2,1,0:T(8,128)} %get-tuple-element.151.y_ref, f32[48,8,1024]{2,1,0:T(8,128)} %get-tuple-element.152.qf_ref, f32[16,8,1024]{2,1,0:T(8,128)} %get-tuple-element.153.carry_ref, f32[16,1024]{1,0:T(8,128)} %add_select_fusion.entering_ref, f32[16,1024]{1,0:T(8,128)} %rates_ref.3, ...), custom_call_target="tpu_custom_call" | custom-call | tf_op jit(solution)/shard_map/finish_part/pallas_call | solution.py:212
  53.8 2.2 %collective-permute-start.12 = (bf16[1024,512]{1,0:T(8,128)(2,1)S(1)}, bf16[1024,512]{1,0:T(8,128)(2,1)}, u32[]{:S(2)}, u32[]{:S(2)}) collective-permute-start(bf16[1024,512]{1,0:T(8,128)(2,1)S(1)} %collective-permute-done.7), channel_id=1, source_target_pairs={{0,16},{8,56},{16,32},{24,8},{32,48},{40,24},{48,0},{56,40},{1,17}... | collective-permute-start | bytes 3145736 | tf_op jit(solution)/shard_map/ppermute | solution.py:33
  56.4 2.8 %collective-permute-start.9 = (bf16[384,1024]{1,0:T(8,128)(2,1)}, bf16[384,1024]{1,0:T(8,128)(2,1)S(1)}, u32[]{:S(2)}, u32[]{:S(2)}) collective-permute-start(bf16[384,1024]{1,0:T(8,128)(2,1)} %finish_part.1), channel_id=1, source_target_pairs={{0,3},{1,0},{2,1},{3,2},{4,7},{5,4},{6,5},{7,6},{8,11},{9,8},{10,9... | collective-permute-start | bytes 2359304 | tf_op jit(solution)/shard_map/ppermute | solution.py:33
  59.2 3.4 %collective-permute-start.10 = (bf16[384,1024]{1,0:T(8,128)(2,1)}, bf16[384,1024]{1,0:T(8,128)(2,1)}, u32[]{:S(2)}, u32[]{:S(2)}) collective-permute-start(bf16[384,1024]{1,0:T(8,128)(2,1)} %finish_part.1), channel_id=1, source_target_pairs={{0,4},{4,0},{1,5},{5,1},{2,6},{6,2},{3,7},{7,3},{8,12},{12,8},{9,1... | collective-permute-start | bytes 2359304 | tf_op jit(solution)/shard_map/ppermute | solution.py:33
  62.6 6.7 %collective-permute-done.11 = bf16[1024,512]{1,0:T(8,128)(2,1)S(1)} collective-permute-done((bf16[1024,512]{1,0:T(8,128)(2,1)}, bf16[1024,512]{1,0:T(8,128)(2,1)S(1)}, u32[]{:S(2)}, u32[]{:S(2)}) %collective-permute-start.11) | collective-permute-done | bytes 1048608 | tf_op jit(solution)/shard_map/ppermute | solution.py:33
  69.3 3.7 %collective-permute-done.8 = bf16[384,1024]{1,0:T(8,128)(2,1)S(1)} collective-permute-done((bf16[384,1024]{1,0:T(8,128)(2,1)}, bf16[384,1024]{1,0:T(8,128)(2,1)S(1)}, u32[]{:S(2)}, u32[]{:S(2)}) %collective-permute-start.8) | collective-permute-done | bytes 786464 | tf_op jit(solution)/shard_map/ppermute | solution.py:33
  73.0 10.1 %collective-permute-done.10 = bf16[384,1024]{1,0:T(8,128)(2,1)} collective-permute-done((bf16[384,1024]{1,0:T(8,128)(2,1)}, bf16[384,1024]{1,0:T(8,128)(2,1)}, u32[]{:S(2)}, u32[]{:S(2)}) %collective-permute-start.10) | collective-permute-done | bytes 786464 | tf_op jit(solution)/shard_map/ppermute | solution.py:33
  83.1 1.6 collective-permute-start.13
  84.7 2.2 %collective-permute-start.14 = (bf16[384,1024]{1,0:T(8,128)(2,1)}, bf16[384,1024]{1,0:T(8,128)(2,1)}, u32[]{:S(2)}, u32[]{:S(2)}) collective-permute-start(bf16[384,1024]{1,0:T(8,128)(2,1)} %collective-permute-done.10), channel_id=1, source_target_pairs={{0,3},{1,0},{2,1},{3,2},{4,7},{5,4},{6,5},{7,6},{8,11},{9,8},{10,9... | collective-permute-start | bytes 2359304 | tf_op jit(solution)/shard_map/ppermute | solution.py:33
  86.9 3.1 %collective-permute-start.16 = (bf16[1024,512]{1,0:T(8,128)(2,1)}, bf16[1024,512]{1,0:T(8,128)(2,1)}, u32[]{:S(2)}, u32[]{:S(2)}) collective-permute-start(bf16[1024,512]{1,0:T(8,128)(2,1)} %collective-permute-done.12), channel_id=1, source_target_pairs={{0,16},{8,56},{16,32},{24,8},{32,48},{40,24},{48,0},{56,40},{1,17}... | collective-permute-start | bytes 3145736 | tf_op jit(solution)/shard_map/ppermute | solution.py:33
  90.0 1.4 collective-permute-start.17
  91.4 1.0 broadcast_select_fusion.1
  92.4 1.2 bitcast_dynamic-update-slice_fusion.6
  93.6 1.2 bitcast_dynamic-update-slice_fusion.5
  94.7 8.1 %collective-permute-done.13 = bf16[384,1024]{1,0:T(8,128)(2,1)} collective-permute-done((bf16[384,1024]{1,0:T(8,128)(2,1)}, bf16[384,1024]{1,0:T(8,128)(2,1)}, u32[]{:S(2)}, u32[]{:S(2)}) %collective-permute-start.13) | collective-permute-done | bytes 786464 | tf_op jit(solution)/shard_map/ppermute | solution.py:33
  102.9 2.7 %collective-permute-done.14 = bf16[384,1024]{1,0:T(8,128)(2,1)} collective-permute-done((bf16[384,1024]{1,0:T(8,128)(2,1)}, bf16[384,1024]{1,0:T(8,128)(2,1)}, u32[]{:S(2)}, u32[]{:S(2)}) %collective-permute-start.14) | collective-permute-done | bytes 786464 | tf_op jit(solution)/shard_map/ppermute | solution.py:33
  105.5 5.7 %collective-permute-done.15 = bf16[384,1024]{1,0:T(8,128)(2,1)} collective-permute-done((bf16[384,1024]{1,0:T(8,128)(2,1)}, bf16[384,1024]{1,0:T(8,128)(2,1)}, u32[]{:S(2)}, u32[]{:S(2)}) %collective-permute-start.15) | collective-permute-done | bytes 786464 | tf_op jit(solution)/shard_map/ppermute | solution.py:33
  111.3 2.5 %collective-permute-done.17 = bf16[1024,512]{1,0:T(8,128)(2,1)} collective-permute-done((bf16[1024,512]{1,0:T(8,128)(2,1)S(1)}, bf16[1024,512]{1,0:T(8,128)(2,1)}, u32[]{:S(2)}, u32[]{:S(2)}) %collective-permute-start.17) | collective-permute-done | bytes 1048608 | tf_op jit(solution)/shard_map/ppermute | solution.py:33
  113.8 3.8 %collective-permute-start.19 = (bf16[1024,512]{1,0:T(8,128)(2,1)}, bf16[1024,512]{1,0:T(8,128)(2,1)S(1)}, u32[]{:S(2)}, u32[]{:S(2)}) collective-permute-start(bf16[1024,512]{1,0:T(8,128)(2,1)} %collective-permute-done.17), channel_id=1, source_target_pairs={{0,16},{8,56},{16,32},{24,8},{32,48},{40,24},{48,0},{56,40},{1,17}... | collective-permute-start | bytes 3145736 | tf_op jit(solution)/shard_map/ppermute | solution.py:33
  118.0 1.2 bitcast_dynamic-update-slice_fusion.4
  119.2 1.2 bitcast_dynamic-update-slice_fusion.2
  120.4 1.2 broadcast_select_fusion
  121.7 1.2 bitcast_dynamic-update-slice_fusion.1
  122.9 1.2 bitcast_dynamic-update-slice_fusion
  124.4 1.8 %fusion.26 = f32[384,512]{1,0:T(8,128)S(1)} fusion(bf16[1024,512]{1,0:T(8,128)(2,1)} %collective-permute-done.17, bf16[8,384,1024]{2,1,0:T(8,128)(2,1)S(1)} %bitcast_dynamic-update-slice_fusion, s32[]{:T(128)S(6)} %select_n.265), kind=kOutput, calls=%fused_computation.46 | convolution fusion | flops 402653184 | bytes 2621444 | tf_op jit(solution)/shard_map/dot_general | solution.py:318
  126.2 0.6 fusion.30
  126.8 1.8 %fusion.32 = f32[384,512]{1,0:T(8,128)S(1)} fusion(bf16[1024,512]{1,0:T(8,128)(2,1)} %collective-permute-done.16, bf16[8,384,1024]{2,1,0:T(8,128)(2,1)S(1)} %bitcast_dynamic-update-slice_fusion, s32[]{:T(128)S(6)} %select_n.263), kind=kOutput, calls=%fused_computation.52 | convolution fusion | flops 402653184 | bytes 2621444 | tf_op jit(solution)/shard_map/dot_general | solution.py:318
  128.6 1.8 %fusion.34 = f32[384,512]{1,0:T(8,128)S(1)} fusion(bf16[1024,512]{1,0:T(8,128)(2,1)} %collective-permute-done.12, bf16[8,384,1024]{2,1,0:T(8,128)(2,1)S(1)} %bitcast_dynamic-update-slice_fusion, s32[]{:T(128)S(6)} %select_n.261), kind=kOutput, calls=%fused_computation.54 | convolution fusion | flops 402653184 | bytes 2621444 | tf_op jit(solution)/shard_map/dot_general | solution.py:318
  130.4 0.6 fusion.36
  131.4 0.6 fusion.28
  131.9 11.4 %collective-permute-done.20 = bf16[1024,512]{1,0:T(8,128)(2,1)S(1)} collective-permute-done((bf16[1024,512]{1,0:T(8,128)(2,1)}, bf16[1024,512]{1,0:T(8,128)(2,1)S(1)}, u32[]{:S(2)}, u32[]{:S(2)}) %collective-permute-start.20) | collective-permute-done | bytes 1048608 | tf_op jit(solution)/shard_map/ppermute | solution.py:33
  143.4 0.6 fusion.22
  143.9 0.6 collective-permute-start.22
  144.5 0.6 fusion.24
  145.2 0.6 fusion.14
  145.8 1.6 collective-permute-start.28
  147.4 0.6 fusion.16
  148.1 0.6 fusion.18
  148.6 0.6 fusion.20
  149.2 2.0 %fusion.10 = f32[384,512]{1,0:T(8,128)S(1)} fusion(f32[384,512]{1,0:T(8,128)S(1)} %fusion.22, f32[384,512]{1,0:T(8,128)S(1)} %fusion.24, f32[384,512]{1,0:T(8,128)S(1)} %fusion.26, f32[384,512]{1,0:T(8,128)S(1)} %fusion.30, f32[384,512]{1,0:T(8,128)S(1)} %fusion.32, f32[384,512]{1,0:T(8,128)S(1)} %fusion.34, f32[384,512]{1,0:T(8,128)S(1)} %fusion.36, ...), kind=kOutput, calls=%fused_computation.30 | convolution fusion | flops 404029440 | bytes 8126468 | tf_op jit(solution)/shard_map/dot_general | solution.py:318
  151.2 0.6 fusion.8
  151.9 0.6 fusion.11
  152.5 0.6 fusion.9
  153.1 5.3 %collective-permute-done.18 = bf16[384,1024]{1,0:T(8,128)(2,1)S(1)} collective-permute-done((bf16[384,1024]{1,0:T(8,128)(2,1)S(1)}, bf16[384,1024]{1,0:T(8,128)(2,1)S(1)}, u32[]{:S(2)}, u32[]{:S(2)}) %collective-permute-start.18) | collective-permute-done | bytes 786464 | tf_op jit(solution)/shard_map/ppermute | solution.py:33
  158.4 2.4 %conditional.1 = (f32[384,512]{1,0:T(8,128)S(1)}, f32[384,512]{1,0:T(8,128)S(1)}) conditional(s32[]{:T(128)} %clamp.3, (bf16[384,1024]{1,0:T(8,128)(2,1)S(1)}, bf16[1024,512]{1,0:T(8,128)(2,1)}, f32[384,512]{1,0:T(8,128)S(1)}, bf16[1024,512]{1,0:T(8,128)(2,1)S(1)}, f32[384,512]{1,0:T(8,128)S(1)}) %tuple.47, ...), branch_computations={%region_0.1_spmd, %region_1.2_spmd, %region_2.3_spmd, %region_3.4_... | conditional | flops 805699584 | bytes 6815760 | solution.py:337
  158.4 1.8 %convolution_add_fusion.11 = f32[384,512]{1,0:T(8,128)S(1)} fusion(f32[384,512]{1,0:T(8,128)S(1)} %get-tuple-element.110, bf16[384,1024]{1,0:T(8,128)(2,1)S(1)} %get-tuple-element.111, bf16[1024,512]{1,0:T(8,128)(2,1)} %get-tuple-element.112), kind=kOutput, calls=%fused_computation.11 | convolution fusion | flops 402849792 | bytes 3407872 | tf_op jit(solution)/shard_map/cond/branch_5_fun/dot_general | solution.py:318
  160.2 0.6 convolution_add_fusion.10
  161.0 1.3 pad_maximum_fusion
  (44 shorter events, 2.2 us)
Async XLA Ops:
  0.0 23.1 %copy-start.5 = (f32[16,1024]{1,0:T(8,128)S(1)}, f32[16,1024]{1,0:T(8,128)}, u32[]{:S(2)}) copy-start(f32[16,1024]{1,0:T(8,128)} %rates_ref.3) | copy-start | bytes 196612
  1.5 4.3 %collective-permute-start = (f32[24,1024]{1,0:T(8,128)}, f32[24,1024]{1,0:T(8,128)S(1)}, u32[]{:S(2)}, u32[]{:S(2)}) collective-permute-start(f32[24,1024]{1,0:T(8,128)} %last_tokens.1), channel_id=1, source_target_pairs={{0,8},{8,16},{16,24},{24,32},{32,40},{40,48},{48,56},{56,64},{64,7... | collective-permute-start | bytes 294920 | tf_op jit(solution)/shard_map/ppermute | solution.py:33
  5.7 31.3 %collective-permute-start.5 = (bf16[1024,512]{1,0:T(8,128)(2,1)}, bf16[1024,512]{1,0:T(8,128)(2,1)}, u32[]{:S(2)}, u32[]{:S(2)}) collective-permute-start(bf16[1024,512]{1,0:T(8,128)(2,1)} %param.23), channel_id=1, source_target_pairs={{0,0},{1,48},{2,32},{3,16},{4,64},{5,112},{6,96},{7,80},{8,8},{9,5... | collective-permute-start | bytes 3145736 | tf_op jit(solution)/shard_map/ppermute | solution.py:33
  21.5 1.5 collective-permute-start.1
  23.9 10.9 %collective-permute-start.4 = (f32[16,1024]{1,0:T(8,128)S(1)}, f32[16,1024]{1,0:T(8,128)S(1)}, u32[]{:S(2)}, u32[]{:S(2)}) collective-permute-start(f32[16,1024]{1,0:T(8,128)S(1)} %add_select_fusion.1), channel_id=1, source_target_pairs={{0,48},{16,0},{32,16},{48,32},{1,49},{17,1},{33,17},{49,33},{2,50}... | collective-permute-start | bytes 196616 | tf_op jit(solution)/shard_map/ppermute | solution.py:33
  26.8 9.0 %collective-permute-start.3 = (f32[16,1024]{1,0:T(8,128)S(1)}, f32[16,1024]{1,0:T(8,128)S(1)}, u32[]{:S(2)}, u32[]{:S(2)}) collective-permute-start(f32[16,1024]{1,0:T(8,128)S(1)} %add_select_fusion.1), channel_id=1, source_target_pairs={{0,32},{16,48},{32,0},{48,16},{1,33},{17,49},{33,1},{49,17},{2,34}... | collective-permute-start | bytes 196616 | tf_op jit(solution)/shard_map/ppermute | solution.py:33
  32.2 4.7 %collective-permute-start.2 = (f32[16,1024]{1,0:T(8,128)S(1)}, f32[16,1024]{1,0:T(8,128)S(1)}, u32[]{:S(2)}, u32[]{:S(2)}) collective-permute-start(f32[16,1024]{1,0:T(8,128)S(1)} %add_select_fusion.1), channel_id=1, source_target_pairs={{0,16},{16,32},{32,48},{48,0},{1,17},{17,33},{33,49},{49,1},{2,18}... | collective-permute-start | bytes 196616 | tf_op jit(solution)/shard_map/ppermute | solution.py:33
  37.0 16.7 %collective-permute-start.7 = (bf16[1024,512]{1,0:T(8,128)(2,1)}, bf16[1024,512]{1,0:T(8,128)(2,1)S(1)}, u32[]{:S(2)}, u32[]{:S(2)}) collective-permute-start(bf16[1024,512]{1,0:T(8,128)(2,1)} %collective-permute-done.5), channel_id=1, source_target_pairs={{0,16},{8,56},{16,32},{24,8},{32,48},{40,24},{48,0},{56,40},{1,17}... | collective-permute-start | bytes 3145736 | tf_op jit(solution)/shard_map/ppermute | solution.py:33
  39.8 6.3 %collective-permute-start.6 = (f32[16,1024]{1,0:T(8,128)S(1)}, f32[16,1024]{1,0:T(8,128)S(1)}, u32[]{:S(2)}, u32[]{:S(2)}) collective-permute-start(f32[16,1024]{1,0:T(8,128)S(1)} %multiply_add_fusion), channel_id=1, source_target_pairs={{0,64},{64,0},{1,65},{65,1},{2,66},{66,2},{3,67},{67,3},{4,68},{68... | collective-permute-start | bytes 196616 | tf_op jit(solution)/shard_map/ppermute | solution.py:33
  43.0 26.3 %collective-permute-start.11 = (bf16[1024,512]{1,0:T(8,128)(2,1)}, bf16[1024,512]{1,0:T(8,128)(2,1)S(1)}, u32[]{:S(2)}, u32[]{:S(2)}) collective-permute-start(bf16[1024,512]{1,0:T(8,128)(2,1)} %collective-permute-done.5), channel_id=1, source_target_pairs={{0,64},{64,0},{1,65},{65,1},{2,66},{66,2},{3,67},{67,3},{4,68},{68... | collective-permute-start | bytes 3145736 | tf_op jit(solution)/shard_map/ppermute | solution.py:33
  53.7 90.2 %copy-start = (bf16[1024,512]{1,0:T(8,128)(2,1)}, bf16[1024,512]{1,0:T(8,128)(2,1)S(1)}, u32[]{:S(2)}) copy-start(bf16[1024,512]{1,0:T(8,128)(2,1)S(1)} %collective-permute-done.7) | copy-start | bytes 3145732
  53.8 29.3 %collective-permute-start.12 = (bf16[1024,512]{1,0:T(8,128)(2,1)S(1)}, bf16[1024,512]{1,0:T(8,128)(2,1)}, u32[]{:S(2)}, u32[]{:S(2)}) collective-permute-start(bf16[1024,512]{1,0:T(8,128)(2,1)S(1)} %collective-permute-done.7), channel_id=1, source_target_pairs={{0,16},{8,56},{16,32},{24,8},{32,48},{40,24},{48,0},{56,40},{1,17}... | collective-permute-start | bytes 3145736 | tf_op jit(solution)/shard_map/ppermute | solution.py:33
  56.0 17.0 %collective-permute-start.8 = (bf16[384,1024]{1,0:T(8,128)(2,1)}, bf16[384,1024]{1,0:T(8,128)(2,1)S(1)}, u32[]{:S(2)}, u32[]{:S(2)}) collective-permute-start(bf16[384,1024]{1,0:T(8,128)(2,1)} %finish_part.1), channel_id=1, source_target_pairs={{0,1},{1,2},{2,3},{3,0},{4,5},{5,6},{6,7},{7,4},{8,9},{9,10},{10,1... | collective-permute-start | bytes 2359304 | tf_op jit(solution)/shard_map/ppermute | solution.py:33
  56.4 16.6 %collective-permute-start.9 = (bf16[384,1024]{1,0:T(8,128)(2,1)}, bf16[384,1024]{1,0:T(8,128)(2,1)S(1)}, u32[]{:S(2)}, u32[]{:S(2)}) collective-permute-start(bf16[384,1024]{1,0:T(8,128)(2,1)} %finish_part.1), channel_id=1, source_target_pairs={{0,3},{1,0},{2,1},{3,2},{4,7},{5,4},{6,5},{7,6},{8,11},{9,8},{10,9... | collective-permute-start | bytes 2359304 | tf_op jit(solution)/shard_map/ppermute | solution.py:33
  59.2 23.9 %collective-permute-start.10 = (bf16[384,1024]{1,0:T(8,128)(2,1)}, bf16[384,1024]{1,0:T(8,128)(2,1)}, u32[]{:S(2)}, u32[]{:S(2)}) collective-permute-start(bf16[384,1024]{1,0:T(8,128)(2,1)} %finish_part.1), channel_id=1, source_target_pairs={{0,4},{4,0},{1,5},{5,1},{2,6},{6,2},{3,7},{7,3},{8,12},{12,8},{9,1... | collective-permute-start | bytes 2359304 | tf_op jit(solution)/shard_map/ppermute | solution.py:33
  69.3 56.9 %copy-start.2 = (bf16[1024,512]{1,0:T(8,128)(2,1)}, bf16[1024,512]{1,0:T(8,128)(2,1)S(1)}, u32[]{:S(2)}) copy-start(bf16[1024,512]{1,0:T(8,128)(2,1)S(1)} %collective-permute-done.11) | copy-start | bytes 3145732
  73.0 18.4 %copy-start.4 = (bf16[384,1024]{1,0:T(8,128)(2,1)}, bf16[384,1024]{1,0:T(8,128)(2,1)S(1)}, u32[]{:S(2)}) copy-start(bf16[384,1024]{1,0:T(8,128)(2,1)S(1)} %collective-permute-done.8) | copy-start | bytes 2359300
  83.1 19.8 %collective-permute-start.13 = (bf16[384,1024]{1,0:T(8,128)(2,1)}, bf16[384,1024]{1,0:T(8,128)(2,1)}, u32[]{:S(2)}, u32[]{:S(2)}) collective-permute-start(bf16[384,1024]{1,0:T(8,128)(2,1)} %collective-permute-done.10), channel_id=1, source_target_pairs={{0,1},{1,2},{2,3},{3,0},{4,5},{5,6},{6,7},{7,4},{8,9},{9,10},{10,1... | collective-permute-start | bytes 2359304 | tf_op jit(solution)/shard_map/ppermute | solution.py:33
  84.7 20.9 %collective-permute-start.14 = (bf16[384,1024]{1,0:T(8,128)(2,1)}, bf16[384,1024]{1,0:T(8,128)(2,1)}, u32[]{:S(2)}, u32[]{:S(2)}) collective-permute-start(bf16[384,1024]{1,0:T(8,128)(2,1)} %collective-permute-done.10), channel_id=1, source_target_pairs={{0,3},{1,0},{2,1},{3,2},{4,7},{5,4},{6,5},{7,6},{8,11},{9,8},{10,9... | collective-permute-start | bytes 2359304 | tf_op jit(solution)/shard_map/ppermute | solution.py:33
  86.9 24.4 %collective-permute-start.16 = (bf16[1024,512]{1,0:T(8,128)(2,1)}, bf16[1024,512]{1,0:T(8,128)(2,1)}, u32[]{:S(2)}, u32[]{:S(2)}) collective-permute-start(bf16[1024,512]{1,0:T(8,128)(2,1)} %collective-permute-done.12), channel_id=1, source_target_pairs={{0,16},{8,56},{16,32},{24,8},{32,48},{40,24},{48,0},{56,40},{1,17}... | collective-permute-start | bytes 3145736 | tf_op jit(solution)/shard_map/ppermute | solution.py:33
  90.0 23.8 %collective-permute-start.17 = (bf16[1024,512]{1,0:T(8,128)(2,1)S(1)}, bf16[1024,512]{1,0:T(8,128)(2,1)}, u32[]{:S(2)}, u32[]{:S(2)}) collective-permute-start(bf16[1024,512]{1,0:T(8,128)(2,1)S(1)} %collective-permute-done.11), channel_id=1, source_target_pairs={{0,16},{8,56},{16,32},{24,8},{32,48},{40,24},{48,0},{56,40},{1,17}... | collective-permute-start | bytes 3145736 | tf_op jit(solution)/shard_map/ppermute | solution.py:33
  92.4 18.9 %collective-permute-start.15 = (bf16[384,1024]{1,0:T(8,128)(2,1)}, bf16[384,1024]{1,0:T(8,128)(2,1)}, u32[]{:S(2)}, u32[]{:S(2)}) collective-permute-start(bf16[384,1024]{1,0:T(8,128)(2,1)} %broadcast_select_fusion.1), channel_id=1, source_target_pairs={{0,1},{1,2},{2,3},{3,0},{8,11},{9,8},{10,9},{11,10},{4,5},{5,6},{6... | collective-permute-start | bytes 2359304 | tf_op jit(solution)/shard_map/ppermute | solution.py:33
  102.9 48.4 %collective-permute-start.21 = (bf16[1024,512]{1,0:T(8,128)(2,1)}, bf16[1024,512]{1,0:T(8,128)(2,1)S(1)}, u32[]{:S(2)}, u32[]{:S(2)}) collective-permute-start(bf16[1024,512]{1,0:T(8,128)(2,1)} %collective-permute-done.5), channel_id=1, source_target_pairs={{0,8},{8,0},{1,9},{9,1},{2,10},{10,2},{3,11},{11,3},{4,12},{12,4},... | collective-permute-start | bytes 3145736 | tf_op jit(solution)/shard_map/ppermute | solution.py:33
  113.8 30.2 %collective-permute-start.19 = (bf16[1024,512]{1,0:T(8,128)(2,1)}, bf16[1024,512]{1,0:T(8,128)(2,1)S(1)}, u32[]{:S(2)}, u32[]{:S(2)}) collective-permute-start(bf16[1024,512]{1,0:T(8,128)(2,1)} %collective-permute-done.17), channel_id=1, source_target_pairs={{0,16},{8,56},{16,32},{24,8},{32,48},{40,24},{48,0},{56,40},{1,17}... | collective-permute-start | bytes 3145736 | tf_op jit(solution)/shard_map/ppermute | solution.py:33
  117.6 27.5 %collective-permute-start.26 = (bf16[1024,512]{1,0:T(8,128)(2,1)}, bf16[1024,512]{1,0:T(8,128)(2,1)S(1)}, u32[]{:S(2)}, u32[]{:S(2)}) collective-permute-start(bf16[1024,512]{1,0:T(8,128)(2,1)} %collective-permute-done.17), channel_id=1, source_target_pairs={{0,8},{8,0},{1,9},{9,1},{2,10},{10,2},{3,11},{11,3},{4,12},{12,4},... | collective-permute-start | bytes 3145736 | tf_op jit(solution)/shard_map/ppermute | solution.py:33
  117.6 25.8 %collective-permute-start.20 = (bf16[1024,512]{1,0:T(8,128)(2,1)}, bf16[1024,512]{1,0:T(8,128)(2,1)S(1)}, u32[]{:S(2)}, u32[]{:S(2)}) collective-permute-start(bf16[1024,512]{1,0:T(8,128)(2,1)} %collective-permute-done.16), channel_id=1, source_target_pairs={{0,64},{64,0},{1,65},{65,1},{2,66},{66,2},{3,67},{67,3},{4,68},{68... | collective-permute-start | bytes 3145736 | tf_op jit(solution)/shard_map/ppermute | solution.py:33
  124.1 6.9 %collective-permute-start.25 = (bf16[1024,512]{1,0:T(8,128)(2,1)S(1)}, bf16[1024,512]{1,0:T(8,128)(2,1)S(1)}, u32[]{:S(2)}, u32[]{:S(2)}) collective-permute-start(bf16[1024,512]{1,0:T(8,128)(2,1)S(1)} %collective-permute-done.11), channel_id=1, source_target_pairs={{0,8},{8,0},{1,9},{9,1},{2,10},{10,2},{3,11},{11,3},{4,12},{12,4},... | collective-permute-start | bytes 3145736 | tf_op jit(solution)/shard_map/ppermute | solution.py:33
  131.0 14.8 %collective-permute-start.24 = (bf16[1024,512]{1,0:T(8,128)(2,1)}, bf16[1024,512]{1,0:T(8,128)(2,1)S(1)}, u32[]{:S(2)}, u32[]{:S(2)}) collective-permute-start(bf16[1024,512]{1,0:T(8,128)(2,1)} %collective-permute-done.16), channel_id=1, source_target_pairs={{0,8},{8,0},{1,9},{9,1},{2,10},{10,2},{3,11},{11,3},{4,12},{12,4},... | collective-permute-start | bytes 3145736 | tf_op jit(solution)/shard_map/ppermute | solution.py:33
  143.3 4.6 %collective-permute-start.23 = (bf16[1024,512]{1,0:T(8,128)(2,1)}, bf16[1024,512]{1,0:T(8,128)(2,1)S(1)}, u32[]{:S(2)}, u32[]{:S(2)}) collective-permute-start(bf16[1024,512]{1,0:T(8,128)(2,1)} %collective-permute-done.12), channel_id=1, source_target_pairs={{0,8},{8,0},{1,9},{9,1},{2,10},{10,2},{3,11},{11,3},{4,12},{12,4},... | collective-permute-start | bytes 3145736 | tf_op jit(solution)/shard_map/ppermute | solution.py:33
  143.9 4.7 %collective-permute-start.22 = (bf16[1024,512]{1,0:T(8,128)(2,1)S(1)}, bf16[1024,512]{1,0:T(8,128)(2,1)S(1)}, u32[]{:S(2)}, u32[]{:S(2)}) collective-permute-start(bf16[1024,512]{1,0:T(8,128)(2,1)S(1)} %collective-permute-done.7), channel_id=1, source_target_pairs={{0,8},{8,0},{1,9},{9,1},{2,10},{10,2},{3,11},{11,3},{4,12},{12,4},... | collective-permute-start | bytes 3145736 | tf_op jit(solution)/shard_map/ppermute | solution.py:33
  145.1 13.3 %collective-permute-start.18 = (bf16[384,1024]{1,0:T(8,128)(2,1)S(1)}, bf16[384,1024]{1,0:T(8,128)(2,1)S(1)}, u32[]{:S(2)}, u32[]{:S(2)}) collective-permute-start(bf16[384,1024]{1,0:T(8,128)(2,1)S(1)} %broadcast_select_fusion), channel_id=1, source_target_pairs={{0,1},{1,2},{2,3},{3,0},{8,11},{9,8},{10,9},{11,10},{4,5},{5,6},{6... | collective-permute-start | bytes 2359304 | tf_op jit(solution)/shard_map/ppermute | solution.py:33
  145.8 6.1 %collective-permute-start.28 = (bf16[1024,512]{1,0:T(8,128)(2,1)S(1)}, bf16[1024,512]{1,0:T(8,128)(2,1)S(1)}, u32[]{:S(2)}, u32[]{:S(2)}) collective-permute-start(bf16[1024,512]{1,0:T(8,128)(2,1)S(1)} %collective-permute-done.20), channel_id=1, source_target_pairs={{0,8},{8,0},{1,9},{9,1},{2,10},{10,2},{3,11},{11,3},{4,12},{12,4},... | collective-permute-start | bytes 3145736 | tf_op jit(solution)/shard_map/ppermute | solution.py:33
  148.0 4.5 %collective-permute-start.27 = (bf16[1024,512]{1,0:T(8,128)(2,1)S(1)}, bf16[1024,512]{1,0:T(8,128)(2,1)S(1)}, u32[]{:S(2)}, u32[]{:S(2)}) collective-permute-start(bf16[1024,512]{1,0:T(8,128)(2,1)S(1)} %collective-permute-done.19), channel_id=1, source_target_pairs={{0,8},{8,0},{1,9},{9,1},{2,10},{10,2},{3,11},{11,3},{4,12},{12,4},... | collective-permute-start | bytes 3145736 | tf_op jit(solution)/shard_map/ppermute | solution.py:33
  151.2 7.2 %copy-start.1 = (bf16[1024,512]{1,0:T(8,128)(2,1)S(1)}, bf16[1024,512]{1,0:T(8,128)(2,1)}, u32[]{:S(2)}) copy-start(bf16[1024,512]{1,0:T(8,128)(2,1)} %copy-done) | copy-start | bytes 3145732
  151.2 7.2 %copy-start.3 = (bf16[1024,512]{1,0:T(8,128)(2,1)S(1)}, bf16[1024,512]{1,0:T(8,128)(2,1)}, u32[]{:S(2)}) copy-start(bf16[1024,512]{1,0:T(8,128)(2,1)} %copy-done.2) | copy-start | bytes 3145732

commit v3 on v2

--- a/solution.py
+++ b/solution.py
@@ -14,6 +14,7 @@
 TP = ("zh", "y")
 SEGS = 8
 LANES = 128
+LOCAL_BYTES = 0
 
 
 def coords(axes):
@@ -64,63 +65,78 @@
     return lax.optimization_barrier(values)
 
 
-def rows_of(ref, j, seg_len):
-    return ref[pl.ds(j, SEGS, stride=seg_len), :]
-
-
-def local_kernel(seg_len, modes, q_ref, k_ref, v_ref, halo_ref, taps_ref, rates_ref, res_ref, skip_ref, y_ref, qf_ref, total_ref, carry_ref):
+def local_kernel(seg_len, modes, tiles, q_hbm, k_hbm, v_hbm, halo_ref, taps_ref, rates_ref, res_ref, skip_ref, y_ref, qf_ref, total_ref, carry_ref, buffer, arrived):
     wide = (SEGS, LANES)
     sub = lax.broadcasted_iota(jnp.int32, wide, 0)
-    rates = rates_ref[...]
-    pole = jnp.exp(-rates)
+    sources = (q_hbm, k_hbm, v_hbm)
+
+    def copy_in(a, c):
+        lanes = pl.ds(c * LANES, LANES)
+        return pltpu.make_async_copy(sources[a].at[:, lanes], buffer.at[a, c], arrived.at[a, c])
+
+    for c in range(tiles):
+        for a in range(3):
+            copy_in(a, c).start()
 
     def spread(row):
         return jnp.broadcast_to(row, wide)
 
-    taps = [[spread(taps_ref[a, b : b + 1, :]) for b in range(3)] for a in range(3)]
-    skip = spread(skip_ref[...])
-    poles = [spread(pole[m : m + 1, :]) for m in range(modes)]
-    gains = [spread(res_ref[m : m + 1, :]) for m in range(modes)]
-
-    def before(ref, back, halo_row):
-        rolled = pltpu.roll(rows_of(ref, seg_len - back, seg_len), 1, 0)
-        return jnp.where(sub == 0, spread(halo_ref[halo_row : halo_row + 1, :]), rolled)
-
-    refs = (q_ref, k_ref, v_ref)
-    past = tuple((before(ref, 1, 8 * a + 7), before(ref, 2, 8 * a + 6)) for a, ref in enumerate(refs))
-
-    def step(j, carried):
-        past, states = carried
-        feats, new_past = [], []
-        for a, ref in enumerate(refs):
-            now = rows_of(ref, j, seg_len)
-            one, two = past[a]
-            feats.append(taps[a][0] * now + taps[a][1] * one + taps[a][2] * two)
-            new_past.append((now, one))
-        gated = feats[1] * feats[2]
-        parts = [skip * gated, None, None, None]
-        new_states = []
+    def tile(c, nothing):
+        for a in range(3):
+            copy_in(a, c).wait()
+        lanes = pl.ds(pl.multiple_of(c * LANES, LANES), LANES)
+        rates = rates_ref[:, lanes]
+        pole = jnp.exp(-rates)
+        gain = res_ref[:, lanes]
+        taps = [[spread(taps_ref[a, b : b + 1, lanes]) for b in range(3)] for a in range(3)]
+        skip = spread(skip_ref[:, lanes])
+        poles = [spread(pole[m : m + 1, :]) for m in range(modes)]
+        gains = [spread(gain[m : m + 1, :]) for m in range(modes)]
+
+        def rows_at(a, j):
+            return buffer[a, c, pl.ds(j, SEGS, stride=seg_len), :]
+
+        def before(a, back):
+            row = 8 * a + 8 - back
+            rolled = pltpu.roll(rows_at(a, seg_len - back), 1, 0)
+            return jnp.where(sub == 0, spread(halo_ref[row : row + 1, lanes]), rolled)
+
+        def step(j, carried):
+            past, states = carried
+            feats, new_past = [], []
+            for a in range(3):
+                now = rows_at(a, j)
+                one, two = past[a]
+                feats.append(taps[a][0] * now + taps[a][1] * one + taps[a][2] * two)
+                new_past.append((now, one))
+            gated = feats[1] * feats[2]
+            parts = [skip * gated, None, None, None]
+            new_states = []
+            for m in range(modes):
+                state = poles[m] * states[m] + gated
+                new_states.append(state)
+                term = gains[m] * state
+                parts[m % 4] = term if parts[m % 4] is None else parts[m % 4] + term
+            y_ref[j, :, lanes] = (parts[0] + parts[1]) + (parts[2] + parts[3])
+            qf_ref[j, :, lanes] = feats[0]
+            return tuple(new_past), tuple(new_states)
+
+        past = tuple((before(a, 1), before(a, 2)) for a in range(3))
+        zeros = tuple(jnp.zeros(wide, jnp.float32) for _ in range(modes))
+        _, ends = lax.fori_loop(0, seg_len, step, (past, zeros), unroll=4)
+
+        seg = jnp.exp(-float(seg_len) * rates)
         for m in range(modes):
-            state = poles[m] * states[m] + gated
-            new_states.append(state)
-            term = gains[m] * state
-            parts[m % 4] = term if parts[m % 4] is None else parts[m % 4] + term
-        y_ref[j] = (parts[0] + parts[1]) + (parts[2] + parts[3])
-        qf_ref[j] = feats[0]
-        return tuple(new_past), tuple(new_states)
-
-    zeros = tuple(jnp.zeros(wide, jnp.float32) for _ in range(modes))
-    _, ends = lax.fori_loop(0, seg_len, step, (past, zeros), unroll=4)
-
-    seg = jnp.exp(-float(seg_len) * rates)
-    for m in range(modes):
-        power = spread(seg[m : m + 1, :])
-        run = ends[m]
-        for by in (1, 2, 4):
-            run = run + jnp.where(sub >= by, power * pltpu.roll(run, by, 0), 0.0)
-            power = power * power
-        total_ref[m : m + 1, :] = run[SEGS - 1 : SEGS, :]
-        carry_ref[m] = jnp.where(sub >= 1, pltpu.roll(run, 1, 0), 0.0)
+            power = spread(seg[m : m + 1, :])
+            run = ends[m]
+            for by in (1, 2, 4):
+                run = run + jnp.where(sub >= by, power * pltpu.roll(run, by, 0), 0.0)
+                power = power * power
+            total_ref[m : m + 1, lanes] = run[SEGS - 1 : SEGS, :]
+            carry_ref[m, :, lanes] = jnp.where(sub >= 1, pltpu.roll(run, 1, 0), 0.0)
+        return nothing
+
+    lax.fori_loop(0, tiles, tile, 0)
 
 
 def finish_kernel(seg_len, modes, y_ref, qf_ref, carry_ref, entering_ref, rates_ref, res_ref, hidden_ref, rows_ref):
@@ -174,27 +190,23 @@
     rows, channels = q.shape
     modes = rates.shape[0]
     seg_len = rows // SEGS
-    tall = pl.BlockSpec((rows, LANES), lambda c: (0, c))
-
-    def short(n):
-        return pl.BlockSpec((n, LANES), lambda c: (0, c))
-
-    cube = pl.BlockSpec((seg_len, SEGS, LANES), lambda c: (0, 0, c))
-    mode_cube = pl.BlockSpec((modes, SEGS, LANES), lambda c: (0, 0, c))
+    tiles = channels // LANES
     f32 = jnp.float32
+    outside = pl.BlockSpec(memory_space=pltpu.HBM)
+    inside = pl.BlockSpec(memory_space=pltpu.VMEM)
     return pl.pallas_call(
-        functools.partial(local_kernel, seg_len, modes),
-        grid=(channels // LANES,),
-        in_specs=[tall, tall, tall, short(24), pl.BlockSpec((3, 3, LANES), lambda c: (0, 0, c)), short(modes), short(modes), short(1)],
-        out_specs=[cube, cube, short(modes), mode_cube],
+        functools.partial(local_kernel, seg_len, modes, tiles),
+        in_specs=[outside] * 3 + [inside] * 5,
+        out_specs=[inside] * 4,
         out_shape=[
             jax.ShapeDtypeStruct((seg_len, SEGS, channels), f32),
             jax.ShapeDtypeStruct((seg_len, SEGS, channels), f32),
             jax.ShapeDtypeStruct((modes, channels), f32),
             jax.ShapeDtypeStruct((modes, SEGS, channels), f32),
         ],
-        compiler_params=pltpu.CompilerParams(vmem_limit_bytes=56 * 2**20),
-        cost_estimate=pl.CostEstimate(flops=0, bytes_accessed=0, transcendentals=0),
+        scratch_shapes=[pltpu.VMEM((3, tiles, rows, LANES), f32), pltpu.SemaphoreType.DMA((3, tiles))],
+        compiler_params=pltpu.CompilerParams(vmem_limit_bytes=20 * 2**20),
+        cost_estimate=pl.CostEstimate(flops=0, bytes_accessed=LOCAL_BYTES, transcendentals=0),
         name="local_part",
     )(q, k, v, halo, taps, rates, res, skip)
 
@@ -216,7 +228,7 @@
         out_specs=pl.BlockSpec((rows, LANES), lambda c: (0, c)),
         out_shape=jax.ShapeDtypeStruct((rows, channels), jnp.bfloat16),
         scratch_shapes=[pltpu.VMEM((rows, LANES), jnp.float32)],
-        compiler_params=pltpu.CompilerParams(vmem_limit_bytes=56 * 2**20),
+        compiler_params=pltpu.CompilerParams(vmem_limit_bytes=20 * 2**20),
         cost_estimate=pl.CostEstimate(flops=0, bytes_accessed=0, transcendentals=0),
         name="finish_part",
     )(y, qf, carry, entering, rates, res)
@@ -237,9 +249,9 @@
         near = near + jnp.where(x >= back, decay(2 * back - 2) * came, 0.0)
         plane = plane + decay(2 * (3 - (x - back) % 4)) * came
     plane, also = tie(plane, also)
-    before = moved(plane, "zl", 1)
+    before, later = tie(moved(plane, "zl", 1), also)
     at_chip = near + jnp.where(zl == 1, decay(2 * x) * before, 0.0)
-    return jnp.where(core == 0, at_chip, decay(1) * at_chip + beside), also
+    return jnp.where(core == 0, at_chip, decay(1) * at_chip + beside), also, later
 
 
 def on_device(q, k, v, short_taps, rates, res, skip, weight):
@@ -274,40 +286,49 @@
     def swap(block):
         return moved(block, "core", 1)
 
-    entering, block = entering_state(total, decay, block)
+    entering, block, block_later = entering_state(total, decay, block)
     w, s, h = {(0, 0): block}, {}, {}
     w[0, 1] = turn_x(block)
     hidden = finish_part(y, qf, carry, entering, rates, res)
 
-    hidden, w[0, 1] = tie(hidden, w[0, 1])
+    s[0, 0] = swap(block_later)
+    hidden, w[0, 1], s[0, 0] = tie(hidden, w[0, 1], s[0, 0])
     h[0, 0] = hidden
     plus, minus = moved(hidden, "y", 1), moved(hidden, "y", -1)
     h[1, 0] = moved(hidden, "zh", 1)
-    w[1, 0] = across(block)
+    w[1, 0] = across(block_later)
     w[0, 2] = turn_x(w[0, 1])
 
-    plus, minus, h[1, 0], w[1, 0], w[0, 2] = tie(plus, minus, h[1, 0], w[1, 0], w[0, 2])
+    w[1, 1] = turn_x(w[1, 0])
+
+    plus, minus, h[1, 0], w[1, 0], w[0, 2], w[1, 1] = tie(plus, minus, h[1, 0], w[1, 0], w[0, 2], w[1, 1])
     h[0, 1], h[0, 3] = plus, minus
+    held = jnp.zeros((8, *hidden.shape), hidden.dtype)
+    for at in ((0, 0), (0, 1), (0, 3), (1, 0)):
+        held = held.at[at[0] * 4 + at[1]].set(h[at])
     h[0, 2] = onward(pick(plus, minus), "y")
     plus, minus = moved(h[1, 0], "y", 1), moved(h[1, 0], "y", -1)
     w[0, 3] = turn_x(w[0, 2])
-    w[1, 1] = turn_x(w[1, 0])
-
-    plus, minus, h[0, 2], w[0, 1], w[0, 2], w[0, 3], w[1, 0], w[1, 1] = tie(
-        plus, minus, h[0, 2], w[0, 1], w[0, 2], w[0, 3], w[1, 0], w[1, 1]
+    w[1, 2] = turn_x(w[1, 1])
+
+    plus, minus, h[0, 2], w[0, 3], w[1, 2], w[0, 1], w[0, 2], w[1, 0], w[1, 1] = tie(
+        plus, minus, h[0, 2], w[0, 3], w[1, 2], w[0, 1], w[0, 2], w[1, 0], w[1, 1]
     )
-    w[1, 3] = across(w[0, 3])
-    w[1, 2] = turn_x(w[1, 1])
-    for at in ((0, 0), (0, 1), (0, 2), (0, 3), (1, 0), (1, 1)):
+    next_on = pick(plus, minus)
+    next_on, plus, minus, h[0, 2], held = tie(next_on, plus, minus, h[0, 2], held)
+    h[1, 1], h[1, 3] = plus, minus
+    h[1, 2] = onward(next_on, "y")
+    w[1, 3] = turn_x(w[1, 2])
+    for at in ((0, 1), (0, 2), (1, 0)):
         s[at] = swap(w[at])
-    h[1, 1], h[1, 3] = plus, minus
-    h[1, 2] = onward(pick(plus, minus), "y")
-    for at in ((1, 2), (1, 3)):
+    h[1, 2], w[0, 3], w[1, 1], w[1, 2] = tie(h[1, 2], w[0, 3], w[1, 1], w[1, 2])
+    for at in ((0, 3), (1, 1), (1, 2), (1, 3)):
         s[at] = swap(w[at])
 
     slots = [(a, b) for a in (0, 1) for b in range(4)]
     late = h[1, 2]
-    held = jnp.stack([jnp.zeros_like(late) if at == (1, 2) else h[at] for at in slots])
+    for at in ((0, 2), (1, 1), (1, 3)):
+        held = held.at[at[0] * 4 + at[1]].set(h[at])
     flip = (lax.axis_index("zh") + lax.axis_index("zl")) % 2
     apart = lax.axis_index("y") - lax.axis_index("x")
     sign = jnp.where(lax.axis_index("core") == 0, 1, -1)

time: 164 us -> 160 us (0.976)
  the two profiles are of different devices: /device:TPU:6 before, /device:TPU:1 now
where the time goes in v3:
time: 160 us; the launch traced here: 158 us
  waiting for transfers between devices  75 us (47%)
  starting transfers between devices  39.8 us (25%)
  matrix products  16.9 us (11%)
  Pallas kernels  12.4 us (8%)
  local copies, waits for them, and re-layouts  12.2 us (8%)
  other arithmetic  1.76 us (1%)
    ppermute x29, waiting for transfers between devices, permute(): return lax.ppermute(value, axes, pairs)  75 us
    ppermute x29, starting transfers between devices, permute(): return lax.ppermute(value, axes, pairs)  39.8 us
    dot_general x18, matrix products, dot(): return jnp.dot(a, b, preferred_element_type=jnp.float32)  16.9 us
    unnamed x22, local copies, waits for them, and re-layouts  9.93 us
    pallas_call x1, Pallas kernels, local_part(): pl.pallas_call(functools.partial(local_kernel, seg_len, modes, tiles), in...  7.52 us
    pallas_call x1, Pallas kernels, finish_part(): pl.pallas_call(functools.partial(finish_kernel, seg_len, modes), grid=(ch...  3.38 us
  transfers between devices with their start and end apart: 29, of which 13 were waited for; matrix products, arithmetic and copies ran while one was open for 11% of the time, Pallas kernels for 7%

profile of v3, /device:TPU:1, one launch (start us, length us, event | category | flops | bytes accessed | tf_op | source)
XLA Modules:
  0.0 158.4 jit_solution(15681260186706206202)
XLA Ops:
  0.0 1.5 last_tokens.1
  1.5 2.6 %collective-permute-start = (f32[24,1024]{1,0:T(8,128)}, f32[24,1024]{1,0:T(8,128)S(1)}, u32[]{:S(2)}, u32[]{:S(2)}) collective-permute-start(f32[24,1024]{1,0:T(8,128)} %last_tokens.1), channel_id=1, source_target_pairs={{0,8},{8,16},{16,24},{24,32},{32,40},{40,48},{48,56},{56,64},{64,7... | collective-permute-start | bytes 294920 | tf_op jit(solution)/shard_map/ppermute | solution.py:34
  4.1 2.0 %collective-permute-done = f32[24,1024]{1,0:T(8,128)S(1)} collective-permute-done((f32[24,1024]{1,0:T(8,128)}, f32[24,1024]{1,0:T(8,128)S(1)}, u32[]{:S(2)}, u32[]{:S(2)}) %collective-permute-start) | collective-permute-done | bytes 98336 | tf_op jit(solution)/shard_map/ppermute | solution.py:34
  6.0 9.5 %collective-permute-start.5 = (bf16[1024,512]{1,0:T(8,128)(2,1)}, bf16[1024,512]{1,0:T(8,128)(2,1)}, u32[]{:S(2)}, u32[]{:S(2)}) collective-permute-start(bf16[1024,512]{1,0:T(8,128)(2,1)} %param.37), channel_id=1, source_target_pairs={{0,0},{1,48},{2,32},{3,16},{4,64},{5,112},{6,96},{7,80},{8,8},{9,5... | collective-permute-start | bytes 3145736 | tf_op jit(solution)/shard_map/ppermute | solution.py:34
  15.6 1.4 copy-done
  17.0 1.4 copy-done.1
  18.4 1.4 copy-done.2
  19.8 0.8 copy-done.3
  20.6 0.8 copy-done.7
  21.5 0.8 copy-done.9
  22.3 0.7 copy-done.10
  22.9 7.5 %local_part.1 = (f32[48,8,1024]{2,1,0:T(8,128)S(1)}, f32[48,8,1024]{2,1,0:T(8,128)S(1)}, f32[16,1024]{1,0:T(8,128)S(1)}, f32[16,8,1024]{2,1,0:T(8,128)S(1)}) custom-call(f32[384,1024]{1,0:T(8,128)S(1)} %copy-done, f32[384,1024]{1,0:T(8,128)S(1)} %copy-done.1, f32[384,1024]{1,0:T(8,128)S(1)} %copy-done.2, f32[24,1024]{1,0:T(8,128)S(1)} %broadcast_select_fusion.4.halo_ref, ...), custom_call_target="tpu_custom_call" | custom-call | tf_op jit(solution)/shard_map/local_part/pallas_call | solution.py:197
  30.5 1.1 copy-done.5
  31.6 3.2 %collective-permute-start.1 = (f32[16,1024]{1,0:T(8,128)S(1)}, f32[16,1024]{1,0:T(8,128)S(1)}, u32[]{:S(2)}, u32[]{:S(2)}) collective-permute-start(f32[16,1024]{1,0:T(8,128)S(1)} %get-tuple-element.252), channel_id=1, source_target_pairs={{0,8},{8,0},{1,9},{9,1},{2,10},{10,2},{3,11},{11,3},{4,12},{12,4},... | collective-permute-start | bytes 196616 | tf_op jit(solution)/shard_map/ppermute | solution.py:34
  34.8 0.9 collective-permute-done.1
  36.0 1.4 collective-permute-start.2
  37.3 1.6 %collective-permute-done.4 = f32[16,1024]{1,0:T(8,128)S(1)} collective-permute-done((f32[16,1024]{1,0:T(8,128)S(1)}, f32[16,1024]{1,0:T(8,128)S(1)}, u32[]{:S(2)}, u32[]{:S(2)}) %collective-permute-start.4) | collective-permute-done | bytes 65568 | tf_op jit(solution)/shard_map/ppermute | solution.py:34
  39.0 1.6 %collective-permute-done.3 = f32[16,1024]{1,0:T(8,128)S(1)} collective-permute-done((f32[16,1024]{1,0:T(8,128)S(1)}, f32[16,1024]{1,0:T(8,128)S(1)}, u32[]{:S(2)}, u32[]{:S(2)}) %collective-permute-start.3) | collective-permute-done | bytes 65568 | tf_op jit(solution)/shard_map/ppermute | solution.py:34
  40.6 2.1 %collective-permute-done.2 = f32[16,1024]{1,0:T(8,128)S(1)} collective-permute-done((f32[16,1024]{1,0:T(8,128)S(1)}, f32[16,1024]{1,0:T(8,128)S(1)}, u32[]{:S(2)}, u32[]{:S(2)}) %collective-permute-start.2) | collective-permute-done | bytes 65568 | tf_op jit(solution)/shard_map/ppermute | solution.py:34
  42.7 0.4 collective-permute-start.6
  43.1 0.2 collective-permute-start.7
  43.4 2.6 %collective-permute-done.6 = f32[16,1024]{1,0:T(8,128)S(1)} collective-permute-done((f32[16,1024]{1,0:T(8,128)S(1)}, f32[16,1024]{1,0:T(8,128)S(1)}, u32[]{:S(2)}, u32[]{:S(2)}) %collective-permute-start.6) | collective-permute-done | bytes 65568 | tf_op jit(solution)/shard_map/ppermute | solution.py:34
  45.9 1.9 %collective-permute-start.8 = (bf16[1024,512]{1,0:T(8,128)(2,1)}, bf16[1024,512]{1,0:T(8,128)(2,1)}, u32[]{:S(2)}, u32[]{:S(2)}) collective-permute-start(bf16[1024,512]{1,0:T(8,128)(2,1)} %collective-permute-done.5), channel_id=1, source_target_pairs={{0,8},{8,0},{1,9},{9,1},{2,10},{10,2},{3,11},{11,3},{4,12},{12,4},... | collective-permute-start | bytes 3145736 | tf_op jit(solution)/shard_map/ppermute | solution.py:34
  47.9 0.5 collective-permute-start.12
  48.4 1.4 copy-done.6
  49.8 3.4 %finish_part.1 = bf16[384,1024]{1,0:T(8,128)(2,1)S(1)} custom-call(f32[48,8,1024]{2,1,0:T(8,128)S(1)} %get-tuple-element.249.y_ref, f32[48,8,1024]{2,1,0:T(8,128)S(1)} %copy-done.6, f32[16,8,1024]{2,1,0:T(8,128)S(1)} %get-tuple-element.251.carry_ref, f32[16,1024]{1,0:T(8,128)S(1)} %add_select_fusion.entering_ref, f32[16,1024]{1,0:T(8,128)S(1)} %copy-done.4, ...), custom_call_target="tpu_custom_call" | custom-call | tf_op jit(solution)/shard_map/finish_part/pallas_call | solution.py:224
  53.2 4.2 %collective-permute-done.7 = bf16[1024,512]{1,0:T(8,128)(2,1)} collective-permute-done((bf16[1024,512]{1,0:T(8,128)(2,1)}, bf16[1024,512]{1,0:T(8,128)(2,1)}, u32[]{:S(2)}, u32[]{:S(2)}) %collective-permute-start.7) | collective-permute-done | bytes 1048608 | tf_op jit(solution)/shard_map/ppermute | solution.py:34
  57.4 1.1 collective-permute-start.13
  58.5 14.4 %collective-permute-done.12 = bf16[1024,512]{1,0:T(8,128)(2,1)} collective-permute-done((bf16[1024,512]{1,0:T(8,128)(2,1)}, bf16[1024,512]{1,0:T(8,128)(2,1)}, u32[]{:S(2)}, u32[]{:S(2)}) %collective-permute-start.12) | collective-permute-done | bytes 1048608 | tf_op jit(solution)/shard_map/ppermute | solution.py:34
  73.0 1.4 collective-permute-start.14
  74.4 2.7 %collective-permute-start.10 = (bf16[384,1024]{1,0:T(8,128)(2,1)S(1)}, bf16[384,1024]{1,0:T(8,128)(2,1)S(1)}, u32[]{:S(2)}, u32[]{:S(2)}) collective-permute-start(bf16[384,1024]{1,0:T(8,128)(2,1)S(1)} %finish_part.1), channel_id=1, source_target_pairs={{0,3},{1,0},{2,1},{3,2},{4,7},{5,4},{6,5},{7,6},{8,11},{9,8},{10,9... | collective-permute-start | bytes 2359304 | tf_op jit(solution)/shard_map/ppermute | solution.py:34
  77.1 3.8 %collective-permute-start.11 = (bf16[384,1024]{1,0:T(8,128)(2,1)S(1)}, bf16[384,1024]{1,0:T(8,128)(2,1)}, u32[]{:S(2)}, u32[]{:S(2)}) collective-permute-start(bf16[384,1024]{1,0:T(8,128)(2,1)S(1)} %finish_part.1), channel_id=1, source_target_pairs={{0,4},{4,0},{1,5},{5,1},{2,6},{6,2},{3,7},{7,3},{8,12},{12,8},{9,1... | collective-permute-start | bytes 2359304 | tf_op jit(solution)/shard_map/ppermute | solution.py:34
  80.8 0.8 scatter.24
  81.7 13.4 %collective-permute-done.9 = bf16[384,1024]{1,0:T(8,128)(2,1)S(1)} collective-permute-done((bf16[384,1024]{1,0:T(8,128)(2,1)S(1)}, bf16[384,1024]{1,0:T(8,128)(2,1)S(1)}, u32[]{:S(2)}, u32[]{:S(2)}) %collective-permute-start.9) | collective-permute-done | bytes 786464 | tf_op jit(solution)/shard_map/ppermute | solution.py:34
  95.0 3.7 %collective-permute-done.11 = bf16[384,1024]{1,0:T(8,128)(2,1)} collective-permute-done((bf16[384,1024]{1,0:T(8,128)(2,1)S(1)}, bf16[384,1024]{1,0:T(8,128)(2,1)}, u32[]{:S(2)}, u32[]{:S(2)}) %collective-permute-start.11) | collective-permute-done | bytes 786464 | tf_op jit(solution)/shard_map/ppermute | solution.py:34
  98.7 2.7 %collective-permute-start.16 = (bf16[384,1024]{1,0:T(8,128)(2,1)}, bf16[384,1024]{1,0:T(8,128)(2,1)S(1)}, u32[]{:S(2)}, u32[]{:S(2)}) collective-permute-start(bf16[384,1024]{1,0:T(8,128)(2,1)} %collective-permute-done.11), channel_id=1, source_target_pairs={{0,3},{1,0},{2,1},{3,2},{4,7},{5,4},{6,5},{7,6},{8,11},{9,8},{10,9... | collective-permute-start | bytes 2359304 | tf_op jit(solution)/shard_map/ppermute | solution.py:34
  101.7 1.2 bitcast_dynamic-update-slice_fusion.3
  102.9 15.6 %collective-permute-done.15 = bf16[384,1024]{1,0:T(8,128)(2,1)S(1)} collective-permute-done((bf16[384,1024]{1,0:T(8,128)(2,1)}, bf16[384,1024]{1,0:T(8,128)(2,1)S(1)}, u32[]{:S(2)}, u32[]{:S(2)}) %collective-permute-start.15) | collective-permute-done | bytes 786464 | tf_op jit(solution)/shard_map/ppermute | solution.py:34
  118.5 8.9 %collective-permute-done.17 = bf16[384,1024]{1,0:T(8,128)(2,1)S(1)} collective-permute-done((bf16[384,1024]{1,0:T(8,128)(2,1)S(1)}, bf16[384,1024]{1,0:T(8,128)(2,1)S(1)}, u32[]{:S(2)}, u32[]{:S(2)}) %collective-permute-start.17) | collective-permute-done | bytes 786464 | tf_op jit(solution)/shard_map/ppermute | solution.py:34
  127.5 3.2 %collective-permute-start.20 = (bf16[384,1024]{1,0:T(8,128)(2,1)S(1)}, bf16[384,1024]{1,0:T(8,128)(2,1)S(1)}, u32[]{:S(2)}, u32[]{:S(2)}) collective-permute-start(bf16[384,1024]{1,0:T(8,128)(2,1)S(1)} %broadcast_select_fusion), channel_id=1, source_target_pairs={{0,1},{1,2},{2,3},{3,0},{8,11},{9,8},{10,9},{11,10},{4,5},{5,6},{6... | collective-permute-start | bytes 2359304 | tf_op jit(solution)/shard_map/ppermute | solution.py:34
  130.7 0.5 collective-permute-start.23
  131.4 1.8 %fusion.30 = f32[384,512]{1,0:T(8,128)S(1)} fusion(bf16[1024,512]{1,0:T(8,128)(2,1)} %collective-permute-done.12, bf16[8,384,1024]{2,1,0:T(8,128)(2,1)S(1)} %bitcast_dynamic-update-slice_fusion, s32[]{:T(128)S(6)} %select_n.264), kind=kOutput, calls=%fused_computation.50 | convolution fusion | flops 402653184 | bytes 2621444 | tf_op jit(solution)/shard_map/dot_general | solution.py:339
  133.2 0.6 fusion.34
  133.7 1.8 %fusion.36 = f32[384,512]{1,0:T(8,128)S(1)} fusion(bf16[1024,512]{1,0:T(8,128)(2,1)} %collective-permute-done.7, bf16[8,384,1024]{2,1,0:T(8,128)(2,1)S(1)} %bitcast_dynamic-update-slice_fusion, s32[]{:T(128)S(6)} %select_n.259), kind=kOutput, calls=%fused_computation.56 | convolution fusion | flops 402653184 | bytes 2621444 | tf_op jit(solution)/shard_map/dot_general | solution.py:339
  135.6 4.0 %collective-permute-done.20 = bf16[384,1024]{1,0:T(8,128)(2,1)S(1)} collective-permute-done((bf16[384,1024]{1,0:T(8,128)(2,1)S(1)}, bf16[384,1024]{1,0:T(8,128)(2,1)S(1)}, u32[]{:S(2)}, u32[]{:S(2)}) %collective-permute-start.20) | collective-permute-done | bytes 786464 | tf_op jit(solution)/shard_map/ppermute | solution.py:34
  139.6 3.7 %collective-permute-start.27 = (bf16[1024,512]{1,0:T(8,128)(2,1)S(1)}, bf16[1024,512]{1,0:T(8,128)(2,1)S(1)}, u32[]{:S(2)}, u32[]{:S(2)}) collective-permute-start(bf16[1024,512]{1,0:T(8,128)(2,1)S(1)} %collective-permute-done.19), channel_id=1, source_target_pairs={{0,8},{8,0},{1,9},{9,1},{2,10},{10,2},{3,11},{11,3},{4,12},{12,4},... | collective-permute-start | bytes 3145736 | tf_op jit(solution)/shard_map/ppermute | solution.py:34
  143.3 0.6 fusion.24
  143.9 1.8 %fusion.26 = f32[384,512]{1,0:T(8,128)S(1)} fusion(bf16[1024,512]{1,0:T(8,128)(2,1)} %collective-permute-done.14, bf16[8,384,1024]{2,1,0:T(8,128)(2,1)S(1)} %bitcast_dynamic-update-slice_fusion, s32[]{:T(128)S(6)} %select_n.265), kind=kOutput, calls=%fused_computation.46 | convolution fusion | flops 402653184 | bytes 2621444 | tf_op jit(solution)/shard_map/dot_general | solution.py:339
  145.7 0.6 fusion.32
  146.4 0.6 fusion.28
  146.9 0.6 collective-permute-start.24
  147.5 0.6 fusion.22
  148.2 0.6 fusion.18
  148.8 0.6 fusion.20
  149.4 2.1 %fusion.10 = f32[384,512]{1,0:T(8,128)S(1)} fusion(f32[384,512]{1,0:T(8,128)S(1)} %fusion.22, f32[384,512]{1,0:T(8,128)S(1)} %fusion.24, f32[384,512]{1,0:T(8,128)S(1)} %fusion.26, f32[384,512]{1,0:T(8,128)S(1)} %fusion.30, f32[384,512]{1,0:T(8,128)S(1)} %fusion.32, f32[384,512]{1,0:T(8,128)S(1)} %fusion.34, f32[384,512]{1,0:T(8,128)S(1)} %fusion.36, ...), kind=kOutput, calls=%fused_computation.30 | convolution fusion | flops 404029440 | bytes 8126468 | tf_op jit(solution)/shard_map/dot_general | solution.py:339
  151.4 0.6 fusion.12
  152.0 0.6 fusion.14
  152.6 0.6 fusion.16
  153.2 2.0 %fusion.9 = f32[384,512]{1,0:T(8,128)S(1)} fusion(f32[384,512]{1,0:T(8,128)S(1)} %fusion.12, f32[384,512]{1,0:T(8,128)S(1)} %fusion.14, f32[384,512]{1,0:T(8,128)S(1)} %fusion.28, f32[384,512]{1,0:T(8,128)S(1)} %fusion.16, f32[384,512]{1,0:T(8,128)S(1)} %fusion.18, f32[384,512]{1,0:T(8,128)S(1)} %fusion.20, bf16[1024,512]{1,0:T(8,128)(2,1)} %collective-permute-done.8, ...), kind=kOutput, calls=%fused_computation.29 | convolution fusion | flops 403832832 | bytes 7340036 | tf_op jit(solution)/shard_map/dot_general | solution.py:339
  155.2 0.6 convolution_add_fusion.16
  155.8 1.2 conditional.1
  155.8 0.6 convolution_add_fusion.13
  156.4 0.6 convolution_add_fusion.12
  157.2 1.3 pad_maximum_fusion
  (53 shorter events, 1.3 us)
Async XLA Ops:
  0.0 35.8 %copy-start.4 = (f32[16,1024]{1,0:T(8,128)S(1)}, f32[16,1024]{1,0:T(8,128)}, u32[]{:S(2)}) copy-start(f32[16,1024]{1,0:T(8,128)} %rates_ref.3) | copy-start | bytes 196612
  0.0 48.4 %copy-start.8 = (f32[16,1024]{1,0:T(8,128)S(1)}, f32[16,1024]{1,0:T(8,128)}, u32[]{:S(2)}) copy-start(f32[16,1024]{1,0:T(8,128)} %res_ref.3) | copy-start | bytes 196612
  1.5 4.6 %collective-permute-start = (f32[24,1024]{1,0:T(8,128)}, f32[24,1024]{1,0:T(8,128)S(1)}, u32[]{:S(2)}, u32[]{:S(2)}) collective-permute-start(f32[24,1024]{1,0:T(8,128)} %last_tokens.1), channel_id=1, source_target_pairs={{0,8},{8,16},{16,24},{24,32},{32,40},{40,48},{48,56},{56,64},{64,7... | collective-permute-start | bytes 294920 | tf_op jit(solution)/shard_map/ppermute | solution.py:34
  6.0 36.7 %collective-permute-start.5 = (bf16[1024,512]{1,0:T(8,128)(2,1)}, bf16[1024,512]{1,0:T(8,128)(2,1)}, u32[]{:S(2)}, u32[]{:S(2)}) collective-permute-start(bf16[1024,512]{1,0:T(8,128)(2,1)} %param.37), channel_id=1, source_target_pairs={{0,0},{1,48},{2,32},{3,16},{4,64},{5,112},{6,96},{7,80},{8,8},{9,5... | collective-permute-start | bytes 3145736 | tf_op jit(solution)/shard_map/ppermute | solution.py:34
  15.6 1.4 copy-start
  17.0 1.4 copy-start.1
  18.4 1.4 copy-start.2
  19.8 0.8 copy-start.3
  20.6 0.8 copy-start.7
  21.5 0.8 copy-start.9
  22.3 0.7 copy-start.10
  30.5 1.1 copy-start.5
  31.6 4.1 %collective-permute-start.1 = (f32[16,1024]{1,0:T(8,128)S(1)}, f32[16,1024]{1,0:T(8,128)S(1)}, u32[]{:S(2)}, u32[]{:S(2)}) collective-permute-start(f32[16,1024]{1,0:T(8,128)S(1)} %get-tuple-element.252), channel_id=1, source_target_pairs={{0,8},{8,0},{1,9},{9,1},{2,10},{10,2},{3,11},{11,3},{4,12},{12,4},... | collective-permute-start | bytes 196616 | tf_op jit(solution)/shard_map/ppermute | solution.py:34
  35.8 3.2 %collective-permute-start.4 = (f32[16,1024]{1,0:T(8,128)S(1)}, f32[16,1024]{1,0:T(8,128)S(1)}, u32[]{:S(2)}, u32[]{:S(2)}) collective-permute-start(f32[16,1024]{1,0:T(8,128)S(1)} %add_select_fusion.1), channel_id=1, source_target_pairs={{0,48},{16,0},{32,16},{48,32},{1,49},{17,1},{33,17},{49,33},{2,50}... | collective-permute-start | bytes 196616 | tf_op jit(solution)/shard_map/ppermute | solution.py:34
  35.9 4.7 %collective-permute-start.3 = (f32[16,1024]{1,0:T(8,128)S(1)}, f32[16,1024]{1,0:T(8,128)S(1)}, u32[]{:S(2)}, u32[]{:S(2)}) collective-permute-start(f32[16,1024]{1,0:T(8,128)S(1)} %add_select_fusion.1), channel_id=1, source_target_pairs={{0,32},{16,48},{32,0},{48,16},{1,33},{17,49},{33,1},{49,17},{2,34}... | collective-permute-start | bytes 196616 | tf_op jit(solution)/shard_map/ppermute | solution.py:34
  36.0 6.7 %collective-permute-start.2 = (f32[16,1024]{1,0:T(8,128)S(1)}, f32[16,1024]{1,0:T(8,128)S(1)}, u32[]{:S(2)}, u32[]{:S(2)}) collective-permute-start(f32[16,1024]{1,0:T(8,128)S(1)} %add_select_fusion.1), channel_id=1, source_target_pairs={{0,16},{16,32},{32,48},{48,0},{1,17},{17,33},{33,49},{49,1},{2,18}... | collective-permute-start | bytes 196616 | tf_op jit(solution)/shard_map/ppermute | solution.py:34
  42.7 3.2 %collective-permute-start.6 = (f32[16,1024]{1,0:T(8,128)S(1)}, f32[16,1024]{1,0:T(8,128)S(1)}, u32[]{:S(2)}, u32[]{:S(2)}) collective-permute-start(f32[16,1024]{1,0:T(8,128)S(1)} %multiply_add_fusion), channel_id=1, source_target_pairs={{0,64},{64,0},{1,65},{65,1},{2,66},{66,2},{3,67},{67,3},{4,68},{68... | collective-permute-start | bytes 196616 | tf_op jit(solution)/shard_map/ppermute | solution.py:34
  43.1 14.3 %collective-permute-start.7 = (bf16[1024,512]{1,0:T(8,128)(2,1)}, bf16[1024,512]{1,0:T(8,128)(2,1)}, u32[]{:S(2)}, u32[]{:S(2)}) collective-permute-start(bf16[1024,512]{1,0:T(8,128)(2,1)} %collective-permute-done.5), channel_id=1, source_target_pairs={{0,16},{8,56},{16,32},{24,8},{32,48},{40,24},{48,0},{56,40},{1,17}... | collective-permute-start | bytes 3145736 | tf_op jit(solution)/shard_map/ppermute | solution.py:34
  45.9 11.5 %collective-permute-start.8 = (bf16[1024,512]{1,0:T(8,128)(2,1)}, bf16[1024,512]{1,0:T(8,128)(2,1)}, u32[]{:S(2)}, u32[]{:S(2)}) collective-permute-start(bf16[1024,512]{1,0:T(8,128)(2,1)} %collective-permute-done.5), channel_id=1, source_target_pairs={{0,8},{8,0},{1,9},{9,1},{2,10},{10,2},{3,11},{11,3},{4,12},{12,4},... | collective-permute-start | bytes 3145736 | tf_op jit(solution)/shard_map/ppermute | solution.py:34
  47.9 25.1 %collective-permute-start.12 = (bf16[1024,512]{1,0:T(8,128)(2,1)}, bf16[1024,512]{1,0:T(8,128)(2,1)}, u32[]{:S(2)}, u32[]{:S(2)}) collective-permute-start(bf16[1024,512]{1,0:T(8,128)(2,1)} %collective-permute-done.5), channel_id=1, source_target_pairs={{0,64},{64,0},{1,65},{65,1},{2,66},{66,2},{3,67},{67,3},{4,68},{68... | collective-permute-start | bytes 3145736 | tf_op jit(solution)/shard_map/ppermute | solution.py:34
  48.4 1.4 copy-start.6
  57.4 41.3 %collective-permute-start.13 = (bf16[1024,512]{1,0:T(8,128)(2,1)}, bf16[1024,512]{1,0:T(8,128)(2,1)S(1)}, u32[]{:S(2)}, u32[]{:S(2)}) collective-permute-start(bf16[1024,512]{1,0:T(8,128)(2,1)} %collective-permute-done.7), channel_id=1, source_target_pairs={{0,16},{8,56},{16,32},{24,8},{32,48},{40,24},{48,0},{56,40},{1,17}... | collective-permute-start | bytes 3145736 | tf_op jit(solution)/shard_map/ppermute | solution.py:34
  73.0 25.7 %collective-permute-start.14 = (bf16[1024,512]{1,0:T(8,128)(2,1)}, bf16[1024,512]{1,0:T(8,128)(2,1)}, u32[]{:S(2)}, u32[]{:S(2)}) collective-permute-start(bf16[1024,512]{1,0:T(8,128)(2,1)} %collective-permute-done.12), channel_id=1, source_target_pairs={{0,16},{8,56},{16,32},{24,8},{32,48},{40,24},{48,0},{56,40},{1,17}... | collective-permute-start | bytes 3145736 | tf_op jit(solution)/shard_map/ppermute | solution.py:34
  74.4 20.6 %collective-permute-start.9 = (bf16[384,1024]{1,0:T(8,128)(2,1)S(1)}, bf16[384,1024]{1,0:T(8,128)(2,1)S(1)}, u32[]{:S(2)}, u32[]{:S(2)}) collective-permute-start(bf16[384,1024]{1,0:T(8,128)(2,1)S(1)} %finish_part.1), channel_id=1, source_target_pairs={{0,1},{1,2},{2,3},{3,0},{4,5},{5,6},{6,7},{7,4},{8,9},{9,10},{10,1... | collective-permute-start | bytes 2359304 | tf_op jit(solution)/shard_map/ppermute | solution.py:34
  74.4 20.6 %collective-permute-start.10 = (bf16[384,1024]{1,0:T(8,128)(2,1)S(1)}, bf16[384,1024]{1,0:T(8,128)(2,1)S(1)}, u32[]{:S(2)}, u32[]{:S(2)}) collective-permute-start(bf16[384,1024]{1,0:T(8,128)(2,1)S(1)} %finish_part.1), channel_id=1, source_target_pairs={{0,3},{1,0},{2,1},{3,2},{4,7},{5,4},{6,5},{7,6},{8,11},{9,8},{10,9... | collective-permute-start | bytes 2359304 | tf_op jit(solution)/shard_map/ppermute | solution.py:34
  77.1 21.6 %collective-permute-start.11 = (bf16[384,1024]{1,0:T(8,128)(2,1)S(1)}, bf16[384,1024]{1,0:T(8,128)(2,1)}, u32[]{:S(2)}, u32[]{:S(2)}) collective-permute-start(bf16[384,1024]{1,0:T(8,128)(2,1)S(1)} %finish_part.1), channel_id=1, source_target_pairs={{0,4},{4,0},{1,5},{5,1},{2,6},{6,2},{3,7},{7,3},{8,12},{12,8},{9,1... | collective-permute-start | bytes 2359304 | tf_op jit(solution)/shard_map/ppermute | solution.py:34
  98.7 19.7 %collective-permute-start.15 = (bf16[384,1024]{1,0:T(8,128)(2,1)}, bf16[384,1024]{1,0:T(8,128)(2,1)S(1)}, u32[]{:S(2)}, u32[]{:S(2)}) collective-permute-start(bf16[384,1024]{1,0:T(8,128)(2,1)} %collective-permute-done.11), channel_id=1, source_target_pairs={{0,1},{1,2},{2,3},{3,0},{4,5},{5,6},{6,7},{7,4},{8,9},{9,10},{10,1... | collective-permute-start | bytes 2359304 | tf_op jit(solution)/shard_map/ppermute | solution.py:34
  98.7 19.7 %collective-permute-start.16 = (bf16[384,1024]{1,0:T(8,128)(2,1)}, bf16[384,1024]{1,0:T(8,128)(2,1)S(1)}, u32[]{:S(2)}, u32[]{:S(2)}) collective-permute-start(bf16[384,1024]{1,0:T(8,128)(2,1)} %collective-permute-done.11), channel_id=1, source_target_pairs={{0,3},{1,0},{2,1},{3,2},{4,7},{5,4},{6,5},{7,6},{8,11},{9,8},{10,9... | collective-permute-start | bytes 2359304 | tf_op jit(solution)/shard_map/ppermute | solution.py:34
  101.4 26.0 %collective-permute-start.18 = (bf16[1024,512]{1,0:T(8,128)(2,1)S(1)}, bf16[1024,512]{1,0:T(8,128)(2,1)S(1)}, u32[]{:S(2)}, u32[]{:S(2)}) collective-permute-start(bf16[1024,512]{1,0:T(8,128)(2,1)S(1)} %collective-permute-done.13), channel_id=1, source_target_pairs={{0,16},{8,56},{16,32},{24,8},{32,48},{40,24},{48,0},{56,40},{1,17}... | collective-permute-start | bytes 3145736 | tf_op jit(solution)/shard_map/ppermute | solution.py:34
  101.4 26.0 %collective-permute-start.19 = (bf16[1024,512]{1,0:T(8,128)(2,1)}, bf16[1024,512]{1,0:T(8,128)(2,1)S(1)}, u32[]{:S(2)}, u32[]{:S(2)}) collective-permute-start(bf16[1024,512]{1,0:T(8,128)(2,1)} %collective-permute-done.14), channel_id=1, source_target_pairs={{0,16},{8,56},{16,32},{24,8},{32,48},{40,24},{48,0},{56,40},{1,17}... | collective-permute-start | bytes 3145736 | tf_op jit(solution)/shard_map/ppermute | solution.py:34
  101.5 25.9 %collective-permute-start.17 = (bf16[384,1024]{1,0:T(8,128)(2,1)S(1)}, bf16[384,1024]{1,0:T(8,128)(2,1)S(1)}, u32[]{:S(2)}, u32[]{:S(2)}) collective-permute-start(bf16[384,1024]{1,0:T(8,128)(2,1)S(1)} %broadcast_select_fusion.1), channel_id=1, source_target_pairs={{0,1},{1,2},{2,3},{3,0},{8,11},{9,8},{10,9},{11,10},{4,5},{5,6},{6... | collective-permute-start | bytes 2359304 | tf_op jit(solution)/shard_map/ppermute | solution.py:34
  127.5 12.1 %collective-permute-start.20 = (bf16[384,1024]{1,0:T(8,128)(2,1)S(1)}, bf16[384,1024]{1,0:T(8,128)(2,1)S(1)}, u32[]{:S(2)}, u32[]{:S(2)}) collective-permute-start(bf16[384,1024]{1,0:T(8,128)(2,1)S(1)} %broadcast_select_fusion), channel_id=1, source_target_pairs={{0,1},{1,2},{2,3},{3,0},{8,11},{9,8},{10,9},{11,10},{4,5},{5,6},{6... | collective-permute-start | bytes 2359304 | tf_op jit(solution)/shard_map/ppermute | solution.py:34
  130.7 16.3 %collective-permute-start.21 = (bf16[1024,512]{1,0:T(8,128)(2,1)S(1)}, bf16[1024,512]{1,0:T(8,128)(2,1)S(1)}, u32[]{:S(2)}, u32[]{:S(2)}) collective-permute-start(bf16[1024,512]{1,0:T(8,128)(2,1)S(1)} %collective-permute-done.19), channel_id=1, source_target_pairs={{0,16},{8,56},{16,32},{24,8},{32,48},{40,24},{48,0},{56,40},{1,17}... | collective-permute-start | bytes 3145736 | tf_op jit(solution)/shard_map/ppermute | solution.py:34
  130.7 15.6 %collective-permute-start.25 = (bf16[1024,512]{1,0:T(8,128)(2,1)}, bf16[1024,512]{1,0:T(8,128)(2,1)S(1)}, u32[]{:S(2)}, u32[]{:S(2)}) collective-permute-start(bf16[1024,512]{1,0:T(8,128)(2,1)} %collective-permute-done.12), channel_id=1, source_target_pairs={{0,8},{8,0},{1,9},{9,1},{2,10},{10,2},{3,11},{11,3},{4,12},{12,4},... | collective-permute-start | bytes 3145736 | tf_op jit(solution)/shard_map/ppermute | solution.py:34
  130.7 17.4 %collective-permute-start.23 = (bf16[1024,512]{1,0:T(8,128)(2,1)S(1)}, bf16[1024,512]{1,0:T(8,128)(2,1)S(1)}, u32[]{:S(2)}, u32[]{:S(2)}) collective-permute-start(bf16[1024,512]{1,0:T(8,128)(2,1)S(1)} %collective-permute-done.13), channel_id=1, source_target_pairs={{0,8},{8,0},{1,9},{9,1},{2,10},{10,2},{3,11},{11,3},{4,12},{12,4},... | collective-permute-start | bytes 3145736 | tf_op jit(solution)/shard_map/ppermute | solution.py:34
  131.2 17.6 %collective-permute-start.22 = (bf16[1024,512]{1,0:T(8,128)(2,1)}, bf16[1024,512]{1,0:T(8,128)(2,1)S(1)}, u32[]{:S(2)}, u32[]{:S(2)}) collective-permute-start(bf16[1024,512]{1,0:T(8,128)(2,1)} %collective-permute-done.7), channel_id=1, source_target_pairs={{0,8},{8,0},{1,9},{9,1},{2,10},{10,2},{3,11},{11,3},{4,12},{12,4},... | collective-permute-start | bytes 3145736 | tf_op jit(solution)/shard_map/ppermute | solution.py:34
  139.6 11.8 %collective-permute-start.27 = (bf16[1024,512]{1,0:T(8,128)(2,1)S(1)}, bf16[1024,512]{1,0:T(8,128)(2,1)S(1)}, u32[]{:S(2)}, u32[]{:S(2)}) collective-permute-start(bf16[1024,512]{1,0:T(8,128)(2,1)S(1)} %collective-permute-done.19), channel_id=1, source_target_pairs={{0,8},{8,0},{1,9},{9,1},{2,10},{10,2},{3,11},{11,3},{4,12},{12,4},... | collective-permute-start | bytes 3145736 | tf_op jit(solution)/shard_map/ppermute | solution.py:34
  146.3 5.7 %collective-permute-start.26 = (bf16[1024,512]{1,0:T(8,128)(2,1)}, bf16[1024,512]{1,0:T(8,128)(2,1)S(1)}, u32[]{:S(2)}, u32[]{:S(2)}) collective-permute-start(bf16[1024,512]{1,0:T(8,128)(2,1)} %collective-permute-done.14), channel_id=1, source_target_pairs={{0,8},{8,0},{1,9},{9,1},{2,10},{10,2},{3,11},{11,3},{4,12},{12,4},... | collective-permute-start | bytes 3145736 | tf_op jit(solution)/shard_map/ppermute | solution.py:34
  146.9 5.6 %collective-permute-start.24 = (bf16[1024,512]{1,0:T(8,128)(2,1)S(1)}, bf16[1024,512]{1,0:T(8,128)(2,1)S(1)}, u32[]{:S(2)}, u32[]{:S(2)}) collective-permute-start(bf16[1024,512]{1,0:T(8,128)(2,1)S(1)} %collective-permute-done.18), channel_id=1, source_target_pairs={{0,8},{8,0},{1,9},{9,1},{2,10},{10,2},{3,11},{11,3},{4,12},{12,4},... | collective-permute-start | bytes 3145736 | tf_op jit(solution)/shard_map/ppermute | solution.py:34
  148.1 7.1 %collective-permute-start.28 = (bf16[1024,512]{1,0:T(8,128)(2,1)S(1)}, bf16[1024,512]{1,0:T(8,128)(2,1)S(1)}, u32[]{:S(2)}, u32[]{:S(2)}) collective-permute-start(bf16[1024,512]{1,0:T(8,128)(2,1)S(1)} %collective-permute-done.21), channel_id=1, source_target_pairs={{0,8},{8,0},{1,9},{9,1},{2,10},{10,2},{3,11},{11,3},{4,12},{12,4},... | collective-permute-start | bytes 3145736 | tf_op jit(solution)/shard_map/ppermute | solution.py:34

commit v4 on v3

--- a/solution.py
+++ b/solution.py
@@ -321,7 +321,7 @@
     w[1, 3] = turn_x(w[1, 2])
     for at in ((0, 1), (0, 2), (1, 0)):
         s[at] = swap(w[at])
-    h[1, 2], w[0, 3], w[1, 1], w[1, 2] = tie(h[1, 2], w[0, 3], w[1, 1], w[1, 2])
+    s[0, 1], s[0, 2], s[1, 0], w[0, 3], w[1, 1], w[1, 2] = tie(s[0, 1], s[0, 2], s[1, 0], w[0, 3], w[1, 1], w[1, 2])
     for at in ((0, 3), (1, 1), (1, 2), (1, 3)):
         s[at] = swap(w[at])
 

time: 160 us -> 158 us (0.988)
  starting transfers between devices: 39.8 us -> 37.7 us
    ppermute x29, starting transfers between devices: 39.8 us -> 37.7 us  [permute(): return lax.ppermute(value, axes, pairs)]
  transfers between devices with their start and end apart: 29 -> 29, of which waited for: 13 -> 15; matrix products, arithmetic and copies ran while one was open for 11% -> 12% of each run, Pallas kernels for 7% -> 7%
where the time goes in v4:
time: 158 us; the launch traced here: 156 us
  waiting for transfers between devices  74.5 us (47%)
  starting transfers between devices  37.7 us (24%)
  matrix products  16.8 us (11%)
  Pallas kernels  12.4 us (8%)
  local copies, waits for them, and re-layouts  12.2 us (8%)
  other arithmetic  1.76 us (1%)
    ppermute x29, waiting for transfers between devices, permute(): return lax.ppermute(value, axes, pairs)  74.5 us
    ppermute x29, starting transfers between devices, permute(): return lax.ppermute(value, axes, pairs)  37.7 us
    dot_general x18, matrix products, dot(): return jnp.dot(a, b, preferred_element_type=jnp.float32)  16.8 us
    unnamed x22, local copies, waits for them, and re-layouts  9.93 us
    pallas_call x1, Pallas kernels, local_part(): pl.pallas_call(functools.partial(local_kernel, seg_len, modes, tiles), in...  7.52 us
    pallas_call x1, Pallas kernels, finish_part(): pl.pallas_call(functools.partial(finish_kernel, seg_len, modes), grid=(ch...  3.38 us
  transfers between devices with their start and end apart: 29, of which 15 were waited for; matrix products, arithmetic and copies ran while one was open for 12% of the time, Pallas kernels for 7%

profile of v4, /device:TPU:1, one launch (start us, length us, event | category | flops | bytes accessed | tf_op | source)
XLA Modules:
  0.0 155.8 jit_solution(17670875893023349501)
XLA Ops:
  0.0 1.5 last_tokens.1
  1.5 2.6 %collective-permute-start = (f32[24,1024]{1,0:T(8,128)}, f32[24,1024]{1,0:T(8,128)S(1)}, u32[]{:S(2)}, u32[]{:S(2)}) collective-permute-start(f32[24,1024]{1,0:T(8,128)} %last_tokens.1), channel_id=1, source_target_pairs={{0,8},{8,16},{16,24},{24,32},{32,40},{40,48},{48,56},{56,64},{64,7... | collective-permute-start | bytes 294920 | tf_op jit(solution)/shard_map/ppermute | solution.py:34
  4.1 2.0 %collective-permute-done = f32[24,1024]{1,0:T(8,128)S(1)} collective-permute-done((f32[24,1024]{1,0:T(8,128)}, f32[24,1024]{1,0:T(8,128)S(1)}, u32[]{:S(2)}, u32[]{:S(2)}) %collective-permute-start) | collective-permute-done | bytes 98336 | tf_op jit(solution)/shard_map/ppermute | solution.py:34
  6.0 9.5 %collective-permute-start.5 = (bf16[1024,512]{1,0:T(8,128)(2,1)}, bf16[1024,512]{1,0:T(8,128)(2,1)}, u32[]{:S(2)}, u32[]{:S(2)}) collective-permute-start(bf16[1024,512]{1,0:T(8,128)(2,1)} %param.37), channel_id=1, source_target_pairs={{0,0},{1,48},{2,32},{3,16},{4,64},{5,112},{6,96},{7,80},{8,8},{9,5... | collective-permute-start | bytes 3145736 | tf_op jit(solution)/shard_map/ppermute | solution.py:34
  15.6 1.4 copy-done
  17.0 1.4 copy-done.1
  18.4 1.4 copy-done.2
  19.8 0.8 copy-done.3
  20.6 0.8 copy-done.7
  21.5 0.8 copy-done.9
  22.3 0.7 copy-done.10
  22.9 7.5 %local_part.1 = (f32[48,8,1024]{2,1,0:T(8,128)S(1)}, f32[48,8,1024]{2,1,0:T(8,128)S(1)}, f32[16,1024]{1,0:T(8,128)S(1)}, f32[16,8,1024]{2,1,0:T(8,128)S(1)}) custom-call(f32[384,1024]{1,0:T(8,128)S(1)} %copy-done, f32[384,1024]{1,0:T(8,128)S(1)} %copy-done.1, f32[384,1024]{1,0:T(8,128)S(1)} %copy-done.2, f32[24,1024]{1,0:T(8,128)S(1)} %broadcast_select_fusion.4.halo_ref, ...), custom_call_target="tpu_custom_call" | custom-call | tf_op jit(solution)/shard_map/local_part/pallas_call | solution.py:197
  30.5 1.1 copy-done.5
  31.6 3.2 %collective-permute-start.1 = (f32[16,1024]{1,0:T(8,128)S(1)}, f32[16,1024]{1,0:T(8,128)S(1)}, u32[]{:S(2)}, u32[]{:S(2)}) collective-permute-start(f32[16,1024]{1,0:T(8,128)S(1)} %get-tuple-element.254), channel_id=1, source_target_pairs={{0,8},{8,0},{1,9},{9,1},{2,10},{10,2},{3,11},{11,3},{4,12},{12,4},... | collective-permute-start | bytes 196616 | tf_op jit(solution)/shard_map/ppermute | solution.py:34
  34.8 0.9 collective-permute-done.1
  36.0 1.4 collective-permute-start.2
  37.3 1.6 %collective-permute-done.4 = f32[16,1024]{1,0:T(8,128)S(1)} collective-permute-done((f32[16,1024]{1,0:T(8,128)S(1)}, f32[16,1024]{1,0:T(8,128)S(1)}, u32[]{:S(2)}, u32[]{:S(2)}) %collective-permute-start.4) | collective-permute-done | bytes 65568 | tf_op jit(solution)/shard_map/ppermute | solution.py:34
  39.0 1.6 %collective-permute-done.3 = f32[16,1024]{1,0:T(8,128)S(1)} collective-permute-done((f32[16,1024]{1,0:T(8,128)S(1)}, f32[16,1024]{1,0:T(8,128)S(1)}, u32[]{:S(2)}, u32[]{:S(2)}) %collective-permute-start.3) | collective-permute-done | bytes 65568 | tf_op jit(solution)/shard_map/ppermute | solution.py:34
  40.6 2.1 %collective-permute-done.2 = f32[16,1024]{1,0:T(8,128)S(1)} collective-permute-done((f32[16,1024]{1,0:T(8,128)S(1)}, f32[16,1024]{1,0:T(8,128)S(1)}, u32[]{:S(2)}, u32[]{:S(2)}) %collective-permute-start.2) | collective-permute-done | bytes 65568 | tf_op jit(solution)/shard_map/ppermute | solution.py:34
  42.7 0.4 collective-permute-start.6
  43.4 2.6 %collective-permute-done.6 = f32[16,1024]{1,0:T(8,128)S(1)} collective-permute-done((f32[16,1024]{1,0:T(8,128)S(1)}, f32[16,1024]{1,0:T(8,128)S(1)}, u32[]{:S(2)}, u32[]{:S(2)}) %collective-permute-start.6) | collective-permute-done | bytes 65568 | tf_op jit(solution)/shard_map/ppermute | solution.py:34
  45.9 1.9 %collective-permute-start.8 = (bf16[1024,512]{1,0:T(8,128)(2,1)}, bf16[1024,512]{1,0:T(8,128)(2,1)}, u32[]{:S(2)}, u32[]{:S(2)}) collective-permute-start(bf16[1024,512]{1,0:T(8,128)(2,1)} %collective-permute-done.5), channel_id=1, source_target_pairs={{0,8},{8,0},{1,9},{9,1},{2,10},{10,2},{3,11},{11,3},{4,12},{12,4},... | collective-permute-start | bytes 3145736 | tf_op jit(solution)/shard_map/ppermute | solution.py:34
  47.9 0.5 collective-permute-start.12
  48.4 1.4 copy-done.6
  49.8 3.4 %finish_part.1 = bf16[384,1024]{1,0:T(8,128)(2,1)S(1)} custom-call(f32[48,8,1024]{2,1,0:T(8,128)S(1)} %get-tuple-element.251.y_ref, f32[48,8,1024]{2,1,0:T(8,128)S(1)} %copy-done.6, f32[16,8,1024]{2,1,0:T(8,128)S(1)} %get-tuple-element.253.carry_ref, f32[16,1024]{1,0:T(8,128)S(1)} %add_select_fusion.entering_ref, f32[16,1024]{1,0:T(8,128)S(1)} %copy-done.4, ...), custom_call_target="tpu_custom_call" | custom-call | tf_op jit(solution)/shard_map/finish_part/pallas_call | solution.py:224
  53.2 4.2 %collective-permute-done.7 = bf16[1024,512]{1,0:T(8,128)(2,1)} collective-permute-done((bf16[1024,512]{1,0:T(8,128)(2,1)}, bf16[1024,512]{1,0:T(8,128)(2,1)}, u32[]{:S(2)}, u32[]{:S(2)}) %collective-permute-start.7) | collective-permute-done | bytes 1048608 | tf_op jit(solution)/shard_map/ppermute | solution.py:34
  57.4 1.1 collective-permute-start.13
  58.5 14.4 %collective-permute-done.12 = bf16[1024,512]{1,0:T(8,128)(2,1)} collective-permute-done((bf16[1024,512]{1,0:T(8,128)(2,1)}, bf16[1024,512]{1,0:T(8,128)(2,1)}, u32[]{:S(2)}, u32[]{:S(2)}) %collective-permute-start.12) | collective-permute-done | bytes 1048608 | tf_op jit(solution)/shard_map/ppermute | solution.py:34
  73.0 1.4 collective-permute-start.14
  74.4 2.7 %collective-permute-start.10 = (bf16[384,1024]{1,0:T(8,128)(2,1)S(1)}, bf16[384,1024]{1,0:T(8,128)(2,1)S(1)}, u32[]{:S(2)}, u32[]{:S(2)}) collective-permute-start(bf16[384,1024]{1,0:T(8,128)(2,1)S(1)} %finish_part.1), channel_id=1, source_target_pairs={{0,3},{1,0},{2,1},{3,2},{4,7},{5,4},{6,5},{7,6},{8,11},{9,8},{10,9... | collective-permute-start | bytes 2359304 | tf_op jit(solution)/shard_map/ppermute | solution.py:34
  77.1 3.8 %collective-permute-start.11 = (bf16[384,1024]{1,0:T(8,128)(2,1)S(1)}, bf16[384,1024]{1,0:T(8,128)(2,1)}, u32[]{:S(2)}, u32[]{:S(2)}) collective-permute-start(bf16[384,1024]{1,0:T(8,128)(2,1)S(1)} %finish_part.1), channel_id=1, source_target_pairs={{0,4},{4,0},{1,5},{5,1},{2,6},{6,2},{3,7},{7,3},{8,12},{12,8},{9,1... | collective-permute-start | bytes 2359304 | tf_op jit(solution)/shard_map/ppermute | solution.py:34
  80.8 0.8 scatter.24
  81.7 13.4 %collective-permute-done.9 = bf16[384,1024]{1,0:T(8,128)(2,1)S(1)} collective-permute-done((bf16[384,1024]{1,0:T(8,128)(2,1)S(1)}, bf16[384,1024]{1,0:T(8,128)(2,1)S(1)}, u32[]{:S(2)}, u32[]{:S(2)}) %collective-permute-start.9) | collective-permute-done | bytes 786464 | tf_op jit(solution)/shard_map/ppermute | solution.py:34
  95.0 3.7 %collective-permute-done.11 = bf16[384,1024]{1,0:T(8,128)(2,1)} collective-permute-done((bf16[384,1024]{1,0:T(8,128)(2,1)S(1)}, bf16[384,1024]{1,0:T(8,128)(2,1)}, u32[]{:S(2)}, u32[]{:S(2)}) %collective-permute-start.11) | collective-permute-done | bytes 786464 | tf_op jit(solution)/shard_map/ppermute | solution.py:34
  98.7 2.7 %collective-permute-start.16 = (bf16[384,1024]{1,0:T(8,128)(2,1)}, bf16[384,1024]{1,0:T(8,128)(2,1)S(1)}, u32[]{:S(2)}, u32[]{:S(2)}) collective-permute-start(bf16[384,1024]{1,0:T(8,128)(2,1)} %collective-permute-done.11), channel_id=1, source_target_pairs={{0,3},{1,0},{2,1},{3,2},{4,7},{5,4},{6,5},{7,6},{8,11},{9,8},{10,9... | collective-permute-start | bytes 2359304 | tf_op jit(solution)/shard_map/ppermute | solution.py:34
  101.7 1.2 bitcast_dynamic-update-slice_fusion.3
  102.9 15.6 %collective-permute-done.15 = bf16[384,1024]{1,0:T(8,128)(2,1)S(1)} collective-permute-done((bf16[384,1024]{1,0:T(8,128)(2,1)}, bf16[384,1024]{1,0:T(8,128)(2,1)S(1)}, u32[]{:S(2)}, u32[]{:S(2)}) %collective-permute-start.15) | collective-permute-done | bytes 786464 | tf_op jit(solution)/shard_map/ppermute | solution.py:34
  118.5 8.9 %collective-permute-done.17 = bf16[384,1024]{1,0:T(8,128)(2,1)S(1)} collective-permute-done((bf16[384,1024]{1,0:T(8,128)(2,1)S(1)}, bf16[384,1024]{1,0:T(8,128)(2,1)S(1)}, u32[]{:S(2)}, u32[]{:S(2)}) %collective-permute-start.17) | collective-permute-done | bytes 786464 | tf_op jit(solution)/shard_map/ppermute | solution.py:34
  127.5 3.2 %collective-permute-start.20 = (bf16[384,1024]{1,0:T(8,128)(2,1)S(1)}, bf16[384,1024]{1,0:T(8,128)(2,1)S(1)}, u32[]{:S(2)}, u32[]{:S(2)}) collective-permute-start(bf16[384,1024]{1,0:T(8,128)(2,1)S(1)} %broadcast_select_fusion), channel_id=1, source_target_pairs={{0,1},{1,2},{2,3},{3,0},{8,11},{9,8},{10,9},{11,10},{4,5},{5,6},{6... | collective-permute-start | bytes 2359304 | tf_op jit(solution)/shard_map/ppermute | solution.py:34
  130.7 0.5 collective-permute-start.22
  131.4 1.8 %fusion.30 = f32[384,512]{1,0:T(8,128)S(1)} fusion(bf16[1024,512]{1,0:T(8,128)(2,1)} %collective-permute-done.12, bf16[8,384,1024]{2,1,0:T(8,128)(2,1)S(1)} %bitcast_dynamic-update-slice_fusion, s32[]{:T(128)S(6)} %select_n.264), kind=kOutput, calls=%fused_computation.50 | convolution fusion | flops 402653184 | bytes 2621444 | tf_op jit(solution)/shard_map/dot_general | solution.py:339
  133.2 0.6 fusion.34
  133.7 1.8 %fusion.36 = f32[384,512]{1,0:T(8,128)S(1)} fusion(bf16[1024,512]{1,0:T(8,128)(2,1)} %collective-permute-done.7, bf16[8,384,1024]{2,1,0:T(8,128)(2,1)S(1)} %bitcast_dynamic-update-slice_fusion, s32[]{:T(128)S(6)} %select_n.259), kind=kOutput, calls=%fused_computation.56 | convolution fusion | flops 402653184 | bytes 2621444 | tf_op jit(solution)/shard_map/dot_general | solution.py:339
  136.0 0.6 collective-permute-done.23
  136.7 0.6 fusion.24
  137.2 0.5 collective-permute-start.26
  137.7 1.8 %fusion.26 = f32[384,512]{1,0:T(8,128)S(1)} fusion(bf16[1024,512]{1,0:T(8,128)(2,1)} %collective-permute-done.14, bf16[8,384,1024]{2,1,0:T(8,128)(2,1)S(1)} %bitcast_dynamic-update-slice_fusion, s32[]{:T(128)S(6)} %select_n.265), kind=kOutput, calls=%fused_computation.46 | convolution fusion | flops 402653184 | bytes 2621444 | tf_op jit(solution)/shard_map/dot_general | solution.py:339
  139.7 0.6 fusion.32
  140.3 0.6 fusion.28
  140.9 0.6 fusion.18
  141.4 0.6 fusion.20
  142.0 2.6 %collective-permute-done.24 = bf16[1024,512]{1,0:T(8,128)(2,1)S(1)} collective-permute-done((bf16[1024,512]{1,0:T(8,128)(2,1)S(1)}, bf16[1024,512]{1,0:T(8,128)(2,1)S(1)}, u32[]{:S(2)}, u32[]{:S(2)}) %collective-permute-start.24) | collective-permute-done | bytes 1048608 | tf_op jit(solution)/shard_map/ppermute | solution.py:34
  144.6 1.6 %collective-permute-start.28 = (bf16[1024,512]{1,0:T(8,128)(2,1)S(1)}, bf16[1024,512]{1,0:T(8,128)(2,1)S(1)}, u32[]{:S(2)}, u32[]{:S(2)}) collective-permute-start(bf16[1024,512]{1,0:T(8,128)(2,1)S(1)} %collective-permute-done.24), channel_id=1, source_target_pairs={{0,8},{8,0},{1,9},{9,1},{2,10},{10,2},{3,11},{11,3},{4,12},{12,4},... | collective-permute-start | bytes 3145736 | tf_op jit(solution)/shard_map/ppermute | solution.py:34
  146.2 0.6 fusion.22
  146.8 2.0 %fusion.10 = f32[384,512]{1,0:T(8,128)S(1)} fusion(f32[384,512]{1,0:T(8,128)S(1)} %fusion.22, f32[384,512]{1,0:T(8,128)S(1)} %fusion.24, f32[384,512]{1,0:T(8,128)S(1)} %fusion.26, f32[384,512]{1,0:T(8,128)S(1)} %fusion.30, f32[384,512]{1,0:T(8,128)S(1)} %fusion.32, f32[384,512]{1,0:T(8,128)S(1)} %fusion.34, f32[384,512]{1,0:T(8,128)S(1)} %fusion.36, ...), kind=kOutput, calls=%fused_computation.30 | convolution fusion | flops 404029440 | bytes 8126468 | tf_op jit(solution)/shard_map/dot_general | solution.py:339
  148.8 0.6 fusion.12
  149.4 0.6 fusion.14
  150.0 0.6 fusion.16
  150.6 2.0 %fusion.9 = f32[384,512]{1,0:T(8,128)S(1)} fusion(f32[384,512]{1,0:T(8,128)S(1)} %fusion.12, f32[384,512]{1,0:T(8,128)S(1)} %fusion.14, f32[384,512]{1,0:T(8,128)S(1)} %fusion.28, f32[384,512]{1,0:T(8,128)S(1)} %fusion.16, f32[384,512]{1,0:T(8,128)S(1)} %fusion.18, f32[384,512]{1,0:T(8,128)S(1)} %fusion.20, bf16[1024,512]{1,0:T(8,128)(2,1)} %collective-permute-done.8, ...), kind=kOutput, calls=%fused_computation.29 | convolution fusion | flops 403832832 | bytes 7340036 | tf_op jit(solution)/shard_map/dot_general | solution.py:339
  152.6 0.6 convolution_add_fusion.16
  153.2 1.2 conditional.1
  153.2 0.6 convolution_add_fusion.13
  153.8 0.6 convolution_add_fusion.12
  154.6 1.3 pad_maximum_fusion
  (53 shorter events, 2.0 us)
Async XLA Ops:
  0.0 35.8 %copy-start.4 = (f32[16,1024]{1,0:T(8,128)S(1)}, f32[16,1024]{1,0:T(8,128)}, u32[]{:S(2)}) copy-start(f32[16,1024]{1,0:T(8,128)} %rates_ref.3) | copy-start | bytes 196612
  0.0 48.4 %copy-start.8 = (f32[16,1024]{1,0:T(8,128)S(1)}, f32[16,1024]{1,0:T(8,128)}, u32[]{:S(2)}) copy-start(f32[16,1024]{1,0:T(8,128)} %res_ref.3) | copy-start | bytes 196612
  1.5 4.6 %collective-permute-start = (f32[24,1024]{1,0:T(8,128)}, f32[24,1024]{1,0:T(8,128)S(1)}, u32[]{:S(2)}, u32[]{:S(2)}) collective-permute-start(f32[24,1024]{1,0:T(8,128)} %last_tokens.1), channel_id=1, source_target_pairs={{0,8},{8,16},{16,24},{24,32},{32,40},{40,48},{48,56},{56,64},{64,7... | collective-permute-start | bytes 294920 | tf_op jit(solution)/shard_map/ppermute | solution.py:34
  6.0 36.7 %collective-permute-start.5 = (bf16[1024,512]{1,0:T(8,128)(2,1)}, bf16[1024,512]{1,0:T(8,128)(2,1)}, u32[]{:S(2)}, u32[]{:S(2)}) collective-permute-start(bf16[1024,512]{1,0:T(8,128)(2,1)} %param.37), channel_id=1, source_target_pairs={{0,0},{1,48},{2,32},{3,16},{4,64},{5,112},{6,96},{7,80},{8,8},{9,5... | collective-permute-start | bytes 3145736 | tf_op jit(solution)/shard_map/ppermute | solution.py:34
  15.6 1.4 copy-start
  17.0 1.4 copy-start.1
  18.4 1.4 copy-start.2
  19.8 0.8 copy-start.3
  20.6 0.8 copy-start.7
  21.5 0.8 copy-start.9
  22.3 0.7 copy-start.10
  30.5 1.1 copy-start.5
  31.6 4.1 %collective-permute-start.1 = (f32[16,1024]{1,0:T(8,128)S(1)}, f32[16,1024]{1,0:T(8,128)S(1)}, u32[]{:S(2)}, u32[]{:S(2)}) collective-permute-start(f32[16,1024]{1,0:T(8,128)S(1)} %get-tuple-element.254), channel_id=1, source_target_pairs={{0,8},{8,0},{1,9},{9,1},{2,10},{10,2},{3,11},{11,3},{4,12},{12,4},... | collective-permute-start | bytes 196616 | tf_op jit(solution)/shard_map/ppermute | solution.py:34
  35.8 3.2 %collective-permute-start.4 = (f32[16,1024]{1,0:T(8,128)S(1)}, f32[16,1024]{1,0:T(8,128)S(1)}, u32[]{:S(2)}, u32[]{:S(2)}) collective-permute-start(f32[16,1024]{1,0:T(8,128)S(1)} %add_select_fusion.1), channel_id=1, source_target_pairs={{0,48},{16,0},{32,16},{48,32},{1,49},{17,1},{33,17},{49,33},{2,50}... | collective-permute-start | bytes 196616 | tf_op jit(solution)/shard_map/ppermute | solution.py:34
  35.9 4.7 %collective-permute-start.3 = (f32[16,1024]{1,0:T(8,128)S(1)}, f32[16,1024]{1,0:T(8,128)S(1)}, u32[]{:S(2)}, u32[]{:S(2)}) collective-permute-start(f32[16,1024]{1,0:T(8,128)S(1)} %add_select_fusion.1), channel_id=1, source_target_pairs={{0,32},{16,48},{32,0},{48,16},{1,33},{17,49},{33,1},{49,17},{2,34}... | collective-permute-start | bytes 196616 | tf_op jit(solution)/shard_map/ppermute | solution.py:34
  36.0 6.7 %collective-permute-start.2 = (f32[16,1024]{1,0:T(8,128)S(1)}, f32[16,1024]{1,0:T(8,128)S(1)}, u32[]{:S(2)}, u32[]{:S(2)}) collective-permute-start(f32[16,1024]{1,0:T(8,128)S(1)} %add_select_fusion.1), channel_id=1, source_target_pairs={{0,16},{16,32},{32,48},{48,0},{1,17},{17,33},{33,49},{49,1},{2,18}... | collective-permute-start | bytes 196616 | tf_op jit(solution)/shard_map/ppermute | solution.py:34
  42.7 3.2 %collective-permute-start.6 = (f32[16,1024]{1,0:T(8,128)S(1)}, f32[16,1024]{1,0:T(8,128)S(1)}, u32[]{:S(2)}, u32[]{:S(2)}) collective-permute-start(f32[16,1024]{1,0:T(8,128)S(1)} %multiply_add_fusion), channel_id=1, source_target_pairs={{0,64},{64,0},{1,65},{65,1},{2,66},{66,2},{3,67},{67,3},{4,68},{68... | collective-permute-start | bytes 196616 | tf_op jit(solution)/shard_map/ppermute | solution.py:34
  43.1 14.3 %collective-permute-start.7 = (bf16[1024,512]{1,0:T(8,128)(2,1)}, bf16[1024,512]{1,0:T(8,128)(2,1)}, u32[]{:S(2)}, u32[]{:S(2)}) collective-permute-start(bf16[1024,512]{1,0:T(8,128)(2,1)} %collective-permute-done.5), channel_id=1, source_target_pairs={{0,16},{8,56},{16,32},{24,8},{32,48},{40,24},{48,0},{56,40},{1,17}... | collective-permute-start | bytes 3145736 | tf_op jit(solution)/shard_map/ppermute | solution.py:34
  45.9 11.5 %collective-permute-start.8 = (bf16[1024,512]{1,0:T(8,128)(2,1)}, bf16[1024,512]{1,0:T(8,128)(2,1)}, u32[]{:S(2)}, u32[]{:S(2)}) collective-permute-start(bf16[1024,512]{1,0:T(8,128)(2,1)} %collective-permute-done.5), channel_id=1, source_target_pairs={{0,8},{8,0},{1,9},{9,1},{2,10},{10,2},{3,11},{11,3},{4,12},{12,4},... | collective-permute-start | bytes 3145736 | tf_op jit(solution)/shard_map/ppermute | solution.py:34
  47.9 25.1 %collective-permute-start.12 = (bf16[1024,512]{1,0:T(8,128)(2,1)}, bf16[1024,512]{1,0:T(8,128)(2,1)}, u32[]{:S(2)}, u32[]{:S(2)}) collective-permute-start(bf16[1024,512]{1,0:T(8,128)(2,1)} %collective-permute-done.5), channel_id=1, source_target_pairs={{0,64},{64,0},{1,65},{65,1},{2,66},{66,2},{3,67},{67,3},{4,68},{68... | collective-permute-start | bytes 3145736 | tf_op jit(solution)/shard_map/ppermute | solution.py:34
  48.4 1.4 copy-start.6
  57.4 41.3 %collective-permute-start.13 = (bf16[1024,512]{1,0:T(8,128)(2,1)}, bf16[1024,512]{1,0:T(8,128)(2,1)S(1)}, u32[]{:S(2)}, u32[]{:S(2)}) collective-permute-start(bf16[1024,512]{1,0:T(8,128)(2,1)} %collective-permute-done.7), channel_id=1, source_target_pairs={{0,16},{8,56},{16,32},{24,8},{32,48},{40,24},{48,0},{56,40},{1,17}... | collective-permute-start | bytes 3145736 | tf_op jit(solution)/shard_map/ppermute | solution.py:34
  73.0 25.7 %collective-permute-start.14 = (bf16[1024,512]{1,0:T(8,128)(2,1)}, bf16[1024,512]{1,0:T(8,128)(2,1)}, u32[]{:S(2)}, u32[]{:S(2)}) collective-permute-start(bf16[1024,512]{1,0:T(8,128)(2,1)} %collective-permute-done.12), channel_id=1, source_target_pairs={{0,16},{8,56},{16,32},{24,8},{32,48},{40,24},{48,0},{56,40},{1,17}... | collective-permute-start | bytes 3145736 | tf_op jit(solution)/shard_map/ppermute | solution.py:34
  74.4 20.6 %collective-permute-start.9 = (bf16[384,1024]{1,0:T(8,128)(2,1)S(1)}, bf16[384,1024]{1,0:T(8,128)(2,1)S(1)}, u32[]{:S(2)}, u32[]{:S(2)}) collective-permute-start(bf16[384,1024]{1,0:T(8,128)(2,1)S(1)} %finish_part.1), channel_id=1, source_target_pairs={{0,1},{1,2},{2,3},{3,0},{4,5},{5,6},{6,7},{7,4},{8,9},{9,10},{10,1... | collective-permute-start | bytes 2359304 | tf_op jit(solution)/shard_map/ppermute | solution.py:34
  74.4 20.6 %collective-permute-start.10 = (bf16[384,1024]{1,0:T(8,128)(2,1)S(1)}, bf16[384,1024]{1,0:T(8,128)(2,1)S(1)}, u32[]{:S(2)}, u32[]{:S(2)}) collective-permute-start(bf16[384,1024]{1,0:T(8,128)(2,1)S(1)} %finish_part.1), channel_id=1, source_target_pairs={{0,3},{1,0},{2,1},{3,2},{4,7},{5,4},{6,5},{7,6},{8,11},{9,8},{10,9... | collective-permute-start | bytes 2359304 | tf_op jit(solution)/shard_map/ppermute | solution.py:34
  77.1 21.6 %collective-permute-start.11 = (bf16[384,1024]{1,0:T(8,128)(2,1)S(1)}, bf16[384,1024]{1,0:T(8,128)(2,1)}, u32[]{:S(2)}, u32[]{:S(2)}) collective-permute-start(bf16[384,1024]{1,0:T(8,128)(2,1)S(1)} %finish_part.1), channel_id=1, source_target_pairs={{0,4},{4,0},{1,5},{5,1},{2,6},{6,2},{3,7},{7,3},{8,12},{12,8},{9,1... | collective-permute-start | bytes 2359304 | tf_op jit(solution)/shard_map/ppermute | solution.py:34
  98.7 19.7 %collective-permute-start.15 = (bf16[384,1024]{1,0:T(8,128)(2,1)}, bf16[384,1024]{1,0:T(8,128)(2,1)S(1)}, u32[]{:S(2)}, u32[]{:S(2)}) collective-permute-start(bf16[384,1024]{1,0:T(8,128)(2,1)} %collective-permute-done.11), channel_id=1, source_target_pairs={{0,1},{1,2},{2,3},{3,0},{4,5},{5,6},{6,7},{7,4},{8,9},{9,10},{10,1... | collective-permute-start | bytes 2359304 | tf_op jit(solution)/shard_map/ppermute | solution.py:34
  98.7 19.7 %collective-permute-start.16 = (bf16[384,1024]{1,0:T(8,128)(2,1)}, bf16[384,1024]{1,0:T(8,128)(2,1)S(1)}, u32[]{:S(2)}, u32[]{:S(2)}) collective-permute-start(bf16[384,1024]{1,0:T(8,128)(2,1)} %collective-permute-done.11), channel_id=1, source_target_pairs={{0,3},{1,0},{2,1},{3,2},{4,7},{5,4},{6,5},{7,6},{8,11},{9,8},{10,9... | collective-permute-start | bytes 2359304 | tf_op jit(solution)/shard_map/ppermute | solution.py:34
  101.4 26.0 %collective-permute-start.18 = (bf16[1024,512]{1,0:T(8,128)(2,1)S(1)}, bf16[1024,512]{1,0:T(8,128)(2,1)S(1)}, u32[]{:S(2)}, u32[]{:S(2)}) collective-permute-start(bf16[1024,512]{1,0:T(8,128)(2,1)S(1)} %collective-permute-done.13), channel_id=1, source_target_pairs={{0,16},{8,56},{16,32},{24,8},{32,48},{40,24},{48,0},{56,40},{1,17}... | collective-permute-start | bytes 3145736 | tf_op jit(solution)/shard_map/ppermute | solution.py:34
  101.4 26.0 %collective-permute-start.19 = (bf16[1024,512]{1,0:T(8,128)(2,1)}, bf16[1024,512]{1,0:T(8,128)(2,1)S(1)}, u32[]{:S(2)}, u32[]{:S(2)}) collective-permute-start(bf16[1024,512]{1,0:T(8,128)(2,1)} %collective-permute-done.14), channel_id=1, source_target_pairs={{0,16},{8,56},{16,32},{24,8},{32,48},{40,24},{48,0},{56,40},{1,17}... | collective-permute-start | bytes 3145736 | tf_op jit(solution)/shard_map/ppermute | solution.py:34
  101.5 25.9 %collective-permute-start.17 = (bf16[384,1024]{1,0:T(8,128)(2,1)S(1)}, bf16[384,1024]{1,0:T(8,128)(2,1)S(1)}, u32[]{:S(2)}, u32[]{:S(2)}) collective-permute-start(bf16[384,1024]{1,0:T(8,128)(2,1)S(1)} %broadcast_select_fusion.1), channel_id=1, source_target_pairs={{0,1},{1,2},{2,3},{3,0},{8,11},{9,8},{10,9},{11,10},{4,5},{5,6},{6... | collective-permute-start | bytes 2359304 | tf_op jit(solution)/shard_map/ppermute | solution.py:34
  127.5 25.7 %collective-permute-start.20 = (bf16[384,1024]{1,0:T(8,128)(2,1)S(1)}, bf16[384,1024]{1,0:T(8,128)(2,1)S(1)}, u32[]{:S(2)}, u32[]{:S(2)}) collective-permute-start(bf16[384,1024]{1,0:T(8,128)(2,1)S(1)} %broadcast_select_fusion), channel_id=1, source_target_pairs={{0,1},{1,2},{2,3},{3,0},{8,11},{9,8},{10,9},{11,10},{4,5},{5,6},{6... | collective-permute-start | bytes 2359304 | tf_op jit(solution)/shard_map/ppermute | solution.py:34
  130.7 13.9 %collective-permute-start.24 = (bf16[1024,512]{1,0:T(8,128)(2,1)S(1)}, bf16[1024,512]{1,0:T(8,128)(2,1)S(1)}, u32[]{:S(2)}, u32[]{:S(2)}) collective-permute-start(bf16[1024,512]{1,0:T(8,128)(2,1)S(1)} %collective-permute-done.19), channel_id=1, source_target_pairs={{0,16},{8,56},{16,32},{24,8},{32,48},{40,24},{48,0},{56,40},{1,17}... | collective-permute-start | bytes 3145736 | tf_op jit(solution)/shard_map/ppermute | solution.py:34
  130.7 4.9 %collective-permute-start.21 = (bf16[1024,512]{1,0:T(8,128)(2,1)}, bf16[1024,512]{1,0:T(8,128)(2,1)S(1)}, u32[]{:S(2)}, u32[]{:S(2)}) collective-permute-start(bf16[1024,512]{1,0:T(8,128)(2,1)} %collective-permute-done.7), channel_id=1, source_target_pairs={{0,8},{8,0},{1,9},{9,1},{2,10},{10,2},{3,11},{11,3},{4,12},{12,4},... | collective-permute-start | bytes 3145736 | tf_op jit(solution)/shard_map/ppermute | solution.py:34
  130.7 5.3 %collective-permute-start.22 = (bf16[1024,512]{1,0:T(8,128)(2,1)S(1)}, bf16[1024,512]{1,0:T(8,128)(2,1)S(1)}, u32[]{:S(2)}, u32[]{:S(2)}) collective-permute-start(bf16[1024,512]{1,0:T(8,128)(2,1)S(1)} %collective-permute-done.13), channel_id=1, source_target_pairs={{0,8},{8,0},{1,9},{9,1},{2,10},{10,2},{3,11},{11,3},{4,12},{12,4},... | collective-permute-start | bytes 3145736 | tf_op jit(solution)/shard_map/ppermute | solution.py:34
  131.2 5.4 %collective-permute-start.23 = (bf16[1024,512]{1,0:T(8,128)(2,1)}, bf16[1024,512]{1,0:T(8,128)(2,1)S(1)}, u32[]{:S(2)}, u32[]{:S(2)}) collective-permute-start(bf16[1024,512]{1,0:T(8,128)(2,1)} %collective-permute-done.12), channel_id=1, source_target_pairs={{0,8},{8,0},{1,9},{9,1},{2,10},{10,2},{3,11},{11,3},{4,12},{12,4},... | collective-permute-start | bytes 3145736 | tf_op jit(solution)/shard_map/ppermute | solution.py:34
  136.5 12.3 %collective-permute-start.27 = (bf16[1024,512]{1,0:T(8,128)(2,1)S(1)}, bf16[1024,512]{1,0:T(8,128)(2,1)S(1)}, u32[]{:S(2)}, u32[]{:S(2)}) collective-permute-start(bf16[1024,512]{1,0:T(8,128)(2,1)S(1)} %collective-permute-done.19), channel_id=1, source_target_pairs={{0,8},{8,0},{1,9},{9,1},{2,10},{10,2},{3,11},{11,3},{4,12},{12,4},... | collective-permute-start | bytes 3145736 | tf_op jit(solution)/shard_map/ppermute | solution.py:34
  137.2 12.2 %collective-permute-start.26 = (bf16[1024,512]{1,0:T(8,128)(2,1)}, bf16[1024,512]{1,0:T(8,128)(2,1)S(1)}, u32[]{:S(2)}, u32[]{:S(2)}) collective-permute-start(bf16[1024,512]{1,0:T(8,128)(2,1)} %collective-permute-done.14), channel_id=1, source_target_pairs={{0,8},{8,0},{1,9},{9,1},{2,10},{10,2},{3,11},{11,3},{4,12},{12,4},... | collective-permute-start | bytes 3145736 | tf_op jit(solution)/shard_map/ppermute | solution.py:34
  139.5 10.5 %collective-permute-start.25 = (bf16[1024,512]{1,0:T(8,128)(2,1)S(1)}, bf16[1024,512]{1,0:T(8,128)(2,1)S(1)}, u32[]{:S(2)}, u32[]{:S(2)}) collective-permute-start(bf16[1024,512]{1,0:T(8,128)(2,1)S(1)} %collective-permute-done.18), channel_id=1, source_target_pairs={{0,8},{8,0},{1,9},{9,1},{2,10},{10,2},{3,11},{11,3},{4,12},{12,4},... | collective-permute-start | bytes 3145736 | tf_op jit(solution)/shard_map/ppermute | solution.py:34
  144.6 8.0 %collective-permute-start.28 = (bf16[1024,512]{1,0:T(8,128)(2,1)S(1)}, bf16[1024,512]{1,0:T(8,128)(2,1)S(1)}, u32[]{:S(2)}, u32[]{:S(2)}) collective-permute-start(bf16[1024,512]{1,0:T(8,128)(2,1)S(1)} %collective-permute-done.24), channel_id=1, source_target_pairs={{0,8},{8,0},{1,9},{9,1},{2,10},{10,2},{3,11},{11,3},{4,12},{12,4},... | collective-permute-start | bytes 3145736 | tf_op jit(solution)/shard_map/ppermute | solution.py:34
